TPU v7x, 32 devices: a whole 2x2x4 slice. The times are simulated.
32 devices in a mesh: outer: 4 (over x, core), inner: 8 (over z, y).
Axes of the slice: x: 2, y: 2, z: 4, core: 2. Of those that a mesh axis runs over, the one named last changes fastest.
Arguments:
- tokens: bfloat16 [12288, 1152], P(('outer', 'inner')), may hold values from -6 to 6
- conditioning: float32 [3, 1152], replicated, may hold values from -6 to 6
- column_sample: int32 [768], P(('outer', 'inner')), may hold values from 0 to 2, as said below
- is_image: int32 [3], replicated, may hold values from 0 to 1, as said below
- output_grad: bfloat16 [12288, 1152], P(('outer', 'inner')), may hold values from -6 to 6
- weights: float32 [23887872], P(('outer', 'inner'))
- first_moment: float32 [23887872], P(('outer', 'inner')), may hold values from -0.0012207031 to 0.0012207031
- second_moment: float32 [23887872], P(('outer', 'inner')), may hold values from 4.1834003e-08 to 1.6733601e-07
- biases: float32 [16128], replicated, may hold values from -0.25 to 0.25
- bias_first: float32 [16128], replicated, may hold values from -0.0012207031 to 0.0012207031
- bias_second: float32 [16128], replicated, may hold values from 4.1834003e-08 to 1.6733601e-07
Outputs:
- block_out: float32 [12288, 1152], P(('outer', 'inner'))
- input_grad: float32 [12288, 1152], P(('outer', 'inner'))
- cond_grad: float32 [3, 1152], replicated
- grad_norm: float32 [], replicated
- new_weights: float32 [23887872], P(('outer', 'inner'))
- first_out: float32 [23887872], P(('outer', 'inner'))
- second_out: float32 [23887872], P(('outer', 'inner'))
- new_biases: float32 [16128], replicated
- bias_first_out: float32 [16128], replicated
- bias_second_out: float32 [16128], replicated
Inputs may be any that keep to these rules, and one draw needn't show every extreme that they name: `column_sample`: each group number names exactly 256 columns. `is_image`: exactly max(1, 0) groups are images.
All inputs are finite; a program needn't handle non-finite values.
Results may differ from a plain program's by a relative error of at most 0.012.
The roundings to bfloat16 on the way count: a program that leaves them out, or rounds other values in their place, can miss the bound.
Values may be sent and summed in bfloat16 or wider, within the bound.
A program may use at most 384 MiB of HBM per device.

v0:
```python
import math

import jax
import jax.numpy as jnp
from jax import lax
from jax.sharding import PartitionSpec as P

D = 1152
H = 16
HD = 72
FF = 4608
FRAMES = 16
STEP = 8


NORM_EPS = 1e-06
LEARN_RATE = 0.02
BETA_FIRST = 0.5
BETA_SECOND = 0.55
ADAM_EPS = 1e-08
WEIGHT_DECAY = 0.01
CLIP_NORM = 1.0


def unpack_mats(flat):
    shapes = [(D, 3 * D), (D, D), (D, FF), (FF, D), (D, 6 * D)]
    pieces = []
    offset = 0
    for height, breadth in shapes:
        pieces.append(
            lax.slice_in_dim(flat, offset, offset + height * breadth).reshape(height, breadth)
        )
        offset = offset + height * breadth
    return pieces


def split_bias(vector):
    widths = [D, D, D, FF, D, 6 * D]
    pieces = []
    offset = 0
    for span_width in widths:
        pieces.append(lax.slice_in_dim(vector, offset, offset + span_width))
        offset = offset + span_width
    return pieces


def layer_stats(values):
    centered = values - jnp.mean(values, axis=-1, keepdims=True)
    inverse = lax.rsqrt(jnp.mean(centered * centered, axis=-1, keepdims=True) + NORM_EPS)
    return (centered * inverse, inverse)


def norm_back(grad_normed, normed, inverse):
    return inverse * (
        grad_normed
        - jnp.mean(grad_normed, axis=-1, keepdims=True)
        - normed * jnp.mean(grad_normed * normed, axis=-1, keepdims=True)
    )


def plain_dot(left_side, right_side):
    return jnp.dot(left_side, right_side, preferred_element_type=jnp.float32)


def left_dot(left_side, right_side):
    return lax.dot_general(
        left_side, right_side, (((0,), (0,)), ((), ())), preferred_element_type=jnp.float32
    )


def right_dot(left_side, right_side):
    return lax.dot_general(
        left_side, right_side, (((1,), (1,)), ((), ())), preferred_element_type=jnp.float32
    )


def scatter_grads(flat_grad):
    return lax.psum_scatter(flat_grad, ("outer", "inner"), scatter_dimension=0, tiled=True)


def ada_pieces(grad_mods_all, soft_cond, w_ada, conditioning):
    highest = lax.Precision.HIGHEST
    grad_b_ada = jnp.sum(grad_mods_all, axis=0)
    grad_w_ada = lax.dot_general(
        soft_cond.astype(jnp.float32),
        grad_mods_all,
        (((0,), (0,)), ((), ())),
        precision=highest,
        preferred_element_type=jnp.float32,
    )
    grad_soft = lax.dot_general(
        grad_mods_all,
        w_ada.astype(jnp.float32),
        (((1,), (1,)), ((), ())),
        precision=highest,
        preferred_element_type=jnp.float32,
    )
    silu_out, silu_back = jax.vjp(jax.nn.silu, conditioning)
    return (grad_b_ada, grad_w_ada, silu_back(grad_soft)[0])


def adamw(parameter, gradient, first_state, second_state):
    first_new = BETA_FIRST * first_state + (1.0 - BETA_FIRST) * gradient
    second_new = BETA_SECOND * second_state + (1.0 - BETA_SECOND) * gradient * gradient
    first_hat = first_new / (1.0 - BETA_FIRST**STEP)
    second_hat = second_new / (1.0 - BETA_SECOND**STEP)
    updated = parameter - LEARN_RATE * (
        first_hat / (jnp.sqrt(second_hat) + ADAM_EPS) + WEIGHT_DECAY * parameter
    )
    return (updated, first_new, second_new)


def on_device(
    tokens,
    conditioning,
    column_sample,
    is_image,
    output_grad,
    weights,
    first_moment,
    second_moment,
    biases,
    bias_first,
    bias_second,
):
    bf16 = jnp.bfloat16
    highest = lax.Precision.HIGHEST
    columns = column_sample.shape[0]
    groups = conditioning.shape[0]
    row_count = columns * FRAMES
    score_scale = 1.0 / math.sqrt(HD)
    gathered = lax.all_gather(weights.astype(bf16), ("outer", "inner"), axis=0, tiled=True)
    w_qkv, w_proj, w_up, w_down, w_ada = unpack_mats(gathered)
    b_query, b_value, b_proj, b_up, b_down, b_ada = split_bias(biases)
    soft_cond = jax.nn.silu(conditioning).astype(bf16)
    mods_all = plain_dot(soft_cond, w_ada) + b_ada
    mods = jnp.take(mods_all, column_sample, axis=0)
    video_cols = jnp.take(1.0 - is_image.astype(jnp.float32), column_sample)
    mod_parts = mods.reshape(columns, 1, 6, D)
    shift_att, scale_att, gate_att = (mod_parts[:, :, 0], mod_parts[:, :, 1], mod_parts[:, :, 2])
    shift_mlp, scale_mlp, gate_mlp = (mod_parts[:, :, 3], mod_parts[:, :, 4], mod_parts[:, :, 5])
    states = tokens.astype(jnp.float32).reshape(columns, FRAMES, D)
    normed_att, inverse_att = layer_stats(states)
    input_att = (normed_att * (1.0 + scale_att) + shift_att).astype(bf16).reshape(row_count, D)
    qkv_bias = jnp.concatenate([b_query, jnp.zeros((D,), jnp.float32), b_value])
    projected = (plain_dot(input_att, w_qkv) + qkv_bias).astype(bf16)
    queries = projected[:, :D].reshape(columns, FRAMES, H, HD)
    key_part = projected[:, D : 2 * D].reshape(columns, FRAMES, H, HD)
    value_part = projected[:, 2 * D :].reshape(columns, FRAMES, H, HD)
    scores = (
        jnp.einsum("cqhd,ckhd->chqk", queries, key_part, preferred_element_type=jnp.float32)
        * score_scale
    )
    probabilities = jax.nn.softmax(scores, axis=-1)
    prob_low = probabilities.astype(bf16)
    attended = jnp.einsum(
        "chqk,ckhd->cqhd", prob_low, value_part, preferred_element_type=jnp.float32
    )
    attended = attended.reshape(row_count, D).astype(bf16)
    branch = (plain_dot(attended, w_proj) + b_proj).reshape(columns, FRAMES, D)
    middle = states + gate_att * branch
    normed_mlp, inverse_mlp = layer_stats(middle)
    input_mlp = (normed_mlp * (1.0 + scale_mlp) + shift_mlp).astype(bf16).reshape(row_count, D)
    hidden = plain_dot(input_mlp, w_up) + b_up
    gelu_out, gelu_back = jax.vjp(lambda pre_act: jax.nn.gelu(pre_act, approximate=True), hidden)
    active = gelu_out.astype(bf16)
    outcome = (plain_dot(active, w_down) + b_down).reshape(columns, FRAMES, D)
    result = middle + gate_mlp * outcome
    is_video = video_cols[:, None, None] > 0.5
    block_out = jnp.where(is_video, result, states).reshape(row_count, D)
    regathered = lax.all_gather(weights.astype(bf16), ("outer", "inner"), axis=0, tiled=True)
    w_qkv, w_proj, w_up, w_down, w_ada = unpack_mats(regathered)
    upstream = output_grad.astype(jnp.float32).reshape(columns, FRAMES, D)
    grad_block = jnp.where(is_video, upstream, 0.0)
    grad_gate_mlp = jnp.sum(grad_block * outcome, axis=1)
    grad_outcome = (grad_block * gate_mlp).astype(bf16).reshape(row_count, D)
    grad_w_down = left_dot(active, grad_outcome)
    grad_b_down = jnp.sum(grad_outcome.astype(jnp.float32), axis=0)
    grad_active = right_dot(grad_outcome, w_down)
    grad_hidden = gelu_back(grad_active)[0].astype(bf16)
    grad_w_up = left_dot(input_mlp, grad_hidden)
    grad_b_up = jnp.sum(grad_hidden.astype(jnp.float32), axis=0)
    grad_input_mlp = right_dot(grad_hidden, w_up).reshape(columns, FRAMES, D)
    grad_shift_mlp = jnp.sum(grad_input_mlp, axis=1)
    grad_scale_mlp = jnp.sum(grad_input_mlp * normed_mlp, axis=1)
    grad_middle = grad_block + norm_back(
        grad_input_mlp * (1.0 + scale_mlp), normed_mlp, inverse_mlp
    )
    grad_gate_att = jnp.sum(grad_middle * branch, axis=1)
    grad_branch = (grad_middle * gate_att).astype(bf16).reshape(row_count, D)
    grad_w_proj = left_dot(attended, grad_branch)
    grad_b_proj = jnp.sum(grad_branch.astype(jnp.float32), axis=0)
    grad_attended = right_dot(grad_branch, w_proj).astype(bf16).reshape(columns, FRAMES, H, HD)
    grad_probs = jnp.einsum(
        "cqhd,ckhd->chqk", grad_attended, value_part, preferred_element_type=jnp.float32
    )
    grad_values = jnp.einsum(
        "chqk,cqhd->ckhd", prob_low, grad_attended, preferred_element_type=jnp.float32
    )
    grad_scores = probabilities * (
        grad_probs - jnp.sum(grad_probs * probabilities, axis=-1, keepdims=True)
    )
    grad_scores = grad_scores.astype(bf16)
    grad_queries = (
        jnp.einsum("chqk,ckhd->cqhd", grad_scores, key_part, preferred_element_type=jnp.float32)
        * score_scale
    )
    grad_keys = (
        jnp.einsum("chqk,cqhd->ckhd", grad_scores, queries, preferred_element_type=jnp.float32)
        * score_scale
    )
    grad_projected = jnp.concatenate(
        [
            grad_queries.reshape(row_count, D),
            grad_keys.reshape(row_count, D),
            grad_values.reshape(row_count, D),
        ],
        axis=1,
    ).astype(bf16)
    grad_w_qkv = left_dot(input_att, grad_projected)
    grad_qkv_sums = jnp.sum(grad_projected.astype(jnp.float32), axis=0)
    grad_b_query = grad_qkv_sums[:D]
    grad_b_value = grad_qkv_sums[2 * D :]
    grad_input_att = right_dot(grad_projected, w_qkv).reshape(columns, FRAMES, D)
    grad_shift_att = jnp.sum(grad_input_att, axis=1)
    grad_scale_att = jnp.sum(grad_input_att * normed_att, axis=1)
    grad_states = grad_middle + norm_back(
        grad_input_att * (1.0 + scale_att), normed_att, inverse_att
    )
    input_grad = jnp.where(is_video, grad_states, upstream).reshape(row_count, D)
    grad_mods = jnp.stack(
        [
            grad_shift_att,
            grad_scale_att,
            grad_gate_att,
            grad_shift_mlp,
            grad_scale_mlp,
            grad_gate_mlp,
        ],
        axis=1,
    )
    grad_mods = grad_mods.reshape(columns, 6 * D)
    membership = (column_sample[:, None] == jnp.arange(groups, dtype=jnp.int32)[None, :]).astype(
        jnp.float32
    )
    mods_local = lax.dot_general(
        membership,
        grad_mods,
        (((0,), (0,)), ((), ())),
        precision=highest,
        preferred_element_type=jnp.float32,
    )
    prefix_grad = jnp.concatenate(
        [
            grad_w_qkv.reshape(-1),
            grad_w_proj.reshape(-1),
            grad_w_up.reshape(-1),
            grad_w_down.reshape(-1),
        ]
    )
    bias_head = jnp.concatenate([grad_b_query, grad_b_value, grad_b_proj, grad_b_up, grad_b_down])
    grad_b_ada, grad_w_ada, cond_local = ada_pieces(mods_local, soft_cond, w_ada, conditioning)
    flat_grad = jnp.concatenate([prefix_grad, grad_w_ada.reshape(-1)])
    first_small = jnp.concatenate([bias_head, grad_b_ada])
    first_sum, second_sum = lax.psum((first_small, cond_local), ("outer", "inner"))
    grad_shard = scatter_grads(flat_grad)
    square_sum = lax.psum(jnp.sum(grad_shard * grad_shard), ("outer", "inner"))
    grad_norm = jnp.sqrt(square_sum + jnp.sum(first_sum * first_sum))
    factor = jnp.minimum(1.0, CLIP_NORM / (grad_norm + 1e-06))
    new_weights, first_out, second_out = adamw(
        weights, grad_shard * factor, first_moment, second_moment
    )
    new_biases, bias_first_out, bias_second_out = adamw(
        biases, first_sum * factor, bias_first, bias_second
    )
    return (
        block_out,
        input_grad,
        second_sum,
        grad_norm,
        new_weights,
        first_out,
        second_out,
        new_biases,
        bias_first_out,
        bias_second_out,
    )


def solution(mesh):
    in_specs = (
        P(("outer", "inner"), None),
        P(),
        P(("outer", "inner")),
        P(),
        P(("outer", "inner"), None),
        P(("outer", "inner")),
        P(("outer", "inner")),
        P(("outer", "inner")),
        P(),
        P(),
        P(),
    )
    out_specs = (
        P(("outer", "inner"), None),
        P(("outer", "inner"), None),
        P(),
        P(),
        P(("outer", "inner")),
        P(("outer", "inner")),
        P(("outer", "inner")),
        P(),
        P(),
        P(),
    )
    return jax.shard_map(
        on_device, mesh=mesh, in_specs=in_specs, out_specs=out_specs, check_vma=False
    )
```

profile of v0, /device:TPU:0, one launch (start us, length us, event | category | flops | bytes accessed | tf_op | source)
XLA Modules:
  0.0 2207.0 jit_solution(6836669880866880324)
XLA Ops:
  7.3 3.2 convert_element_type.81
  11.7 1.9 fusion.49
  16.4 261.0 %all-gather.2.cloned.1.call-done = bf16[23887872]{0:T(1024)(128)(2,1)} async-done(((bf16[746496]{0:T(1024)(128)(2,1)}), bf16[23887872]{0:T(1024)(128)(2,1)}) %all-gather.2.cloned.1.call-update) | async-done | bytes 47775760 | tf_op jit(solution)/shard_map/all_gather | solution.py:132
  277.4 15.0 fusion.58
  292.4 19.1 slice.141
  311.5 19.1 reshape.342
  330.5 6.8 slice.158
  337.3 15.2 slice.128
  352.5 15.2 reshape.343
  367.7 13.4 slice.154
  381.1 29.1 %slice.122 = bf16[1152,6912]{1,0:T(8,128)(2,1)} reshape(bf16[7962624]{0:T(1024)(128)(2,1)} %slice.154) | data formatting | bytes 31850496 | tf_op jit(solution)/shard_map/slice | solution.py:31
  410.2 7.7 convolution_add_fusion
  422.5 7.6 fusion.8
  431.2 3.7 reshape.303
  434.9 4.1 reshape.305
  439.0 3.6 reshape.304
  442.7 2.4 fusion.36
  445.0 12.3 fusion.63
  459.4 2.5 convert_element_type.87
  462.0 1.7 slice-done.8
  463.7 4.0 slice.135
  467.7 20.4 slice.144
  488.2 3.3 fusion.42
  494.6 11.5 convolution_add_fusion.1
  506.2 11.3 convert_reduce_fusion.2
  517.5 11.3 convert_reduce_fusion
  528.7 15.0 multiply_reduce_fusion.4
  543.8 5.3 convert_reduce_fusion.3
  550.1 2.4 convolution_convert_fusion
  552.4 4.3 reshape.310
  556.8 3.8 fusion.27
  563.3 1.9 fusion.29
  566.4 2.5 concatenate.24
  569.0 2.5 reshape.314
  571.5 1.8 copy.60
  573.3 2.5 concatenate.25
  575.8 2.5 reshape.315
  578.4 1.8 copy.62
  580.2 2.5 concatenate.26
  582.7 2.7 reshape.316
  585.4 5.5 fusion.66
  591.0 10.1 fusion.67
  601.2 10.8 fusion.53
  612.0 7.5 multiply_reduce_fusion.6
  624.2 4.0 multiply_reduce_fusion.3
  628.6 2.3 stack.27
  631.0 1.7 fusion.64
  634.2 7.9 fusion.65
  642.1 16.7 reshape.317
  658.8 10.9 constant_dynamic-update-slice_fusion.3
  669.7 6.6 reshape.318
  676.3 20.9 reshape.319
  697.1 22.0 reshape.320
  719.2 17.0 fusion.52
  736.2 32.7 %reshape.321 = f32[7962624]{0:T(1024)} reshape(f32[1152,6912]{1,0:T(8,128)} %fusion.52) | data formatting | bytes 63700992 | tf_op jit(solution)/shard_map/reshape | solution.py:263
  768.9 4.2 constant_dynamic-update-slice_fusion.9
  773.1 17.6 constant_dynamic-update-slice_fusion.8
  790.7 18.7 constant_dynamic-update-slice_fusion.7
  810.9 10.5 constant_dynamic-update-slice_fusion.6
  822.2 15.5 fusion.45
  837.7 1304.1 %all-reduce.5.cloned.1.call-done = f32[23887872]{0:T(1024)} async-done(((f32[23887872]{0:T(1024)}), f32[23887872]{0:T(1024)}) %all-reduce.5.cloned.1.call-update) | async-done | bytes 95551504
  2141.9 3.2 multiply_reduce_fusion.1
  2145.1 40.7 %all-reduce.6 = (f32[3,1152]{1,0:T(4,128)}, f32[]{:T(128)}, f32[16128]{0:T(1024)S(1)}) all-reduce(f32[3,1152]{1,0:T(4,128)S(1)} %fusion.45, f32[]{:T(128)} %multiply_reduce_fusion.1, f32[16128]{0:T(1024)S(1)} %constant_dynamic-update-slice_fusion.10), channel_id=1, replica_groups=mesh['outer'=4,'inner'=8] {'outer','inner'}, use_global_device_ids=true, to_apply=%region_17.18 | all-reduce | flops 19585 | bytes 156680 | tf_op jit(solution)/shard_map/psum | solution.py:265
  2188.5 10.1 multiply_subtract_fusion
  (212 shorter events, 29.9 us)
Async XLA Ops:
  7.2 3.3 copy-start.34
  7.2 4.0 copy-start.54
  7.2 4.5 copy-start.52
  7.2 7.2 copy-start
  7.2 270.2 %all-gather.2.cloned.1.call-start = ((), (), s32[]{:S(2)}) async-start(), calls=%async_computation | async-start | bytes 49268736 | tf_op jit(solution)/shard_map/all_gather | solution.py:132
  10.5 2131.4 %all-reduce.5.cloned.1.call-start = ((), (), s32[]{:S(2)}) async-start(), calls=%async_computation.1 | async-start | bytes 191102976
  13.7 278.7 %copy-start.49 = (pred[24]{0:T(512)(128)(4,1)}, pred[24]{0:T(512)(128)(4,1)S(1)}, u32[]{:S(2)}) copy-start(pred[24]{0:T(512)(128)(4,1)S(1)} %get-tuple-element.56) | copy-start | bytes 76
  381.1 29.1 %slice-start.16 = ((f32[16128]{0:T(1024)}), f32[6912]{0:T(1024)S(1)}, s32[]{:S(2)}) async-start(f32[16128]{0:T(1024)} %param.19), calls=%async_computation.18 | async-start | bytes 57344 | tf_op jit(solution)/shard_map/slice | solution.py:42
  381.1 29.1 %copy-start.36 = (f32[3,1152]{1,0:T(4,128)S(1)}, f32[3,1152]{1,0:T(4,128)}, u32[]{:S(2)}) copy-start(f32[3,1152]{1,0:T(4,128)} %param.12) | copy-start | bytes 41476
  422.5 7.6 copy-start.18
  439.0 6.0 copy-start.1
  445.0 12.3 copy-start.25
  467.7 20.4 copy-start.8
  491.4 2.5 copy-start.12
  491.5 2.9 copy-start.48
  494.0 12.2 slice-start.9
  494.5 11.6 copy-start.13
  494.5 11.6 slice-start.10
  494.5 11.6 slice-start.11
  494.5 11.6 copy-start.22
  494.5 11.6 copy-start.33
  494.5 11.6 copy-start.51
  528.7 15.1 copy-start.20
  528.7 15.1 copy-start.50
  543.8 6.3 copy-start.7
  550.1 6.7 copy-start.32
  556.8 3.8 copy-start.5
  556.8 3.8 copy-start.26
  563.3 1.9 copy-start.2
  585.4 5.6 copy-start.14
  585.4 5.6 copy-start.21
  585.4 15.7 slice-start.12
  591.0 10.1 slice-start.13
  591.0 10.1 copy-start.23
  591.0 21.0 slice-start.14
  601.1 10.8 slice-start.15
  601.1 10.8 copy-start.24
  601.1 10.8 copy-start.28
  601.1 10.8 copy-start.30
  601.2 10.8 copy-start.43
  601.2 10.8 copy-start.44
  612.0 12.2 copy-start.9
  612.0 12.2 copy-start.10
  612.0 12.2 copy-start.11
  624.2 4.1 copy-start.40
  624.2 4.2 copy-start.39
  628.2 2.8 copy-start.53
  628.2 4.5 copy-start.16
  630.9 3.2 copy-start.17
  631.0 3.2 copy-start.19
  697.1 22.0 copy-start.29
  697.1 22.0 copy-start.37
  773.1 36.3 %slice-start = ((s8[31850496]{0:T(1024)(128)(4,1)}), s8[4194304]{0:T(1024)(128)(4,1)S(1)}, s32[]{:S(2)}) async-start(s8[31850496]{0:T(1024)(128)(4,1)} %bitcast.114), calls=%async_computation.2 | async-start | bytes 8388608
  773.1 36.3 %slice-start.1 = ((s8[31850496]{0:T(1024)(128)(4,1)}), s8[4194304]{0:T(1024)(128)(4,1)S(1)}, s32[]{:S(2)}) async-start(s8[31850496]{0:T(1024)(128)(4,1)} %bitcast.114), calls=%async_computation.3 | async-start | bytes 8388608
  773.1 36.3 %slice-start.2 = ((s8[31850496]{0:T(1024)(128)(4,1)}), s8[4194304]{0:T(1024)(128)(4,1)S(1)}, s32[]{:S(2)}) async-start(s8[31850496]{0:T(1024)(128)(4,1)} %bitcast.114), calls=%async_computation.4 | async-start | bytes 8388608
  773.1 36.3 %slice-start.3 = ((s8[31850496]{0:T(1024)(128)(4,1)}), s8[4194304]{0:T(1024)(128)(4,1)S(1)}, s32[]{:S(2)}) async-start(s8[31850496]{0:T(1024)(128)(4,1)} %bitcast.114), calls=%async_computation.5 | async-start | bytes 8388608
  790.7 18.8 slice-start.4
  790.7 18.8 slice-start.5
  790.7 18.8 slice-start.6
  790.7 20.2 slice-start.7
  822.2 1365.6 %copy-start.42 = (f32[16128]{0:T(1024)S(1)}, f32[16128]{0:T(1024)}, u32[]{:S(2)}) copy-start(f32[16128]{0:T(1024)} %param.21) | copy-start | bytes 193540
  837.7 1350.1 %copy-start.35 = (f32[16128]{0:T(1024)S(1)}, f32[16128]{0:T(1024)}, u32[]{:S(2)}) copy-start(f32[16128]{0:T(1024)} %param.19) | copy-start | bytes 193540
  837.7 1350.1 %copy-start.41 = (f32[16128]{0:T(1024)S(1)}, f32[16128]{0:T(1024)}, u32[]{:S(2)}) copy-start(f32[16128]{0:T(1024)} %param.20) | copy-start | bytes 193540
  837.7 1350.8 %copy-start.6 = (f32[746496]{0:T(1024)S(1)}, f32[746496]{0:T(1024)}, u32[]{:S(2)}) copy-start(f32[746496]{0:T(1024)} %param.16) | copy-start | bytes 8957956
  (10 other events, 11.0 us)
Sparse Core Ops, SparseCore 0:
  11.5 265.8 all-gather.1
  821.6 1320.2 all-reduce.4
where the time goes:
time: 2220 us; the launch traced here: 2210 us
  waiting for transfers between devices  1570 us (71%)
  local copies, waits for them, and re-layouts  378 us (17%)
  matrix products  157 us (7%)
  other arithmetic  48.5 us (2%)
  blocking collectives  40.7 us (2%)
    unnamed x3, waiting for transfers between devices  1300 us
    all_gather x1, waiting for transfers between devices, on_device(): lax.all_gather(weights.astype(bf16), ('outer', 'inner'), axis=0, tiled=True)  261 us
    slice x12, local copies, waits for them, and re-layouts, unpack_mats(): lax.slice_in_dim(flat, offset, offset + height * breadth)  159 us
    unnamed x155, local copies, waits for them, and re-layouts  59.9 us
  transfers between devices with their start and end apart: 2, of which 2 were waited for; matrix products, arithmetic and copies ran while one was open for 1% of the time, Pallas kernels for 0%

commit v1 on v0

--- a/solution.py
+++ b/solution.py
@@ -1,8 +1,11 @@
+import functools
 import math
 
 import jax
 import jax.numpy as jnp
 from jax import lax
+from jax.experimental import pallas as pl
+from jax.experimental.pallas import tpu as pltpu
 from jax.sharding import PartitionSpec as P
 
 D = 1152
@@ -20,10 +23,535 @@
 ADAM_EPS = 1e-08
 WEIGHT_DECAY = 0.01
 CLIP_NORM = 1.0
+BLOCK_UNITS = 4 * D + 2 * FF
+
+MESH = pl.DeviceIdType.MESH
+UNITS = 648
+ROWS = 656
+QUART = 160
+HALFQ = 80
+MAIN = 640
+TAIL = 16
+DEPTH = (4, 4, 3)
+BASE = (0, 4, 8)
+
+
+def flip(z, d):
+    if d == 0:
+        return z
+    if d == 1:
+        return z + 1 - 2 * (z % 2)
+    if d == 2:
+        return z + 2 - 4 * (z // 2)
+    return 3 - z
+
+
+class Place:
+    def __init__(self):
+        self.o = lax.axis_index("outer")
+        self.i = lax.axis_index("inner")
+        self.x, self.c = self.o // 2, self.o % 2
+        self.z, self.y = self.i // 2, self.i % 2
+        self.xo, self.co, self.yo = 1 - self.x, 1 - self.c, 1 - self.y
+
+    def dev(self, dx=0, dc=0, dz=0, dy=0):
+        x = self.xo if dx else self.x
+        c = self.co if dc else self.c
+        y = self.yo if dy else self.y
+        return (x * 2 + c, flip(self.z, dz) * 2 + y)
+
+    def greet(self):
+        peers = [
+            self.dev(dx=1), self.dev(dc=1), self.dev(dx=1, dc=1), self.dev(dy=1),
+            self.dev(dz=1), self.dev(dz=2), self.dev(dz=3),
+        ]
+        barrier = pltpu.get_barrier_semaphore()
+        for peer in peers:
+            pl.semaphore_signal(barrier, inc=1, device_id=peer, device_id_type=MESH)
+        pl.semaphore_wait(barrier, len(peers))
+
+
+class Copies:
+    def __init__(self, send_sems, recv_sems):
+        self.send_sems, self.recv_sems = send_sems, recv_sems
+        self.count = 0
+        self.sent = []
+
+    def slot(self):
+        self.count += 1
+        return self.count - 1
+
+    def make(self, slot, src, dst, device):
+        return pltpu.make_async_remote_copy(
+            src_ref=src, dst_ref=dst, send_sem=self.send_sems.at[slot],
+            recv_sem=self.recv_sems.at[slot], device_id=device, device_id_type=MESH,
+        )
+
+    def send(self, slot, src, dst, device, cond=None):
+        def go():
+            self.make(slot, src, dst, device).start()
+        if cond is None:
+            go()
+        else:
+            pl.when(cond)(go)
+        self.sent.append((slot, src, dst, device, cond))
+
+    def wait_recv(self, slot, dst, device, cond=None):
+        def go():
+            self.make(slot, dst, dst, device).wait_recv()
+        if cond is None:
+            go()
+        else:
+            pl.when(cond)(go)
+
+    def drain(self):
+        for slot, src, dst, device, cond in self.sent:
+            def go(slot=slot, src=src, dst=dst, device=device):
+                self.make(slot, src, dst, device).wait_send()
+            if cond is None:
+                go()
+            else:
+                pl.when(cond)(go)
+        self.sent = []
+
+
+def rows16(start):
+    return pl.multiple_of(start, 16)
+
+
+def ok(zb, p):
+    return None if DEPTH[p] == 4 else zb < DEPTH[p]
+
+
+def both(a, b):
+    if a is None:
+        return b
+    if b is None:
+        return a
+    return jnp.logical_and(a, b)
+
+
+GATHER_COPIES = 3 * (3 + 3 + 4 * 4 + 8) + 7
+
+
+def gather_kernel(shard, full, send_sems, recv_sems, local_sems):
+    me = Place()
+    cp = Copies(send_sems, recv_sems)
+    me.greet()
+
+    def part(p, zb, yb, x, c, first=0, n=QUART):
+        return full.at[p, zb, yb, pl.ds(rows16(320 * x + QUART * c + first), n)]
+
+    def own_of(p):
+        return both(me.o == p, ok(me.z, p))
+
+    quarter = rows16(320 * me.x + QUART * me.c)
+    own_tail = pltpu.make_async_copy(
+        shard.at[pl.ds(MAIN, TAIL)], full.at[me.o, me.z, me.y, pl.ds(MAIN, TAIL)], local_sems.at[0]
+    )
+    own_tail.start()
+
+    def local_quarter(p):
+        return pltpu.make_async_copy(
+            shard.at[pl.ds(quarter, QUART)], part(p, me.z, me.y, me.x, me.c), local_sems.at[1]
+        )
+
+    slots = {}
+
+    def s0(p):
+        @pl.when(own_of(p))
+        def _():
+            local_quarter(p).start()
+        for dx, dc in ((1, 0), (0, 1), (1, 1)):
+            s = slots["s0", p, dx, dc] = cp.slot()
+            x = me.xo if dx else me.x
+            c = me.co if dc else me.c
+            cp.send(
+                s, shard.at[pl.ds(rows16(320 * x + QUART * c), QUART)],
+                part(p, me.z, me.y, x, c), me.dev(dx=dx, dc=dc), own_of(p),
+            )
+
+    def s0_wait(p):
+        @pl.when(own_of(p))
+        def _():
+            local_quarter(p).wait()
+        ox, oc = p // 2, p % 2
+        for dx, dc in ((1, 0), (0, 1), (1, 1)):
+            x = me.xo if dx else me.x
+            c = me.co if dc else me.c
+            cond = both(jnp.logical_and(x == ox, c == oc), ok(me.z, p))
+            cp.wait_recv(
+                slots["s0", p, dx, dc], part(p, me.z, me.y, me.x, me.c), me.dev(dx=dx, dc=dc), cond
+            )
+
+    def spread(p, d):
+        zb = flip(me.z, d)
+        mine = part(p, zb, me.y, me.x, me.c)
+        s = slots["y1", p, d] = cp.slot()
+        cp.send(s, mine, mine, me.dev(dy=1), ok(zb, p))
+        s = slots["x1", p, d] = cp.slot()
+        cp.send(s, mine, mine, me.dev(dx=1), ok(zb, p))
+
+    def s1(p):
+        s0_wait(p)
+        mine = part(p, me.z, me.y, me.x, me.c)
+        for d in (1, 2, 3):
+            s = slots["z", p, d] = cp.slot()
+            cp.send(s, mine, mine, me.dev(dz=d), ok(me.z, p))
+        spread(p, 0)
+
+    def s2(p):
+        for d in (1, 2, 3):
+            zb = flip(me.z, d)
+            cp.wait_recv(
+                slots["z", p, d], part(p, zb, me.y, me.x, me.c), me.dev(dz=d), ok(zb, p)
+            )
+            spread(p, d)
+
+    def s3(p):
+        for d in (0, 1, 2, 3):
+            zb = flip(me.z, d)
+            cp.wait_recv(
+                slots["y1", p, d], part(p, zb, me.yo, me.x, me.c), me.dev(dy=1), ok(zb, p)
+            )
+            s = slots["x2", p, d] = cp.slot()
+            out = part(p, zb, me.yo, me.x, me.c, 0, HALFQ)
+            cp.send(s, out, out, me.dev(dx=1), ok(zb, p))
+            cp.wait_recv(
+                slots["x1", p, d], part(p, zb, me.y, me.xo, me.c), me.dev(dx=1), ok(zb, p)
+            )
+            s = slots["y2", p, d] = cp.slot()
+            out = part(p, zb, me.y, me.xo, me.c, HALFQ, HALFQ)
+            cp.send(s, out, out, me.dev(dy=1), ok(zb, p))
+
+    def lane(p, zb, x, c):
+        return full.at[p, zb, :, pl.ds(rows16(320 * x + QUART * c), QUART)]
+
+    def s4(p):
+        for d in (0, 1, 2, 3):
+            zb = flip(me.z, d)
+            cp.wait_recv(
+                slots["x2", p, d], part(p, zb, me.yo, me.xo, me.c, 0, HALFQ), me.dev(dx=1),
+                ok(zb, p),
+            )
+            cp.wait_recv(
+                slots["y2", p, d], part(p, zb, me.yo, me.xo, me.c, HALFQ, HALFQ), me.dev(dy=1),
+                ok(zb, p),
+            )
+            for h in (0, 1):
+                s = slots["c", p, d, h] = cp.slot()
+                cp.send(s, lane(p, zb, h, me.c), lane(p, zb, h, me.c), me.dev(dc=1), ok(zb, p))
+
+    def s5(p):
+        for d in (0, 1, 2, 3):
+            zb = flip(me.z, d)
+            for h in (0, 1):
+                cp.wait_recv(
+                    slots["c", p, d, h], lane(p, zb, h, me.co), me.dev(dc=1), ok(zb, p)
+                )
+
+    tails = pl.ds(MAIN, TAIL)
+
+    def t1():
+        own_tail.wait()
+        block = full.at[me.o, me.z, me.y, tails]
+        for d in (1, 2, 3):
+            s = slots["tz", d] = cp.slot()
+            cp.send(s, block, block, me.dev(dz=d))
+
+    def t2():
+        for d in (1, 2, 3):
+            zb = flip(me.z, d)
+            cp.wait_recv(slots["tz", d], full.at[me.o, zb, me.y, tails], me.dev(dz=d))
+        s = slots["ty"] = cp.slot()
+        block = full.at[me.o, :, me.y, tails]
+        cp.send(s, block, block, me.dev(dy=1))
+
+    def t3():
+        cp.wait_recv(slots["ty"], full.at[me.o, :, me.yo, tails], me.dev(dy=1))
+        s = slots["tx"] = cp.slot()
+        block = full.at[me.o, :, :, tails]
+        cp.send(s, block, block, me.dev(dx=1))
+
+    def t4():
+        cp.wait_recv(slots["tx"], full.at[me.xo * 2 + me.c, :, :, tails], me.dev(dx=1))
+        for h in (0, 1):
+            s = slots["tc", h] = cp.slot()
+            block = full.at[h * 2 + me.c, :, :, tails]
+            cp.send(s, block, block, me.dev(dc=1))
+
+    def t5():
+        for h in (0, 1):
+            cp.wait_recv(slots["tc", h], full.at[h * 2 + me.co, :, :, tails], me.dev(dc=1))
+
+    s0(0); s0(1); s0(2); s1(0); t1(); s2(0); s1(1); s3(0); t2(); s2(1); s1(2); s4(0); t3()
+    s3(1); s2(2); s5(0); s4(1); t4(); s3(2); s5(1); s4(2); s5(2); t5()
+    cp.drain()
+
+
+def gather_weights(shard):
+    return pl.pallas_call(
+        gather_kernel,
+        out_shape=jax.ShapeDtypeStruct((4, 4, 2, ROWS, D), jnp.bfloat16),
+        in_specs=[pl.BlockSpec(memory_space=pl.ANY)],
+        out_specs=pl.BlockSpec(memory_space=pl.ANY),
+        scratch_shapes=[
+            pltpu.SemaphoreType.DMA((GATHER_COPIES,)),
+            pltpu.SemaphoreType.DMA((GATHER_COPIES,)),
+            pltpu.SemaphoreType.DMA((2,)),
+        ],
+        compiler_params=pltpu.CompilerParams(collective_id=0, has_side_effects=True),
+        name="gather_weights",
+    )(shard)
+
+
+SCATTER_COPIES = 3 * (4 * 2 + 4 * 4 + 3 + 3) + 8
+f32 = jnp.float32
+
+
+def add_rows(dst, srcs, n, step=16):
+    def body(j, carry):
+        at = pl.ds(pl.multiple_of(j * step, step), step)
+        total = srcs[0][at].astype(f32)
+        for src in srcs[1:]:
+            total = total + src[at].astype(f32)
+        dst[at] = total.astype(dst.dtype)
+        return carry
+
+    lax.fori_loop(0, n // step, body, 0)
+
+
+def scatter_kernel(
+    partial, out, own, other, rx2, ry2, rx1, ry1, rz, final, tail, tail_in, tail_z,
+    send_sems, recv_sems, local_sems,
+):
+    me = Place()
+    cp = Copies(send_sems, recv_sems)
+    me.greet()
+    slots = {}
+    order = (3, 2, 1, 0)
+
+    def guarded(cond, fn):
+        if cond is None:
+            fn()
+        else:
+            pl.when(cond)(fn)
+
+    def load(p, d, h):
+        zb = flip(me.z, d)
+        return pltpu.make_async_copy(
+            partial.at[p, zb, :, pl.ds(rows16(320 * h + QUART * me.c), QUART)],
+            own.at[BASE[p] + zb, :, h], local_sems.at[(p * 4 + d) * 2 + h],
+        )
+
+    def s0(p):
+        for d in order:
+            zb = flip(me.z, d)
+            for h in (0, 1):
+                guarded(ok(zb, p), lambda d=d, h=h: load(p, d, h).start())
+                s = slots["c", p, d, h] = cp.slot()
+                cp.send(
+                    s, partial.at[p, zb, :, pl.ds(rows16(320 * h + QUART * me.co), QUART)],
+                    other.at[BASE[p] + zb, :, h], me.dev(dc=1), ok(zb, p),
+                )
+
+    def s1(p):
+        for d in order:
+            zb = flip(me.z, d)
+            b = BASE[p] + zb
+            for h in (0, 1):
+                guarded(ok(zb, p), lambda d=d, h=h: load(p, d, h).wait())
+                cp.wait_recv(slots["c", p, d, h], other.at[b, :, h], me.dev(dc=1), ok(zb, p))
+
+            def fold(b=b):
+                def body(q, carry):
+                    add_rows(own.at[b, q // 2, q % 2], [own.at[b, q // 2, q % 2], other.at[b, q // 2, q % 2]], QUART)
+                    return carry
+                lax.fori_loop(0, 4, body, 0)
+            guarded(ok(zb, p), fold)
+            s = slots["x2", p, d] = cp.slot()
+            cp.send(s, own.at[b, me.yo, me.xo, pl.ds(0, HALFQ)], rx2.at[b], me.dev(dx=1), ok(zb, p))
+            s = slots["y2", p, d] = cp.slot()
+            cp.send(s, own.at[b, me.yo, me.xo, pl.ds(HALFQ, HALFQ)], ry2.at[b], me.dev(dy=1), ok(zb, p))
+
+    def s2(p):
+        for d in order:
+            zb = flip(me.z, d)
+            b = BASE[p] + zb
+            cp.wait_recv(slots["x2", p, d], rx2.at[b], me.dev(dx=1), ok(zb, p))
+            view = own.at[b, me.yo, me.x, pl.ds(0, HALFQ)]
+            guarded(ok(zb, p), lambda view=view, b=b: add_rows(view, [view, rx2.at[b]], HALFQ))
+            s = slots["y1", p, d] = cp.slot()
+            cp.send(s, own.at[b, me.yo, me.x], ry1.at[b], me.dev(dy=1), ok(zb, p))
+            cp.wait_recv(slots["y2", p, d], ry2.at[b], me.dev(dy=1), ok(zb, p))
+            view = own.at[b, me.y, me.xo, pl.ds(HALFQ, HALFQ)]
+            guarded(ok(zb, p), lambda view=view, b=b: add_rows(view, [view, ry2.at[b]], HALFQ))
+            s = slots["x1", p, d] = cp.slot()
+            cp.send(s, own.at[b, me.y, me.xo], rx1.at[b], me.dev(dx=1), ok(zb, p))
+
+    def s3(p):
+        for d in order:
+            zb = flip(me.z, d)
+            b = BASE[p] + zb
+            cp.wait_recv(slots["y1", p, d], ry1.at[b], me.dev(dy=1), ok(zb, p))
+            cp.wait_recv(slots["x1", p, d], rx1.at[b], me.dev(dx=1), ok(zb, p))
+            view = own.at[b, me.y, me.x]
+            guarded(
+                ok(zb, p),
+                lambda view=view, b=b: add_rows(view, [view, ry1.at[b], rx1.at[b]], QUART),
+            )
+            if d:
+                s = slots["z", p, d] = cp.slot()
+                cp.send(s, view, rz.at[p, d - 1], me.dev(dz=d), ok(zb, p))
+
+    def s4(p):
+        mine = ok(me.z, p)
+        for d in (1, 2, 3):
+            cp.wait_recv(slots["z", p, d], rz.at[p, d - 1], me.dev(dz=d), mine)
+        view = own.at[BASE[p] + me.z, me.y, me.x]
+        guarded(
+            mine,
+            lambda: add_rows(final.at[p], [view, rz.at[p, 0], rz.at[p, 1], rz.at[p, 2]], QUART),
+        )
+        ox, oc = p // 2, p % 2
+        quarter = out.at[pl.ds(rows16(320 * me.x + QUART * me.c), QUART)]
+        for dx, dc in ((1, 0), (0, 1), (1, 1)):
+            x = me.xo if dx else me.x
+            c = me.co if dc else me.c
+            s = slots["f", p, dx, dc] = cp.slot()
+            cond = both(jnp.logical_and(x == ox, c == oc), mine)
+            cp.send(s, final.at[p], quarter, me.dev(dx=dx, dc=dc), cond)
+
+        @pl.when(both(me.o == p, mine))
+        def _():
+            pltpu.make_async_copy(final.at[p], quarter, local_sems.at[24]).start()
+
+    def s5(p):
+        mine = both(me.o == p, ok(me.z, p))
+        for dx, dc in ((1, 0), (0, 1), (1, 1)):
+            x = me.xo if dx else me.x
+            c = me.co if dc else me.c
+            cp.wait_recv(
+                slots["f", p, dx, dc], out.at[pl.ds(rows16(320 * x + QUART * c), QUART)],
+                me.dev(dx=dx, dc=dc), mine,
+            )
+
+        @pl.when(mine)
+        def _():
+            quarter = out.at[pl.ds(rows16(320 * me.x + QUART * me.c), QUART)]
+            pltpu.make_async_copy(final.at[p], quarter, local_sems.at[24]).wait()
+
+    tail_load = pltpu.make_async_copy(
+        partial.at[:, :, :, pl.ds(MAIN, TAIL)], tail, local_sems.at[25]
+    )
+    tail_load.start()
+
+    def tail_add(o, zb, yb, srcs):
+        add_rows(tail.at[o, zb, yb], [tail.at[o, zb, yb]] + srcs, TAIL)
+
+    def t1():
+        tail_load.wait()
+        for h in (0, 1):
+            s = slots["tc", h] = cp.slot()
+            cp.send(s, tail.at[2 * h + me.co], tail_in.at[h], me.dev(dc=1))
+
+    def t2():
+        for h in (0, 1):
+            cp.wait_recv(slots["tc", h], tail_in.at[h], me.dev(dc=1))
+
+            def body(q, carry, h=h):
+                tail_add(2 * h + me.c, q // 2, q % 2, [tail_in.at[h, q // 2, q % 2]])
+                return carry
+            lax.fori_loop(0, 8, body, 0)
+        s = slots["tx"] = cp.slot()
+        cp.send(s, tail.at[me.xo * 2 + me.c], tail_in.at[2], me.dev(dx=1))
+
+    def t3():
+        cp.wait_recv(slots["tx"], tail_in.at[2], me.dev(dx=1))
+
+        def body(q, carry):
+            tail_add(me.o, q // 2, q % 2, [tail_in.at[2, q // 2, q % 2]])
+            return carry
+        lax.fori_loop(0, 8, body, 0)
+        s = slots["ty"] = cp.slot()
+        cp.send(s, tail.at[me.o, :, me.yo], tail_in.at[3, :, 0], me.dev(dy=1))
+
+    def t4():
+        cp.wait_recv(slots["ty"], tail_in.at[3, :, 0], me.dev(dy=1))
+
+        def body(q, carry):
+            tail_add(me.o, q, me.y, [tail_in.at[3, q, 0]])
+            return carry
+        lax.fori_loop(0, 4, body, 0)
+        for d in (1, 2, 3):
+            s = slots["tz", d] = cp.slot()
+            cp.send(s, tail.at[me.o, flip(me.z, d), me.y], tail_z.at[d - 1], me.dev(dz=d))
+
+    def t5():
+        for d in (1, 2, 3):
+            cp.wait_recv(slots["tz", d], tail_z.at[d - 1], me.dev(dz=d))
+        tail_add(me.o, me.z, me.y, [tail_z.at[0], tail_z.at[1], tail_z.at[2]])
+        copy = pltpu.make_async_copy(
+            tail.at[me.o, me.z, me.y], out.at[pl.ds(MAIN, TAIL)], local_sems.at[25]
+        )
+        copy.start()
+        copy.wait()
+
+    s0(2); s0(1); s0(0); s1(2); t1(); s1(1); s2(2); t2(); s1(0); s3(2); s2(1); t3(); s4(2)
+    s2(0); s3(1); t4(); s4(1); s3(0); t5(); s4(0); s5(2); s5(1); s5(0)
+    cp.drain()
+
+
+def scatter_grads_kernel(partial):
+    bf = jnp.bfloat16
+    return pl.pallas_call(
+        scatter_kernel,
+        out_shape=jax.ShapeDtypeStruct((ROWS, D), bf),
+        in_specs=[pl.BlockSpec(memory_space=pl.ANY)],
+        out_specs=pl.BlockSpec(memory_space=pl.ANY),
+        scratch_shapes=[
+            pltpu.VMEM((11, 2, 2, QUART, D), bf),
+            pltpu.VMEM((11, 2, 2, QUART, D), bf),
+            pltpu.VMEM((11, HALFQ, D), bf),
+            pltpu.VMEM((11, HALFQ, D), bf),
+            pltpu.VMEM((11, QUART, D), bf),
+            pltpu.VMEM((11, QUART, D), bf),
+            pltpu.VMEM((3, 3, QUART, D), bf),
+            pltpu.VMEM((3, QUART, D), bf),
+            pltpu.VMEM((4, 4, 2, TAIL, D), bf),
+            pltpu.VMEM((4, 4, 2, TAIL, D), bf),
+            pltpu.VMEM((3, TAIL, D), bf),
+            pltpu.SemaphoreType.DMA((SCATTER_COPIES,)),
+            pltpu.SemaphoreType.DMA((SCATTER_COPIES,)),
+            pltpu.SemaphoreType.DMA((26,)),
+        ],
+        compiler_params=pltpu.CompilerParams(
+            collective_id=1, has_side_effects=True, vmem_limit_bytes=60 * 2**20
+        ),
+        name="scatter_grads",
+    )(partial)
+
+def gather_blocks(shard_low, kernels):
+    if not kernels:
+        whole = lax.all_gather(shard_low, ("outer", "inner"), axis=0, tiled=True)
+        return whole[:BLOCK_UNITS]
+    padded = jnp.pad(shard_low, ((0, ROWS - UNITS), (0, 0)))
+    return gather_weights(padded).reshape(32, ROWS, D)[:22, :UNITS].reshape(-1, D)[:BLOCK_UNITS]
+
+
+def scatter_blocks(grads, units, kernels):
+    axes = ("outer", "inner")
+    if not kernels:
+        count = lax.axis_size(axes) * units
+        padded = jnp.pad(grads, ((0, count - BLOCK_UNITS), (0, 0)))
+        return lax.psum_scatter(padded, axes, scatter_dimension=0, tiled=True)
+    padded = jnp.pad(grads, ((0, 32 * UNITS - BLOCK_UNITS), (0, 0))).reshape(32, UNITS, D)
+    padded = jnp.pad(padded, ((0, 0), (0, ROWS - UNITS), (0, 0))).reshape(4, 4, 2, ROWS, D)
+    return scatter_grads_kernel(padded)[:UNITS].astype(jnp.float32)
 
 
 def unpack_mats(flat):
-    shapes = [(D, 3 * D), (D, D), (D, FF), (FF, D), (D, 6 * D)]
+    shapes = [(D, 3 * D), (D, D), (D, FF), (FF, D)]
     pieces = []
     offset = 0
     for height, breadth in shapes:
@@ -74,29 +602,23 @@
     )
 
 
-def scatter_grads(flat_grad):
-    return lax.psum_scatter(flat_grad, ("outer", "inner"), scatter_dimension=0, tiled=True)
-
-
-def ada_pieces(grad_mods_all, soft_cond, w_ada, conditioning):
-    highest = lax.Precision.HIGHEST
-    grad_b_ada = jnp.sum(grad_mods_all, axis=0)
-    grad_w_ada = lax.dot_general(
-        soft_cond.astype(jnp.float32),
-        grad_mods_all,
-        (((0,), (0,)), ((), ())),
-        precision=highest,
-        preferred_element_type=jnp.float32,
-    )
-    grad_soft = lax.dot_general(
-        grad_mods_all,
-        w_ada.astype(jnp.float32),
-        (((1,), (1,)), ((), ())),
-        precision=highest,
-        preferred_element_type=jnp.float32,
-    )
-    silu_out, silu_back = jax.vjp(jax.nn.silu, conditioning)
-    return (grad_b_ada, grad_w_ada, silu_back(grad_soft)[0])
+def exact(left, right, dims):
+    return lax.dot_general(
+        left, right, dims, precision=lax.Precision.HIGHEST, preferred_element_type=jnp.float32
+    )
+
+
+def ada_selector(soft_cond, first_unit, units):
+    groups = soft_cond.shape[0]
+    spread = jnp.repeat(soft_cond.astype(jnp.float32), 6, axis=1)
+    spread = jnp.pad(spread, ((0, 0), (units, units)))
+    start = jnp.clip(first_unit - BLOCK_UNITS + units, 0, 6 * D + units)
+    local = lax.dynamic_slice(spread, (jnp.int32(0), start), (groups, units))
+    unit = first_unit - BLOCK_UNITS + jnp.arange(units, dtype=jnp.int32)
+    part = (unit[:, None] % 6 == jnp.arange(6, dtype=jnp.int32)[None, :]) & (unit[:, None] >= 0)
+    part = part.astype(jnp.float32)
+    selector = local.T[:, :, None] * part[:, None, :]
+    return selector.reshape(units, groups * 6), part
 
 
 def adamw(parameter, gradient, first_state, second_state):
@@ -122,6 +644,7 @@
     biases,
     bias_first,
     bias_second,
+    kernels,
 ):
     bf16 = jnp.bfloat16
     highest = lax.Precision.HIGHEST
@@ -129,11 +652,17 @@
     groups = conditioning.shape[0]
     row_count = columns * FRAMES
     score_scale = 1.0 / math.sqrt(HD)
-    gathered = lax.all_gather(weights.astype(bf16), ("outer", "inner"), axis=0, tiled=True)
-    w_qkv, w_proj, w_up, w_down, w_ada = unpack_mats(gathered)
+    units = weights.shape[0] // D
+    axes = ("outer", "inner")
+    first_unit = lax.axis_index(axes).astype(jnp.int32) * units
+    shard = weights.reshape(units, D)
+    shard_low = shard.astype(bf16)
+    w_qkv, w_proj, w_up, w_down = unpack_mats(gather_blocks(shard_low, kernels).reshape(-1))
     b_query, b_value, b_proj, b_up, b_down, b_ada = split_bias(biases)
     soft_cond = jax.nn.silu(conditioning).astype(bf16)
-    mods_all = plain_dot(soft_cond, w_ada) + b_ada
+    selector, ada_part = ada_selector(soft_cond, first_unit, units)
+    mods_all = left_dot(selector.astype(bf16), shard_low)
+    mods_all = lax.psum(mods_all, axes).reshape(groups, 6 * D) + b_ada
     mods = jnp.take(mods_all, column_sample, axis=0)
     video_cols = jnp.take(1.0 - is_image.astype(jnp.float32), column_sample)
     mod_parts = mods.reshape(columns, 1, 6, D)
@@ -168,8 +697,6 @@
     result = middle + gate_mlp * outcome
     is_video = video_cols[:, None, None] > 0.5
     block_out = jnp.where(is_video, result, states).reshape(row_count, D)
-    regathered = lax.all_gather(weights.astype(bf16), ("outer", "inner"), axis=0, tiled=True)
-    w_qkv, w_proj, w_up, w_down, w_ada = unpack_mats(regathered)
     upstream = output_grad.astype(jnp.float32).reshape(columns, FRAMES, D)
     grad_block = jnp.where(is_video, upstream, 0.0)
     grad_gate_mlp = jnp.sum(grad_block * outcome, axis=1)
@@ -250,21 +777,28 @@
         precision=highest,
         preferred_element_type=jnp.float32,
     )
-    prefix_grad = jnp.concatenate(
-        [
-            grad_w_qkv.reshape(-1),
-            grad_w_proj.reshape(-1),
-            grad_w_up.reshape(-1),
-            grad_w_down.reshape(-1),
-        ]
-    )
+    block_grads = [
+        grad.astype(bf16 if kernels else jnp.float32).reshape(-1, D)
+        for grad in (grad_w_qkv, grad_w_proj, grad_w_up, grad_w_down)
+    ]
     bias_head = jnp.concatenate([grad_b_query, grad_b_value, grad_b_proj, grad_b_up, grad_b_down])
-    grad_b_ada, grad_w_ada, cond_local = ada_pieces(mods_local, soft_cond, w_ada, conditioning)
-    flat_grad = jnp.concatenate([prefix_grad, grad_w_ada.reshape(-1)])
-    first_small = jnp.concatenate([bias_head, grad_b_ada])
-    first_sum, second_sum = lax.psum((first_small, cond_local), ("outer", "inner"))
-    grad_shard = scatter_grads(flat_grad)
-    square_sum = lax.psum(jnp.sum(grad_shard * grad_shard), ("outer", "inner"))
+    bias_head, grad_mods_all = lax.psum((bias_head, mods_local), axes)
+    first_sum = jnp.concatenate([bias_head, jnp.sum(grad_mods_all, axis=0)])
+    block_shard = scatter_blocks(jnp.concatenate(block_grads), units, kernels)
+    mods_parts = grad_mods_all.reshape(groups * 6, D)
+    ada_shard = exact(selector, mods_parts, (((1,), (0,)), ((), ())))
+    unit = first_unit + jnp.arange(units, dtype=jnp.int32)
+    grad_units = jnp.where(unit[:, None] >= BLOCK_UNITS, ada_shard, block_shard)
+    products = exact(shard_low.astype(jnp.float32), mods_parts, (((1,), (1,)), ((), ())))
+    products = jnp.sum(products.reshape(units, groups, 6) * ada_part[:, None, :], axis=2)
+    spread = jnp.zeros((groups, 6 * D + 2 * units), jnp.float32)
+    start = jnp.clip(first_unit - BLOCK_UNITS + units, 0, 6 * D + units)
+    spread = lax.dynamic_update_slice(spread, products.T, (jnp.int32(0), start))
+    grad_soft = jnp.sum(spread[:, units : units + 6 * D].reshape(groups, D, 6), axis=2)
+    square_sum, grad_soft = lax.psum((jnp.sum(grad_units * grad_units), grad_soft), axes)
+    silu_out, silu_back = jax.vjp(jax.nn.silu, conditioning)
+    second_sum = silu_back(grad_soft)[0]
+    grad_shard = grad_units.reshape(-1)
     grad_norm = jnp.sqrt(square_sum + jnp.sum(first_sum * first_sum))
     factor = jnp.minimum(1.0, CLIP_NORM / (grad_norm + 1e-06))
     new_weights, first_out, second_out = adamw(
@@ -313,6 +847,7 @@
         P(),
         P(),
     )
+    kernels = dict(mesh.shape) == {"outer": 4, "inner": 8}
     return jax.shard_map(
-        on_device, mesh=mesh, in_specs=in_specs, out_specs=out_specs, check_vma=False
-    )
+        functools.partial(on_device, kernels=kernels), mesh=mesh, in_specs=in_specs, out_specs=out_specs, check_vma=False
+    )

time: 2220 us -> 923 us (0.42)
  waiting for transfers between devices: 1570 us -> 0.06 us
  Pallas kernels: 0 us -> 350 us
  local copies, waits for them, and re-layouts: 378 us -> 231 us
  other arithmetic: 48.5 us -> 158 us
  matrix products: 157 us -> 119 us
    unnamed x3 -> x2, waiting for transfers between devices: 1300 us -> 0.03 us
    pallas_call x0 -> x2, Pallas kernels: none -> 350 us  [the longest x1 185 us: scatter_grads_kernel(): pl.pallas_call(scatter_kernel, out_shape=jax.ShapeDtypeStruct((ROWS, D),...]
    all_gather x1 -> x0, waiting for transfers between devices: 261 us -> none  [on_device(): lax.all_gather(weights.astype(bf16), ('outer', 'inner'), axis=0, tiled=True)]
    slice x12 -> x2, local copies, waits for them, and re-layouts: 159 us -> 16.9 us  [unpack_mats(): lax.slice_in_dim(flat, offset, offset + height * breadth)]
    concatenate x0 -> x1, other arithmetic: none -> 114 us  [on_device(): block_shard = scatter_blocks(jnp.concatenate(block_grads), units, kernels)]
    unnamed x155 -> x122, local copies, waits for them, and re-layouts: 59.9 us -> 4.19 us
    pad x0 -> x2, local copies, waits for them, and re-layouts: none -> 33.6 us  [the longest x1 32.4 us: scatter_blocks(): jnp.pad(padded, ((0, 0), (0, ROWS - UNITS), (0, 0)))]
    dot_general x2, matrix products: 32.5 us -> 6.43 us  [exact(): lax.dot_general(left, right, dims, precision=lax.Precision.HIGHEST, prefe...]
  transfers between devices with their start and end apart: 2 -> 2, of which waited for: 2 -> 0; matrix products, arithmetic and copies ran while one was open for 1% -> 31% of each run, Pallas kernels for 0% -> 38%
where the time goes in v1:
time: 923 us; the launch traced here: 915 us
  Pallas kernels  350 us (38%)
  local copies, waits for them, and re-layouts  231 us (25%)
  other arithmetic  158 us (17%)
  matrix products  119 us (13%)
  blocking collectives  38.5 us (4%)
  between operations  18 us (2%)
    pallas_call x1, Pallas kernels, scatter_grads_kernel(): pl.pallas_call(scatter_kernel, out_shape=jax.ShapeDtypeStruct((ROWS, D),...  185 us
    pallas_call x1, Pallas kernels, gather_weights(): pl.pallas_call(gather_kernel, out_shape=jax.ShapeDtypeStruct((4, 4, 2, RO...  165 us
    concatenate x1, other arithmetic, on_device(): block_shard = scatter_blocks(jnp.concatenate(block_grads), units, kernels)  114 us
    reshape x4, local copies, waits for them, and re-layouts, unpack_mats(): lax.slice_in_dim(flat, offset, offset + height * breadth)  58.4 us
    psum x1, blocking collectives, on_device(): lax.psum((jnp.sum(grad_units * grad_units), grad_soft), axes)  38.5 us
    dot_general x4, matrix products, right_dot(): lax.dot_general(left_side, right_side, (((1,), (1,)), ((), ())), preferre...  36.9 us
    dot_general x4, matrix products, plain_dot(): return jnp.dot(left_side, right_side, preferred_element_type=jnp.float32)  33.3 us
    pad x1, local copies, waits for them, and re-layouts, scatter_blocks(): jnp.pad(padded, ((0, 0), (0, ROWS - UNITS), (0, 0)))  32.4 us
  transfers between devices with their start and end apart: 2, of which 0 were waited for; matrix products, arithmetic and copies ran while one was open for 31% of the time, Pallas kernels for 38%

profile of v1, /device:TPU:0, one launch (start us, length us, event | category | flops | bytes accessed | tf_op | source)
XLA Modules:
  0.0 915.2 jit_solution(975979904925154889)
XLA Ops:
  8.0 2.0 convert_element_type.133
  10.0 1.7 convert_element_type.134
  11.8 1.7 broadcast_in_dim.91
  13.5 2.6 reshape.375
  18.6 1.9 fusion.77
  21.9 1.2 pad.17.shard
  23.1 165.3 %gather_weights.1 = bf16[4,4,2,656,1152]{4,3,2,1,0:T(8,128)(2,1)} custom-call(bf16[656,1152]{1,0:T(8,128)(2,1)} %pad.17.shard), custom_call_target="tpu_custom_call" | custom-call | tf_op jit(solution)/shard_map/gather_weights/pallas_call | solution.py:293
  188.4 22.7 %slice.114 = bf16[22,648,1152]{2,1,0:T(8,128)(2,1)} slice(bf16[32,656,1152]{2,1,0:T(8,128)(2,1)} %bitcast.129), slice={[0:22], [0:648], [0:1152]} | slice | bytes 65691648 | tf_op jit(solution)/shard_map/slice | solution.py:539
  211.1 7.0 slice.115
  218.1 12.8 %reshape.423 = bf16[1152,3456,1]{1,0,2:T(8,128)(2,1)} reshape(bf16[3456,1152]{1,0:T(8,128)(2,1)} %slice.115) | data formatting | bytes 15925248 | tf_op jit(solution)/shard_map/reshape | solution.py:559
  230.9 12.8 %reshape.379 = bf16[1152,3456]{1,0:T(8,128)(2,1)} reshape(bf16[3456,1152]{1,0:T(8,128)(2,1)} %slice.115) | data formatting | bytes 15925248 | tf_op jit(solution)/shard_map/reshape | solution.py:559
  243.8 9.9 %slice.123 = bf16[4608,1152]{1,0:T(8,128)(2,1)} slice(bf16[14256,1152]{1,0:T(8,128)(2,1)} %bitcast.131), slice={[4608:9216], [0:1152]} | slice | bytes 21233664 | tf_op jit(solution)/shard_map/slice | solution.py:559
  253.7 16.3 %reshape.422 = bf16[1152,4608,1]{1,0,2:T(8,128)(2,1)} reshape(bf16[4608,1152]{1,0:T(8,128)(2,1)} %slice.123) | data formatting | bytes 21233664 | tf_op jit(solution)/shard_map/reshape | solution.py:559
  270.0 16.4 %reshape.383 = bf16[1152,4608]{1,0:T(8,128)(2,1)} reshape(bf16[4608,1152]{1,0:T(8,128)(2,1)} %slice.123) | data formatting | bytes 21233664 | tf_op jit(solution)/shard_map/reshape | solution.py:559
  291.5 7.6 fusion.21
  299.1 1.6 fusion.83
  300.7 4.0 reshape.381
  304.6 5.0 reshape.382
  309.6 4.6 reshape.380
  314.2 2.4 fusion.54
  316.6 12.3 %fusion.87 = (f32[24,16,16]{2,1,0:T(8,128)S(1)}, f32[24,16,16,16]{2,3,1,0:T(8,128)S(1)}) fusion(f32[24,16,16,16]{2,3,1,0:T(8,128)S(1)} %fusion.54), kind=kOutput, calls=%fused_computation.185 | output fusion | flops 393231 | bytes 811008 | tf_op jit(solution)/shard_map/sub | solution.py:683
  331.0 2.7 convert_element_type.140
  333.7 3.5 fusion.60
  338.4 7.8 convolution_add_fusion
  346.3 14.4 %convert_reduce_fusion.2 = (f32[1152]{0:T(1024)}, bf16[384,1152]{1,0:T(8,128)(2,1)S(1)}, f32[384,1152]{1,0:T(8,128)}, f32[384,1152]{1,0:T(8,128)}) fusion(f32[24,1152]{1,0:T(8,128)S(1)} %get-tuple-element.74, bf16[384,1152]{1,0:T(8,128)(2,1)S(1)} %copy-done.17, pred[384]{0:T(512)(128)(4,1)S(1)} %broadcast_in_dim.88, f32[384,1152]{1,0:T(8,128)S(1)} %get-tuple-element.62, ...), kind=kOutput, calls=%fused_computation.69 | convolution fusion | flops 4098538496 | bytes 25888128 | tf_op jit(solution)/shard_map/dot_general | solution.py:590
  360.7 12.5 %convert_reduce_fusion = (f32[4608]{0:T(1024)}, bf16[384,4608]{1,0:T(8,128)(2,1)}) fusion(f32[384,4608]{1,0:T(8,128)S(1)} %convolution_add_fusion, bf16[384,1152]{1,0:T(8,128)(2,1)S(1)} %get-tuple-element.26, bf16[14256,1152]{1,0:T(8,128)(2,1)} %bitcast.134), kind=kOutput, calls=%fused_computation.28 | convolution fusion | flops 4115787264 | bytes 22136832 | tf_op jit(solution)/shard_map/dot_general | solution.py:600
  373.2 12.7 %multiply_reduce_fusion.4 = (f32[24,1152]{1,0:T(8,128)}, f32[24,16]{1,0:T(8,128)S(1)}, f32[24,16]{1,0:T(8,128)S(1)}, f32[24,1152]{1,0:T(8,128)}, f32[24,16,1152]...) fusion(f32[24,1152]{1,0:T(8,128)S(1)} %get-tuple-element.73, f32[24,16]{1,0:T(8,128)S(1)} %rsqrt.26, ...), kind=kOutput, calls=%fused_computation.72 | convolution fusion | flops 4082115584 | bytes 22566912 | tf_op jit(solution)/shard_map/dot_general | solution.py:600
  385.9 4.6 convert_reduce_fusion.3
  390.5 4.2 convolution_convert_fusion.4
  394.7 3.2 convolution_convert_fusion.3
  397.9 4.4 reshape.388
  402.3 3.8 fusion.45
  406.1 1.3 multiply_reduce_fusion
  410.2 1.8 fusion.46
  412.4 2.5 reshape.396
  415.0 2.5 concatenate.28
  417.5 1.8 copy.41
  419.3 2.5 reshape.395
  421.8 2.5 concatenate.27
  424.3 1.8 copy.45
  426.2 2.6 reshape.397
  428.7 2.5 concatenate.29
  431.2 11.7 %convolution_convert_fusion = bf16[4608,1152]{1,0:T(8,128)(2,1)} fusion(bf16[384,1152]{1,0:T(8,128)(2,1)} %copy-done.29, f32[384,4608]{1,0:T(8,128)} %copy-done.9), kind=kOutput, calls=%fused_computation.10 | convolution fusion | flops 4098097152 | bytes 18579456 | tf_op jit(solution)/shard_map/dot_general | solution.py:594
  443.1 0.9 copy-done.16
  444.7 6.7 convolution_convert_fusion.2
  451.5 8.6 convolution_convert_fusion.1
  461.6 7.5 multiply_reduce_fusion.6
  469.1 1.6 stack.22
  472.1 3.9 multiply_reduce_fusion.3
  476.3 2.3 stack.27
  478.8 1.1 fusion.67
  479.9 12.9 %reshape.398 = bf16[3456,1152]{1,0:T(8,128)(2,1)} reshape(bf16[1152,3456]{1,0:T(8,128)(2,1)} %convolution_convert_fusion.2) | data formatting | bytes 15925248 | tf_op jit(solution)/shard_map/reshape | solution.py:781
  492.8 16.5 %reshape.399 = bf16[4608,1152]{1,0:T(8,128)(2,1)} reshape(bf16[1152,4608]{1,0:T(8,128)(2,1)} %convolution_convert_fusion.1) | data formatting | bytes 21233664 | tf_op jit(solution)/shard_map/reshape | solution.py:781
  509.3 114.4 %fusion.7 = bf16[20736,1152]{1,0:T(8,128)(2,1)} fusion(bf16[4608,1152]{1,0:T(8,128)(2,1)} %convolution_convert_fusion, bf16[4608,1152]{1,0:T(8,128)(2,1)} %reshape.399, bf16[1152,1152]{1,0:T(8,128)(2,1)S(1)} %copy-done.18, bf16[3456,1152]{1,0:T(8,128)(2,1)} %reshape.398), kind=kLoop, calls=%fused_computation.9 | loop fusion | flops 310542336 | bytes 79626240 | tf_op jit(solution)/shard_map/concatenate | solution.py:787
  623.7 32.4 %pad.19 = bf16[32,656,1152]{2,1,0:T(8,128)(2,1)} pad(bf16[32,648,1152]{2,1,0:T(8,128)(2,1)} %bitcast.128, bf16[]{:T(256)} %constant.70.clone.1), padding=0_0x0_8x0_0 | pad | bytes 96141312 | tf_op jit(solution)/shard_map/jit(_pad)/pad | solution.py:549
  656.1 185.0 %scatter_grads.1 = bf16[656,1152]{1,0:T(8,128)(2,1)} custom-call(bf16[4,4,2,656,1152]{4,3,2,1,0:T(8,128)(2,1)} %bitcast.127), custom_call_target="tpu_custom_call" | custom-call | tf_op jit(solution)/shard_map/scatter_grads/pallas_call | solution.py:507
  841.2 1.0 reshape.392
  842.2 1.3 convolution_bitcast_fusion
  844.0 1.8 reshape.394
  846.4 5.1 multiply_reduce_fusion.1
  851.6 38.5 %all-reduce.4 = (f32[3,1152]{1,0:T(4,128)S(1)}, f32[]{:T(128)}, f32[9216]{0:T(1024)S(1)}) all-reduce(f32[3,1152]{1,0:T(4,128)S(1)} %reduce_sum.242, f32[]{:T(128)} %get-tuple-element.68, f32[9216]{0:T(1024)S(1)} %constant_dynamic-update-slice_fusion.4), channel_id=1, replica_groups=mesh['outer'=4,'inner'=8] {'outer','inner'}, use_global_device_ids=true, to_apply=%region_21.22 | all-reduce | flops 12673 | bytes 101384 | tf_op jit(solution)/shard_map/psum | solution.py:798
  892.8 1.8 broadcast_multiply_fusion.1
  894.6 4.6 mul.451
  899.9 6.8 multiply_subtract_fusion
  (197 shorter events, 23.4 us)
Async XLA Ops:
  7.2 280.7 %all-reduce.8.cloned.1.call-start = ((), (), s32[]{:S(2)}) async-start(), calls=%async_computation | async-start | bytes 221184 | tf_op jit(solution)/shard_map/psum | solution.py:665
  11.7 10.2 %copy-start.1 = (bf16[648,1152]{1,0:T(8,128)(2,1)}, bf16[648,1152]{1,0:T(8,128)(2,1)S(1)}, u32[]{:S(2)}) copy-start(bf16[648,1152]{1,0:T(8,128)(2,1)S(1)} %convert_element_type.134) | copy-start | bytes 4478980
  11.7 5.6 copy-start.52
  11.7 5.6 copy-start.49
  11.7 6.2 copy-start
  13.5 5.1 copy-start.31
  16.1 7.0 copy-start.34
  17.3 823.9 %all-reduce.10.cloned.1.call-start = ((), (), s32[]{:S(2)}) async-start(), calls=%async_computation.1 | async-start | bytes 221184 | tf_op jit(solution)/shard_map/psum | solution.py:785
  20.5 365.4 %copy-start.47 = (pred[24]{0:T(512)(128)(4,1)}, pred[24]{0:T(512)(128)(4,1)S(1)}, u32[]{:S(2)}) copy-start(pred[24]{0:T(512)(128)(4,1)S(1)} %get-tuple-element.54) | copy-start | bytes 76
  270.0 17.9 %slice-start.2 = ((f32[16128]{0:T(1024)}), f32[6912]{0:T(1024)S(1)}, s32[]{:S(2)}) async-start(f32[16128]{0:T(1024)} %param.19), calls=%async_computation.4 | async-start | bytes 57344 | tf_op jit(solution)/shard_map/slice | solution.py:570
  290.4 0.6 copy-start.22
  291.5 7.6 copy-start.25
  304.6 12.0 %copy-start.3 = (bf16[24,16,16,72]{3,2,1,0:T(8,128)(2,1)}, bf16[24,16,16,72]{3,2,1,0:T(8,128)(2,1)S(1)}, u32[]{:S(2)}) copy-start(bf16[24,16,16,72]{3,2,1,0:T(8,128)(2,1)S(1)} %reshape.381) | copy-start | bytes 2654212
  316.6 12.3 %copy-start.20 = (bf16[24,16,16,72]{3,2,1,0:T(8,128)(2,1)S(1)}, bf16[24,16,16,72]{3,2,1,0:T(8,128)(2,1)}, u32[]{:S(2)}) copy-start(bf16[24,16,16,72]{3,2,1,0:T(8,128)(2,1)} %reshape.380) | copy-start | bytes 2654212
  328.9 1.7 copy-start.6
  338.4 7.9 copy-start.27
  338.4 7.9 copy-start.17
  346.3 14.4 %copy-start.9 = (f32[384,4608]{1,0:T(8,128)}, f32[384,4608]{1,0:T(8,128)S(1)}, u32[]{:S(2)}) copy-start(f32[384,4608]{1,0:T(8,128)S(1)} %convolution_add_fusion) | copy-start | bytes 21233668
  360.7 12.5 %copy-start.29 = (bf16[384,1152]{1,0:T(8,128)(2,1)}, bf16[384,1152]{1,0:T(8,128)(2,1)S(1)}, u32[]{:S(2)}) copy-start(bf16[384,1152]{1,0:T(8,128)(2,1)S(1)} %get-tuple-element.26) | copy-start | bytes 2654212
  390.5 4.2 copy-start.13
  402.3 3.8 copy-start.7
  402.3 3.8 copy-start.21
  407.4 1.4 copy-start.4
  408.8 1.4 copy-start.5
  431.2 11.7 %copy-start.15 = (bf16[384,1152]{1,0:T(8,128)(2,1)S(1)}, bf16[384,1152]{1,0:T(8,128)(2,1)}, u32[]{:S(2)}) copy-start(bf16[384,1152]{1,0:T(8,128)(2,1)} %reshape.395) | copy-start | bytes 2654212
  431.2 11.8 %copy-start.14 = (bf16[384,1152]{1,0:T(8,128)(2,1)S(1)}, bf16[384,1152]{1,0:T(8,128)(2,1)}, u32[]{:S(2)}) copy-start(bf16[384,1152]{1,0:T(8,128)(2,1)} %reshape.396) | copy-start | bytes 2654212
  442.9 1.2 copy-start.16
  443.0 1.7 copy-start.26
  444.7 6.7 copy-start.28
  444.7 6.7 copy-start.53
  444.7 16.8 %slice-start = ((s8[7962624]{0:T(1024)(128)(4,1)}), s8[4194304]{0:T(1024)(128)(4,1)S(1)}, s32[]{:S(2)}) async-start(s8[7962624]{0:T(1024)(128)(4,1)} %bitcast.139), calls=%async_computation.2 | async-start | bytes 8388608
  451.4 8.6 copy-start.37
  451.4 9.4 %copy-start.36 = (f32[24,1152]{1,0:T(8,128)S(1)}, f32[24,1152]{1,0:T(8,128)}, u32[]{:S(2)}) copy-start(f32[24,1152]{1,0:T(8,128)} %get-tuple-element.16) | copy-start | bytes 331780
  451.4 10.1 %slice-start.1 = ((s8[7962624]{0:T(1024)(128)(4,1)}), s8[3768320]{0:T(1024)(128)(4,1)S(1)}, s32[]{:S(2)}) async-start(s8[7962624]{0:T(1024)(128)(4,1)} %bitcast.139), calls=%async_computation.3 | async-start | bytes 7536640
  451.4 10.1 %copy-start.19 = (f32[24,16,1152]{2,1,0:T(8,128)S(1)}, f32[24,16,1152]{2,1,0:T(8,128)}, u32[]{:S(2)}) copy-start(f32[24,16,1152]{2,1,0:T(8,128)} %get-tuple-element.32) | copy-start | bytes 5308420
  451.4 10.1 %copy-start.23 = (f32[24,1152]{1,0:T(8,128)S(1)}, f32[24,1152]{1,0:T(8,128)}, u32[]{:S(2)}) copy-start(f32[24,1152]{1,0:T(8,128)} %copy-done.22) | copy-start | bytes 331780
  451.4 10.1 %copy-start.24 = (bf16[24,16,1152]{2,1,0:T(8,128)(2,1)S(1)}, bf16[24,16,1152]{2,1,0:T(8,128)(2,1)}, u32[]{:S(2)}) copy-start(bf16[24,16,1152]{2,1,0:T(8,128)(2,1)} %concatenate.28) | copy-start | bytes 2654212
  451.4 10.1 %copy-start.42 = (f32[24,16]{1,0:T(8,128)S(1)}, f32[24,16]{1,0:T(8,128)}, u32[]{:S(2)}) copy-start(f32[24,16]{1,0:T(8,128)} %div.86) | copy-start | bytes 4612
  461.5 10.6 %copy-start.10 = (f32[384,1152]{1,0:T(8,128)S(1)}, f32[384,1152]{1,0:T(8,128)}, u32[]{:S(2)}) copy-start(f32[384,1152]{1,0:T(8,128)} %get-tuple-element.63) | copy-start | bytes 5308420
  461.5 10.6 %copy-start.11 = (f32[24,16,1152]{2,1,0:T(8,128)S(1)}, f32[24,16,1152]{2,1,0:T(8,128)}, u32[]{:S(2)}) copy-start(f32[24,16,1152]{2,1,0:T(8,128)} %get-tuple-element.29) | copy-start | bytes 5308420
  461.5 10.6 %copy-start.12 = (f32[24,16,1152]{2,1,0:T(8,128)S(1)}, f32[24,16,1152]{2,1,0:T(8,128)}, u32[]{:S(2)}) copy-start(f32[24,16,1152]{2,1,0:T(8,128)} %get-tuple-element.30) | copy-start | bytes 5308420
  461.6 10.6 %copy-start.48 = (pred[24]{0:T(512)(128)(4,1)S(1)}, pred[24]{0:T(512)(128)(4,1)}, u32[]{:S(2)}) copy-start(pred[24]{0:T(512)(128)(4,1)} %copy-done.47) | copy-start | bytes 76
  472.1 4.1 copy-start.38
  476.0 2.7 copy-start.50
  476.0 3.8 copy-start.43
  492.8 16.5 %copy-start.45 = (f32[1152]{0:T(1024)S(1)}, f32[1152]{0:T(1024)}, u32[]{:S(2)}) copy-start(f32[1152]{0:T(1024)} %get-tuple-element.27) | copy-start | bytes 13828
  492.8 16.5 %copy-start.46 = (f32[4608]{0:T(1024)S(1)}, f32[4608]{0:T(1024)}, u32[]{:S(2)}) copy-start(f32[4608]{0:T(1024)} %get-tuple-element.70) | copy-start | bytes 55300
  492.8 16.5 %copy-start.18 = (bf16[1152,1152]{1,0:T(8,128)(2,1)S(1)}, bf16[1152,1152]{1,0:T(8,128)(2,1)}, u32[]{:S(2)}) copy-start(bf16[1152,1152]{1,0:T(8,128)(2,1)} %convolution_convert_fusion.3) | copy-start | bytes 7962628
  509.3 114.4 %copy-start.44 = (f32[1152]{0:T(1024)S(1)}, f32[1152]{0:T(1024)}, u32[]{:S(2)}) copy-start(f32[1152]{0:T(1024)} %get-tuple-element.25) | copy-start | bytes 13828
  656.1 186.0 %copy-start.2 = (bf16[648,1152]{1,0:T(8,128)(2,1)S(1)}, bf16[648,1152]{1,0:T(8,128)(2,1)}, u32[]{:S(2)}) copy-start(bf16[648,1152]{1,0:T(8,128)(2,1)} %copy-done.1) | copy-start | bytes 4478980
  656.1 187.4 %copy-start.35 = (f32[648,6]{0,1:T(8,128)S(1)}, f32[648,6]{0,1:T(8,128)}, u32[]{:S(2)}) copy-start(f32[648,6]{0,1:T(8,128)} %copy-done.34) | copy-start | bytes 46660
  842.1 4.3 copy-start.33
  842.2 4.3 copy-start.51
  845.8 44.2 %copy-start.30 = (f32[3,6912]{1,0:T(4,128)S(1)}, f32[3,6912]{1,0:T(4,128)}, u32[]{:S(2)}) copy-start(f32[3,6912]{1,0:T(4,128)} %all-reduce.10.cloned.1.call-done) | copy-start | bytes 248836
  845.8 46.3 %copy-start.39 = (f32[3,1152]{1,0:T(4,128)S(1)}, f32[3,1152]{1,0:T(4,128)}, u32[]{:S(2)}) copy-start(f32[3,1152]{1,0:T(4,128)} %param.12) | copy-start | bytes 41476
  894.6 4.6 copy-start.32
  894.6 4.6 copy-start.40
  894.6 4.6 copy-start.41
  894.6 5.3 copy-start.8
Sparse Core Ops, SparseCore 0:
  17.4 152.7 all-reduce.7
  480.0 129.7 all-reduce.9

commit v2 on v1

--- a/solution.py
+++ b/solution.py
@@ -25,13 +25,14 @@
 CLIP_NORM = 1.0
 BLOCK_UNITS = 4 * D + 2 * FF
 
+
 MESH = pl.DeviceIdType.MESH
 UNITS = 648
-ROWS = 656
-QUART = 160
-HALFQ = 80
-MAIN = 640
-TAIL = 16
+GROUPS8 = 81
+QUART = 20
+HALFQ = 10
+MAIN = 80
+TAIL = 1
 DEPTH = (4, 4, 3)
 BASE = (0, 4, 8)
 
@@ -115,10 +116,6 @@
         self.sent = []
 
 
-def rows16(start):
-    return pl.multiple_of(start, 16)
-
-
 def ok(zb, p):
     return None if DEPTH[p] == 4 else zb < DEPTH[p]
 
@@ -140,12 +137,12 @@
     me.greet()
 
     def part(p, zb, yb, x, c, first=0, n=QUART):
-        return full.at[p, zb, yb, pl.ds(rows16(320 * x + QUART * c + first), n)]
+        return full.at[p, zb, yb, pl.ds((2 * QUART * x + QUART * c + first), n)]
 
     def own_of(p):
         return both(me.o == p, ok(me.z, p))
 
-    quarter = rows16(320 * me.x + QUART * me.c)
+    quarter = (2 * QUART * me.x + QUART * me.c)
     own_tail = pltpu.make_async_copy(
         shard.at[pl.ds(MAIN, TAIL)], full.at[me.o, me.z, me.y, pl.ds(MAIN, TAIL)], local_sems.at[0]
     )
@@ -167,7 +164,7 @@
             x = me.xo if dx else me.x
             c = me.co if dc else me.c
             cp.send(
-                s, shard.at[pl.ds(rows16(320 * x + QUART * c), QUART)],
+                s, shard.at[pl.ds((2 * QUART * x + QUART * c), QUART)],
                 part(p, me.z, me.y, x, c), me.dev(dx=dx, dc=dc), own_of(p),
             )
 
@@ -225,7 +222,7 @@
             cp.send(s, out, out, me.dev(dy=1), ok(zb, p))
 
     def lane(p, zb, x, c):
-        return full.at[p, zb, :, pl.ds(rows16(320 * x + QUART * c), QUART)]
+        return full.at[p, zb, :, pl.ds((2 * QUART * x + QUART * c), QUART)]
 
     def s4(p):
         for d in (0, 1, 2, 3):
@@ -292,7 +289,7 @@
 def gather_weights(shard):
     return pl.pallas_call(
         gather_kernel,
-        out_shape=jax.ShapeDtypeStruct((4, 4, 2, ROWS, D), jnp.bfloat16),
+        out_shape=jax.ShapeDtypeStruct((4, 4, 2, GROUPS8, 8, D), jnp.bfloat16),
         in_specs=[pl.BlockSpec(memory_space=pl.ANY)],
         out_specs=pl.BlockSpec(memory_space=pl.ANY),
         scratch_shapes=[
@@ -309,9 +306,11 @@
 f32 = jnp.float32
 
 
-def add_rows(dst, srcs, n, step=16):
+def add_rows(dst, srcs, n):
+    step = 2 if n % 2 == 0 else 1
+
     def body(j, carry):
-        at = pl.ds(pl.multiple_of(j * step, step), step)
+        at = pl.ds(j * step, step)
         total = srcs[0][at].astype(f32)
         for src in srcs[1:]:
             total = total + src[at].astype(f32)
@@ -340,7 +339,7 @@
     def load(p, d, h):
         zb = flip(me.z, d)
         return pltpu.make_async_copy(
-            partial.at[p, zb, :, pl.ds(rows16(320 * h + QUART * me.c), QUART)],
+            partial.at[p, zb, :, pl.ds((2 * QUART * h + QUART * me.c), QUART)],
             own.at[BASE[p] + zb, :, h], local_sems.at[(p * 4 + d) * 2 + h],
         )
 
@@ -351,7 +350,7 @@
                 guarded(ok(zb, p), lambda d=d, h=h: load(p, d, h).start())
                 s = slots["c", p, d, h] = cp.slot()
                 cp.send(
-                    s, partial.at[p, zb, :, pl.ds(rows16(320 * h + QUART * me.co), QUART)],
+                    s, partial.at[p, zb, :, pl.ds((2 * QUART * h + QUART * me.co), QUART)],
                     other.at[BASE[p] + zb, :, h], me.dev(dc=1), ok(zb, p),
                 )
 
@@ -414,7 +413,7 @@
             lambda: add_rows(final.at[p], [view, rz.at[p, 0], rz.at[p, 1], rz.at[p, 2]], QUART),
         )
         ox, oc = p // 2, p % 2
-        quarter = out.at[pl.ds(rows16(320 * me.x + QUART * me.c), QUART)]
+        quarter = out.at[pl.ds((2 * QUART * me.x + QUART * me.c), QUART)]
         for dx, dc in ((1, 0), (0, 1), (1, 1)):
             x = me.xo if dx else me.x
             c = me.co if dc else me.c
@@ -432,13 +431,13 @@
             x = me.xo if dx else me.x
             c = me.co if dc else me.c
             cp.wait_recv(
-                slots["f", p, dx, dc], out.at[pl.ds(rows16(320 * x + QUART * c), QUART)],
+                slots["f", p, dx, dc], out.at[pl.ds((2 * QUART * x + QUART * c), QUART)],
                 me.dev(dx=dx, dc=dc), mine,
             )
 
         @pl.when(mine)
         def _():
-            quarter = out.at[pl.ds(rows16(320 * me.x + QUART * me.c), QUART)]
+            quarter = out.at[pl.ds((2 * QUART * me.x + QUART * me.c), QUART)]
             pltpu.make_async_copy(final.at[p], quarter, local_sems.at[24]).wait()
 
     tail_load = pltpu.make_async_copy(
@@ -506,21 +505,21 @@
     bf = jnp.bfloat16
     return pl.pallas_call(
         scatter_kernel,
-        out_shape=jax.ShapeDtypeStruct((ROWS, D), bf),
+        out_shape=jax.ShapeDtypeStruct((GROUPS8, 8, D), bf),
         in_specs=[pl.BlockSpec(memory_space=pl.ANY)],
         out_specs=pl.BlockSpec(memory_space=pl.ANY),
         scratch_shapes=[
-            pltpu.VMEM((11, 2, 2, QUART, D), bf),
-            pltpu.VMEM((11, 2, 2, QUART, D), bf),
-            pltpu.VMEM((11, HALFQ, D), bf),
-            pltpu.VMEM((11, HALFQ, D), bf),
-            pltpu.VMEM((11, QUART, D), bf),
-            pltpu.VMEM((11, QUART, D), bf),
-            pltpu.VMEM((3, 3, QUART, D), bf),
-            pltpu.VMEM((3, QUART, D), bf),
-            pltpu.VMEM((4, 4, 2, TAIL, D), bf),
-            pltpu.VMEM((4, 4, 2, TAIL, D), bf),
-            pltpu.VMEM((3, TAIL, D), bf),
+            pltpu.VMEM((11, 2, 2, QUART, 8, D), bf),
+            pltpu.VMEM((11, 2, 2, QUART, 8, D), bf),
+            pltpu.VMEM((11, HALFQ, 8, D), bf),
+            pltpu.VMEM((11, HALFQ, 8, D), bf),
+            pltpu.VMEM((11, QUART, 8, D), bf),
+            pltpu.VMEM((11, QUART, 8, D), bf),
+            pltpu.VMEM((3, 3, QUART, 8, D), bf),
+            pltpu.VMEM((3, QUART, 8, D), bf),
+            pltpu.VMEM((4, 4, 2, TAIL, 8, D), bf),
+            pltpu.VMEM((4, 4, 2, TAIL, 8, D), bf),
+            pltpu.VMEM((3, TAIL, 8, D), bf),
             pltpu.SemaphoreType.DMA((SCATTER_COPIES,)),
             pltpu.SemaphoreType.DMA((SCATTER_COPIES,)),
             pltpu.SemaphoreType.DMA((26,)),
@@ -531,35 +530,494 @@
         name="scatter_grads",
     )(partial)
 
+
+bf16 = jnp.bfloat16
+MATS = D // 8
+AT_PROJ = 3 * MATS
+AT_UP = 4 * MATS
+AT_DOWN = 8 * MATS
+ROOT = math.sqrt(2.0 / math.pi)
+CUBIC = 0.044715
+
+
+def nn_dot(left, right):
+    return lax.dot_general(left, right, (((1,), (0,)), ((), ())), preferred_element_type=f32)
+
+
+def nt_dot(left, right):
+    return lax.dot_general(left, right, (((1,), (1,)), ((), ())), preferred_element_type=f32)
+
+
+def tn_dot(left, right):
+    return lax.dot_general(left, right, (((0,), (0,)), ((), ())), preferred_element_type=f32)
+
+
+def square(ref):
+    return ref[...].reshape(D, D)
+
+
+def norm_rows(values):
+    centered = values - jnp.mean(values, axis=-1, keepdims=True)
+    inverse = lax.rsqrt(jnp.mean(centered * centered, axis=-1, keepdims=True) + NORM_EPS)
+    return centered * inverse, inverse
+
+
+def norm_rows_back(grad, normed, inverse):
+    return inverse * (
+        grad
+        - jnp.mean(grad, axis=-1, keepdims=True)
+        - normed * jnp.mean(grad * normed, axis=-1, keepdims=True)
+    )
+
+
+def frames_of(c):
+    return pl.ds(pl.multiple_of(c * FRAMES, FRAMES), FRAMES)
+
+
+def over_columns(count, body):
+    def step(c, carry):
+        body(c, frames_of(c), pl.ds(c, 1))
+        return carry
+
+    lax.fori_loop(0, count, step, 0)
+
+
+def split_rows(src, spread, put, ways, step):
+    units = src.shape[0] * 8
+    rows = units // ways
+    for q in range(9):
+        lanes = slice(128 * q, 128 * q + 128)
+        spread[q, pl.ds(0, units)] = src[:, :, lanes].astype(f32).reshape(units, 128)
+        for w in range(ways):
+            part = spread[q, pl.ds(w, rows, stride=ways), :]
+            put(w, lanes, part.reshape(rows // 8, 8, 128).astype(bf16))
+
+
+def head_window(h):
+    first = min(HD * h // 128, 7) * 128
+    lane = lax.broadcasted_iota(jnp.int32, (1, 256), 1) + first
+    mask = jnp.logical_and(lane >= HD * h, lane < HD * h + HD)
+    return slice(first, first + 256), jnp.where(mask, 1.0, 0.0).astype(bf16)
+
+
+def same_column():
+    row = lax.broadcasted_iota(jnp.int32, (128, 128), 0)
+    col = lax.broadcasted_iota(jnp.int32, (128, 128), 1)
+    return lax.shift_right_logical(row, 4) == lax.shift_right_logical(col, 4)
+
+
+SCORE_SCALE = 1.0 / math.sqrt(HD)
+
+
+def head_probabilities(masked_queries, keys, inside):
+    scores = jnp.where(inside, nt_dot(masked_queries, keys) * SCORE_SCALE, -1e30)
+    grown = jnp.exp(scores - jnp.max(scores, axis=-1, keepdims=True))
+    return grown / jnp.sum(grown, axis=-1, keepdims=True)
+
+
+def forward_kernel(
+    weights, tokens, upstream, mods, b_qkv, b_proj, b_up, b_down,
+    block_out, natural, input_att, proj, attended, branch, input_mlp, active, slope, grad_out,
+    grad_gate, held, stage, spread, acc, hid, copy_sems,
+):
+    columns = mods.shape[1]
+
+    def fetch(first, groups, slot):
+        return pltpu.make_async_copy(
+            weights.at[pl.ds(first, groups)], stage.at[slot, pl.ds(0, groups)], copy_sems.at[slot]
+        )
+
+    def whole(mat, slot):
+        return pltpu.make_async_copy(
+            weights.at[pl.ds(mat * MATS, MATS)], held.at[slot], copy_sems.at[2 + slot]
+        )
+
+    def save(mat, slot):
+        return pltpu.make_async_copy(held.at[slot], natural.at[mat], copy_sems.at[10 + mat])
+
+    def unweave(first, ways, slot0, blocks=9):
+        groups = 16 * ways
+        fetch(first, groups, 0).start()
+
+        def step(j, carry):
+            slot = lax.rem(j, 2)
+            fetch(first + j * groups, groups, slot).wait()
+
+            @pl.when(j + 1 < blocks)
+            def _():
+                fetch(first + (j + 1) * groups, groups, 1 - slot).start()
+
+            def put(w, lanes, block):
+                held[slot0 + w, pl.ds(j * 16, 16), :, lanes] = block
+
+            split_rows(stage.at[slot, pl.ds(0, groups)], spread, put, ways, None)
+            return carry
+
+        lax.fori_loop(0, blocks, step, 0)
+
+    whole(3, 3).start()
+
+    def first_norm(c, rows, at):
+        normed, _ = norm_rows(tokens[rows].astype(f32))
+        input_att[rows] = (normed * (1.0 + mods[1, at]) + mods[0, at]).astype(bf16)
+
+    over_columns(columns, first_norm)
+    unweave(0, 3, 0)
+    for p in range(3):
+        save(p, p).start()
+
+    def project(p, carry):
+        proj[p] = (nn_dot(input_att[...], square(held.at[p])) + b_qkv[pl.ds(p, 1)]).astype(bf16)
+        return carry
+
+    lax.fori_loop(0, 3, project, 0)
+
+    inside = same_column()
+
+    def attend(g, carry):
+        rows = pl.ds(pl.multiple_of(g * 128, 128), 128)
+        acc[pl.ds(0, 128)] = jnp.zeros((128, D), f32)
+        for h in range(H):
+            window, mask = head_window(h)
+            probs = head_probabilities(proj[0, rows, window] * mask, proj[1, rows, window], inside)
+            acc[pl.ds(0, 128), window] += nn_dot(probs.astype(bf16), proj[2, rows, window] * mask)
+        attended[rows] = acc[pl.ds(0, 128)].astype(bf16)
+        return carry
+
+    lax.fori_loop(0, columns * FRAMES // 128, attend, 0)
+    whole(3, 3).wait()
+    branch[...] = nn_dot(attended[...], square(held.at[3])) + b_proj[...]
+    for p in range(3):
+        save(p, p).wait()
+    for b in range(4):
+        whole(8 + b, b).start()
+
+    def second_norm(c, rows, at):
+        middle = tokens[rows].astype(f32) + mods[2, at] * branch[rows]
+        normed, _ = norm_rows(middle)
+        input_mlp[rows] = (normed * (1.0 + mods[4, at]) + mods[3, at]).astype(bf16)
+
+    over_columns(columns, second_norm)
+    unweave(AT_UP, 4, 4)
+    for b in range(4):
+        save(3 + b, 4 + b).start()
+
+    def raise_(b, carry):
+        hid[...] = nn_dot(input_mlp[...], square(held.at[4 + b])) + b_up[pl.ds(b, 1)]
+
+        def gelu(c, rows, at):
+            v = hid[rows]
+            sq = v * v
+            t = jnp.tanh(ROOT * (v + CUBIC * sq * v))
+            half = 0.5 * (1.0 + t)
+            active[b, rows] = (v * half).astype(bf16)
+            slope[b, rows] = half + (0.5 * ROOT) * v * (1.0 - t * t) * (1.0 + 3.0 * CUBIC * sq)
+
+        over_columns(columns, gelu)
+        return carry
+
+    lax.fori_loop(0, 4, raise_, 0)
+    acc[...] = jnp.broadcast_to(b_down[...], acc.shape)
+    for b in range(4):
+        whole(8 + b, b).wait()
+
+    def lower(b, carry):
+        acc[...] += nn_dot(active[b], square(held.at[b]))
+        return carry
+
+    lax.fori_loop(0, 4, lower, 0)
+
+    def last(c, rows, at):
+        x = tokens[rows].astype(f32)
+        middle = x + mods[2, at] * branch[rows]
+        video = mods[6, at] > 0.5
+        outcome = acc[rows]
+        block_out[rows] = jnp.where(video, middle + mods[5, at] * outcome, x)
+        grad_block = jnp.where(video, upstream[rows].astype(f32), 0.0)
+        grad_gate[at] = jnp.sum(grad_block * outcome, axis=0, keepdims=True)
+        grad_out[rows] = (grad_block * mods[5, at]).astype(bf16)
+
+    over_columns(columns, last)
+    for b in range(4):
+        save(3 + b, 4 + b).wait()
+
+
+def forward(weights, tokens, upstream, mods, b_qkv, b_proj, b_up, b_down):
+    rows = tokens.shape[0]
+    columns = mods.shape[1]
+    vmem = pl.BlockSpec(memory_space=pltpu.VMEM)
+    hbm = pl.BlockSpec(memory_space=pl.ANY)
+    shape = jax.ShapeDtypeStruct
+    return pl.pallas_call(
+        forward_kernel,
+        out_shape=[
+            shape((rows, D), f32),
+            shape((7, MATS, 8, D), bf16),
+            shape((rows, D), bf16),
+            shape((3, rows, D), bf16),
+            shape((rows, D), bf16),
+            shape((rows, D), f32),
+            shape((rows, D), bf16),
+            shape((4, rows, D), bf16),
+            shape((4, rows, D), f32),
+            shape((rows, D), bf16),
+            shape((columns, D), f32),
+        ],
+        in_specs=[hbm] + [vmem] * 7,
+        out_specs=[vmem, hbm] + [vmem] * 9,
+        scratch_shapes=[
+            pltpu.VMEM((8, MATS, 8, D), bf16),
+            pltpu.VMEM((2, 64, 8, D), bf16),
+            pltpu.VMEM((9, 512, 128), f32),
+            pltpu.VMEM((rows, D), f32),
+            pltpu.VMEM((rows, D), f32),
+            pltpu.SemaphoreType.DMA((17,)),
+        ],
+        compiler_params=pltpu.CompilerParams(vmem_limit_bytes=60 * 2**20),
+        name="block_forward",
+    )(weights, tokens, upstream, mods, b_qkv, b_proj, b_up, b_down)
+
+
+def backward_kernel(
+    weights, natural, tokens, upstream, mods, input_att, proj, attended, branch, input_mlp, active,
+    slope, grad_out,
+    grads, input_grad, grad_mods, bias_sums,
+    held, woven, spread, flat, grad_hidden, middle_grad, grad_branch, grad_att, grad_proj, acc,
+    copy_sems,
+):
+    columns = mods.shape[1]
+
+    def fetch(source, first, slot):
+        return pltpu.make_async_copy(source.at[first], held.at[slot], copy_sems.at[slot])
+
+    def flat_mat(first, slot):
+        return pltpu.make_async_copy(
+            weights.at[pl.ds(first, MATS)], held.at[slot], copy_sems.at[slot]
+        )
+
+    def store_flat(first, slot):
+        return pltpu.make_async_copy(
+            flat.at[slot], grads.at[pl.ds(first, MATS)], copy_sems.at[2 + slot]
+        )
+
+    bias_sums[...] = jnp.zeros_like(bias_sums)
+
+    def add_bias(row, values):
+        bias_sums[pl.ds(row, 1)] += jnp.sum(values.astype(f32), axis=0, keepdims=True)
+
+    flat_mat(AT_DOWN, 0).start()
+
+    def down(b, carry):
+        slot = lax.rem(b, 2)
+        flat_mat(AT_DOWN + b * MATS, slot).wait()
+
+        @pl.when(b < 3)
+        def _():
+            flat_mat(AT_DOWN + (b + 1) * MATS, 1 - slot).start()
+
+        acc[...] = nt_dot(grad_out[...], square(held.at[slot]))
+
+        def through(c, rows, at):
+            grad = (acc[rows] * slope[b, rows]).astype(bf16)
+            grad_hidden[b, rows] = grad
+            add_bias(5 + b, grad)
+
+        over_columns(columns, through)
+
+        @pl.when(b >= 2)
+        def _():
+            store_flat(AT_DOWN + (b - 2) * MATS, slot).wait()
+
+        flat[slot] = tn_dot(active[b], grad_out[...]).reshape(MATS, 8, D).astype(bf16)
+        store_flat(AT_DOWN + b * MATS, slot).start()
+        return carry
+
+    lax.fori_loop(0, 4, down, 0)
+    fetch(natural, 3, 0).start()
+
+    def down_bias(c, rows, at):
+        add_bias(4, grad_out[rows])
+
+    over_columns(columns, down_bias)
+
+    def weave(first, ways, left, right_of):
+        groups = 48 * ways
+
+        def store(k):
+            return pltpu.make_async_copy(
+                woven.at[pl.ds(0, groups)], grads.at[pl.ds(first + k * groups, groups)],
+                copy_sems.at[4],
+            )
+
+        for k in range(3):
+            for w in range(ways):
+                part = tn_dot(left[:, 384 * k : 384 * k + 384], right_of(w))
+                for q in range(9):
+                    spread[q, pl.ds(w, 384, stride=ways), :] = part[:, 128 * q : 128 * q + 128]
+            if k:
+                store(k - 1).wait()
+
+            def pack(j, carry):
+                for q in range(9):
+                    block = spread[q, pl.ds(pl.multiple_of(j * 128, 128), 128), :]
+                    woven[pl.ds(j * 16, 16), :, 128 * q : 128 * q + 128] = block.reshape(
+                        16, 8, 128
+                    ).astype(bf16)
+                return carry
+
+            lax.fori_loop(0, groups // 16, pack, 0)
+            store(k).start()
+        return lambda: store(2).wait()
+
+    up_done = weave(AT_UP, 4, input_mlp, lambda w: grad_hidden[w])
+    acc[...] = jnp.zeros_like(acc)
+
+    def up(b, carry):
+        slot = lax.rem(b, 2)
+        fetch(natural, 3 + b, slot).wait()
+
+        @pl.when(b < 3)
+        def _():
+            fetch(natural, 4 + b, 1 - slot).start()
+
+        acc[...] += nt_dot(grad_hidden[b], square(held.at[slot]))
+        return carry
+
+    lax.fori_loop(0, 4, up, 0)
+    flat_mat(AT_PROJ, 0).start()
+
+    def second_norm_back(c, rows, at):
+        br = branch[rows]
+        gate = mods[2, at]
+        normed, inverse = norm_rows(tokens[rows].astype(f32) + gate * br)
+        grad = acc[rows]
+        grad_mods[3, at] = jnp.sum(grad, axis=0, keepdims=True)
+        grad_mods[4, at] = jnp.sum(grad * normed, axis=0, keepdims=True)
+        grad_block = jnp.where(mods[6, at] > 0.5, upstream[rows].astype(f32), 0.0)
+        grad_middle = grad_block + norm_rows_back(grad * (1.0 + mods[4, at]), normed, inverse)
+        middle_grad[rows] = grad_middle
+        grad_mods[2, at] = jnp.sum(grad_middle * br, axis=0, keepdims=True)
+        grad = (grad_middle * gate).astype(bf16)
+        grad_branch[rows] = grad
+        add_bias(3, grad)
+
+    over_columns(columns, second_norm_back)
+    store_flat(AT_DOWN + 2 * MATS, 0).wait()
+    store_flat(AT_DOWN + 3 * MATS, 1).wait()
+    flat[0] = tn_dot(attended[...], grad_branch[...]).reshape(MATS, 8, D).astype(bf16)
+    store_flat(AT_PROJ, 0).start()
+    flat_mat(AT_PROJ, 0).wait()
+    grad_att[...] = nt_dot(grad_branch[...], square(held.at[0])).astype(bf16)
+    fetch(natural, 0, 0).start()
+    inside = same_column()
+    top = pl.ds(0, 128)
+
+    def attend_back(g, carry):
+        rows = pl.ds(pl.multiple_of(g * 128, 128), 128)
+        for p in range(3):
+            acc[pl.ds(p * 128, 128)] = jnp.zeros((128, D), f32)
+        for h in range(H):
+            window, mask = head_window(h)
+            queries = proj[0, rows, window] * mask
+            keys = proj[1, rows, window]
+            grad = grad_att[rows, window] * mask
+            probs = head_probabilities(queries, keys, inside)
+            grad_probs = nt_dot(grad, proj[2, rows, window])
+            mean = jnp.sum(grad_probs * probs, axis=-1, keepdims=True)
+            grad_scores = (probs * (grad_probs - mean)).astype(bf16)
+            acc[pl.ds(0, 128), window] += nn_dot(grad_scores, keys * mask)
+            acc[pl.ds(128, 128), window] += tn_dot(grad_scores, queries)
+            acc[pl.ds(256, 128), window] += tn_dot(probs.astype(bf16), grad)
+        for p in range(3):
+            scale = SCORE_SCALE if p < 2 else 1.0
+            grad = (acc[pl.ds(p * 128, 128)] * scale).astype(bf16)
+            grad_proj[p, rows] = grad
+            add_bias(p, grad)
+        return carry
+
+    lax.fori_loop(0, columns * FRAMES // 128, attend_back, 0)
+    up_done()
+    qkv_done = weave(0, 3, input_att, lambda w: grad_proj[w])
+    acc[...] = jnp.zeros_like(acc)
+
+    def qkv(p, carry):
+        slot = lax.rem(p, 2)
+        fetch(natural, p, slot).wait()
+
+        @pl.when(p < 2)
+        def _():
+            fetch(natural, p + 1, 1 - slot).start()
+
+        acc[...] += nt_dot(grad_proj[p], square(held.at[slot]))
+        return carry
+
+    lax.fori_loop(0, 3, qkv, 0)
+
+    def first_norm_back(c, rows, at):
+        normed, inverse = norm_rows(tokens[rows].astype(f32))
+        grad = acc[rows]
+        grad_mods[0, at] = jnp.sum(grad, axis=0, keepdims=True)
+        grad_mods[1, at] = jnp.sum(grad * normed, axis=0, keepdims=True)
+        grad_states = middle_grad[rows] + norm_rows_back(
+            grad * (1.0 + mods[1, at]), normed, inverse
+        )
+        up_rows = upstream[rows].astype(f32)
+        input_grad[rows] = jnp.where(mods[6, at] > 0.5, grad_states, up_rows)
+
+    over_columns(columns, first_norm_back)
+    store_flat(AT_PROJ, 0).wait()
+    qkv_done()
+
+
+def backward(weights, natural, *operands):
+    tokens, mods = operands[0], operands[2]
+    rows = tokens.shape[0]
+    columns = mods.shape[1]
+    vmem = pl.BlockSpec(memory_space=pltpu.VMEM)
+    hbm = pl.BlockSpec(memory_space=pl.ANY)
+    shape = jax.ShapeDtypeStruct
+    return pl.pallas_call(
+        backward_kernel,
+        out_shape=[
+            shape((32 * UNITS // 8, 8, D), bf16),
+            shape((rows, D), f32),
+            shape((5, columns, D), f32),
+            shape((16, D), f32),
+        ],
+        in_specs=[hbm, hbm] + [vmem] * len(operands),
+        out_specs=[hbm] + [vmem] * 3,
+        scratch_shapes=[
+            pltpu.VMEM((2, MATS, 8, D), bf16),
+            pltpu.VMEM((192, 8, D), bf16),
+            pltpu.VMEM((9, 1536, 128), f32),
+            pltpu.VMEM((2, MATS, 8, D), bf16),
+            pltpu.VMEM((4, rows, D), bf16),
+            pltpu.VMEM((rows, D), f32),
+            pltpu.VMEM((rows, D), bf16),
+            pltpu.VMEM((rows, D), bf16),
+            pltpu.VMEM((3, rows, D), bf16),
+            pltpu.VMEM((rows, D), f32),
+            pltpu.SemaphoreType.DMA((5,)),
+        ],
+        compiler_params=pltpu.CompilerParams(vmem_limit_bytes=62 * 2**20),
+        name="block_backward",
+    )(weights, natural, *operands)
+
+
 def gather_blocks(shard_low, kernels):
     if not kernels:
         whole = lax.all_gather(shard_low, ("outer", "inner"), axis=0, tiled=True)
-        return whole[:BLOCK_UNITS]
-    padded = jnp.pad(shard_low, ((0, ROWS - UNITS), (0, 0)))
-    return gather_weights(padded).reshape(32, ROWS, D)[:22, :UNITS].reshape(-1, D)[:BLOCK_UNITS]
+        return whole.reshape(-1, 8, D)
+    return gather_weights(shard_low.reshape(GROUPS8, 8, D)).reshape(-1, 8, D)
 
 
 def scatter_blocks(grads, units, kernels):
     axes = ("outer", "inner")
     if not kernels:
-        count = lax.axis_size(axes) * units
-        padded = jnp.pad(grads, ((0, count - BLOCK_UNITS), (0, 0)))
-        return lax.psum_scatter(padded, axes, scatter_dimension=0, tiled=True)
-    padded = jnp.pad(grads, ((0, 32 * UNITS - BLOCK_UNITS), (0, 0))).reshape(32, UNITS, D)
-    padded = jnp.pad(padded, ((0, 0), (0, ROWS - UNITS), (0, 0))).reshape(4, 4, 2, ROWS, D)
-    return scatter_grads_kernel(padded)[:UNITS].astype(jnp.float32)
-
-
-def unpack_mats(flat):
-    shapes = [(D, 3 * D), (D, D), (D, FF), (FF, D)]
-    pieces = []
-    offset = 0
-    for height, breadth in shapes:
-        pieces.append(
-            lax.slice_in_dim(flat, offset, offset + height * breadth).reshape(height, breadth)
-        )
-        offset = offset + height * breadth
-    return pieces
+        whole = grads.reshape(-1, D)[: lax.axis_size(axes) * units].astype(f32)
+        return lax.psum_scatter(whole, axes, scatter_dimension=0, tiled=True)
+    summed = scatter_grads_kernel(grads.reshape(4, 4, 2, GROUPS8, 8, D))
+    return summed.reshape(UNITS, D).astype(f32)
 
 
 def split_bias(vector):
@@ -570,36 +1028,6 @@
         pieces.append(lax.slice_in_dim(vector, offset, offset + span_width))
         offset = offset + span_width
     return pieces
-
-
-def layer_stats(values):
-    centered = values - jnp.mean(values, axis=-1, keepdims=True)
-    inverse = lax.rsqrt(jnp.mean(centered * centered, axis=-1, keepdims=True) + NORM_EPS)
-    return (centered * inverse, inverse)
-
-
-def norm_back(grad_normed, normed, inverse):
-    return inverse * (
-        grad_normed
-        - jnp.mean(grad_normed, axis=-1, keepdims=True)
-        - normed * jnp.mean(grad_normed * normed, axis=-1, keepdims=True)
-    )
-
-
-def plain_dot(left_side, right_side):
-    return jnp.dot(left_side, right_side, preferred_element_type=jnp.float32)
-
-
-def left_dot(left_side, right_side):
-    return lax.dot_general(
-        left_side, right_side, (((0,), (0,)), ((), ())), preferred_element_type=jnp.float32
-    )
-
-
-def right_dot(left_side, right_side):
-    return lax.dot_general(
-        left_side, right_side, (((1,), (1,)), ((), ())), preferred_element_type=jnp.float32
-    )
 
 
 def exact(left, right, dims):
@@ -646,145 +1074,42 @@
     bias_second,
     kernels,
 ):
-    bf16 = jnp.bfloat16
-    highest = lax.Precision.HIGHEST
     columns = column_sample.shape[0]
     groups = conditioning.shape[0]
-    row_count = columns * FRAMES
-    score_scale = 1.0 / math.sqrt(HD)
     units = weights.shape[0] // D
     axes = ("outer", "inner")
     first_unit = lax.axis_index(axes).astype(jnp.int32) * units
     shard = weights.reshape(units, D)
     shard_low = shard.astype(bf16)
-    w_qkv, w_proj, w_up, w_down = unpack_mats(gather_blocks(shard_low, kernels).reshape(-1))
+    flat = gather_blocks(shard_low, kernels)
     b_query, b_value, b_proj, b_up, b_down, b_ada = split_bias(biases)
     soft_cond = jax.nn.silu(conditioning).astype(bf16)
     selector, ada_part = ada_selector(soft_cond, first_unit, units)
-    mods_all = left_dot(selector.astype(bf16), shard_low)
+    mods_all = tn_dot(selector.astype(bf16), shard_low)
     mods_all = lax.psum(mods_all, axes).reshape(groups, 6 * D) + b_ada
-    mods = jnp.take(mods_all, column_sample, axis=0)
-    video_cols = jnp.take(1.0 - is_image.astype(jnp.float32), column_sample)
-    mod_parts = mods.reshape(columns, 1, 6, D)
-    shift_att, scale_att, gate_att = (mod_parts[:, :, 0], mod_parts[:, :, 1], mod_parts[:, :, 2])
-    shift_mlp, scale_mlp, gate_mlp = (mod_parts[:, :, 3], mod_parts[:, :, 4], mod_parts[:, :, 5])
-    states = tokens.astype(jnp.float32).reshape(columns, FRAMES, D)
-    normed_att, inverse_att = layer_stats(states)
-    input_att = (normed_att * (1.0 + scale_att) + shift_att).astype(bf16).reshape(row_count, D)
-    qkv_bias = jnp.concatenate([b_query, jnp.zeros((D,), jnp.float32), b_value])
-    projected = (plain_dot(input_att, w_qkv) + qkv_bias).astype(bf16)
-    queries = projected[:, :D].reshape(columns, FRAMES, H, HD)
-    key_part = projected[:, D : 2 * D].reshape(columns, FRAMES, H, HD)
-    value_part = projected[:, 2 * D :].reshape(columns, FRAMES, H, HD)
-    scores = (
-        jnp.einsum("cqhd,ckhd->chqk", queries, key_part, preferred_element_type=jnp.float32)
-        * score_scale
-    )
-    probabilities = jax.nn.softmax(scores, axis=-1)
-    prob_low = probabilities.astype(bf16)
-    attended = jnp.einsum(
-        "chqk,ckhd->cqhd", prob_low, value_part, preferred_element_type=jnp.float32
-    )
-    attended = attended.reshape(row_count, D).astype(bf16)
-    branch = (plain_dot(attended, w_proj) + b_proj).reshape(columns, FRAMES, D)
-    middle = states + gate_att * branch
-    normed_mlp, inverse_mlp = layer_stats(middle)
-    input_mlp = (normed_mlp * (1.0 + scale_mlp) + shift_mlp).astype(bf16).reshape(row_count, D)
-    hidden = plain_dot(input_mlp, w_up) + b_up
-    gelu_out, gelu_back = jax.vjp(lambda pre_act: jax.nn.gelu(pre_act, approximate=True), hidden)
-    active = gelu_out.astype(bf16)
-    outcome = (plain_dot(active, w_down) + b_down).reshape(columns, FRAMES, D)
-    result = middle + gate_mlp * outcome
-    is_video = video_cols[:, None, None] > 0.5
-    block_out = jnp.where(is_video, result, states).reshape(row_count, D)
-    upstream = output_grad.astype(jnp.float32).reshape(columns, FRAMES, D)
-    grad_block = jnp.where(is_video, upstream, 0.0)
-    grad_gate_mlp = jnp.sum(grad_block * outcome, axis=1)
-    grad_outcome = (grad_block * gate_mlp).astype(bf16).reshape(row_count, D)
-    grad_w_down = left_dot(active, grad_outcome)
-    grad_b_down = jnp.sum(grad_outcome.astype(jnp.float32), axis=0)
-    grad_active = right_dot(grad_outcome, w_down)
-    grad_hidden = gelu_back(grad_active)[0].astype(bf16)
-    grad_w_up = left_dot(input_mlp, grad_hidden)
-    grad_b_up = jnp.sum(grad_hidden.astype(jnp.float32), axis=0)
-    grad_input_mlp = right_dot(grad_hidden, w_up).reshape(columns, FRAMES, D)
-    grad_shift_mlp = jnp.sum(grad_input_mlp, axis=1)
-    grad_scale_mlp = jnp.sum(grad_input_mlp * normed_mlp, axis=1)
-    grad_middle = grad_block + norm_back(
-        grad_input_mlp * (1.0 + scale_mlp), normed_mlp, inverse_mlp
-    )
-    grad_gate_att = jnp.sum(grad_middle * branch, axis=1)
-    grad_branch = (grad_middle * gate_att).astype(bf16).reshape(row_count, D)
-    grad_w_proj = left_dot(attended, grad_branch)
-    grad_b_proj = jnp.sum(grad_branch.astype(jnp.float32), axis=0)
-    grad_attended = right_dot(grad_branch, w_proj).astype(bf16).reshape(columns, FRAMES, H, HD)
-    grad_probs = jnp.einsum(
-        "cqhd,ckhd->chqk", grad_attended, value_part, preferred_element_type=jnp.float32
-    )
-    grad_values = jnp.einsum(
-        "chqk,cqhd->ckhd", prob_low, grad_attended, preferred_element_type=jnp.float32
-    )
-    grad_scores = probabilities * (
-        grad_probs - jnp.sum(grad_probs * probabilities, axis=-1, keepdims=True)
-    )
-    grad_scores = grad_scores.astype(bf16)
-    grad_queries = (
-        jnp.einsum("chqk,ckhd->cqhd", grad_scores, key_part, preferred_element_type=jnp.float32)
-        * score_scale
-    )
-    grad_keys = (
-        jnp.einsum("chqk,cqhd->ckhd", grad_scores, queries, preferred_element_type=jnp.float32)
-        * score_scale
-    )
-    grad_projected = jnp.concatenate(
-        [
-            grad_queries.reshape(row_count, D),
-            grad_keys.reshape(row_count, D),
-            grad_values.reshape(row_count, D),
-        ],
-        axis=1,
-    ).astype(bf16)
-    grad_w_qkv = left_dot(input_att, grad_projected)
-    grad_qkv_sums = jnp.sum(grad_projected.astype(jnp.float32), axis=0)
-    grad_b_query = grad_qkv_sums[:D]
-    grad_b_value = grad_qkv_sums[2 * D :]
-    grad_input_att = right_dot(grad_projected, w_qkv).reshape(columns, FRAMES, D)
-    grad_shift_att = jnp.sum(grad_input_att, axis=1)
-    grad_scale_att = jnp.sum(grad_input_att * normed_att, axis=1)
-    grad_states = grad_middle + norm_back(
-        grad_input_att * (1.0 + scale_att), normed_att, inverse_att
-    )
-    input_grad = jnp.where(is_video, grad_states, upstream).reshape(row_count, D)
-    grad_mods = jnp.stack(
-        [
-            grad_shift_att,
-            grad_scale_att,
-            grad_gate_att,
-            grad_shift_mlp,
-            grad_scale_mlp,
-            grad_gate_mlp,
-        ],
-        axis=1,
-    )
-    grad_mods = grad_mods.reshape(columns, 6 * D)
+    video = jnp.broadcast_to(1.0 - is_image.astype(f32)[:, None], (groups, D))
+    table = jnp.concatenate([mods_all, video], axis=1)
     membership = (column_sample[:, None] == jnp.arange(groups, dtype=jnp.int32)[None, :]).astype(
-        jnp.float32
-    )
-    mods_local = lax.dot_general(
-        membership,
-        grad_mods,
-        (((0,), (0,)), ((), ())),
-        precision=highest,
-        preferred_element_type=jnp.float32,
-    )
-    block_grads = [
-        grad.astype(bf16 if kernels else jnp.float32).reshape(-1, D)
-        for grad in (grad_w_qkv, grad_w_proj, grad_w_up, grad_w_down)
-    ]
-    bias_head = jnp.concatenate([grad_b_query, grad_b_value, grad_b_proj, grad_b_up, grad_b_down])
-    bias_head, grad_mods_all = lax.psum((bias_head, mods_local), axes)
+        f32
+    )
+    mods = jnp.take(table, column_sample, axis=0).reshape(columns, 7, D).transpose(1, 0, 2)
+    b_qkv = jnp.stack([b_query, jnp.zeros((D,), f32), b_value])
+    (
+        block_out, natural, input_att, proj, attended, branch, input_mlp, active, slope, grad_out,
+        grad_gate,
+    ) = forward(
+        flat, tokens, output_grad, mods, b_qkv, b_proj[None], b_up.reshape(4, D), b_down[None]
+    )
+    grads, input_grad, grad_mods, bias_sums = backward(
+        flat, natural, tokens, output_grad, mods, input_att, proj, attended, branch, input_mlp,
+        active, slope, grad_out,
+    )
+    grad_mods = jnp.concatenate([grad_mods, grad_gate[None]])
+    mods_local = exact(membership, grad_mods, (((0,), (1,)), ((), ()))).reshape(groups, 6 * D)
+    bias_head = jnp.concatenate([bias_sums[:1], bias_sums[2:4], bias_sums[5:9], bias_sums[4:5]])
+    bias_head, grad_mods_all = lax.psum((bias_head.reshape(-1), mods_local), axes)
     first_sum = jnp.concatenate([bias_head, jnp.sum(grad_mods_all, axis=0)])
-    block_shard = scatter_blocks(jnp.concatenate(block_grads), units, kernels)
+    block_shard = scatter_blocks(grads, units, kernels)
     mods_parts = grad_mods_all.reshape(groups * 6, D)
     ada_shard = exact(selector, mods_parts, (((1,), (0,)), ((), ())))
     unit = first_unit + jnp.arange(units, dtype=jnp.int32)

time: 923 us -> 625 us (0.68)
  local copies, waits for them, and re-layouts: 231 us -> 20.3 us
  Pallas kernels: 350 us -> 511 us
  other arithmetic: 158 us -> 19.3 us
  matrix products: 119 us -> 9.63 us
    pallas_call x2 -> x4, Pallas kernels: 350 us -> 511 us  [the longest x1 181 us: scatter_grads_kernel(): pl.pallas_call(scatter_kernel, out_shape=jax.ShapeDtypeStruct((GROUPS8, 8...]
    concatenate x2, other arithmetic: 114 us -> 0.05 us  [the longest x1 0.03 us: on_device(): table = jnp.concatenate([mods_all, video], axis=1)]
    reshape x13 -> x1, local copies, waits for them, and re-layouts: 113 us -> 0.01 us  [on_device(): bias_head.reshape(-1)]
    dot_general x20 -> x1, matrix products: 113 us -> 0.32 us  [tn_dot(): lax.dot_general(left, right, (((0,), (0,)), ((), ())), preferred_element_...]
    slice x4 -> x3, local copies, waits for them, and re-layouts: 41.2 us -> 2.51 us  [the longest x1 0.89 us: on_device(): bias_sums[5:9]]
    pad x2 -> x0, local copies, waits for them, and re-layouts: 33.6 us -> none  [the longest x1 32.4 us: scatter_blocks(): jnp.pad(padded, ((0, 0), (0, ROWS - UNITS), (0, 0)))]
    sub x2 -> x1, other arithmetic: 12.3 us -> 0.01 us  [on_device(): video = jnp.broadcast_to(1.0 - is_image.astype(f32)[:, None], (groups, D))]
    reduce_sum x6 -> x0, other arithmetic: 9.98 us -> none  [the longest x1 4.58 us: on_device(): grad_b_proj = jnp.sum(grad_branch.astype(jnp.float32), axis=0)]
  transfers between devices with their start and end apart: 2 -> 2, of which waited for: 0 -> 0; matrix products, arithmetic and copies ran while one was open for 31% -> 1% of each run, Pallas kernels for 38% -> 56%
where the time goes in v2:
time: 625 us; the launch traced here: 617 us
  Pallas kernels  511 us (82%)
  blocking collectives  39.1 us (6%)
  local copies, waits for them, and re-layouts  20.3 us (3%)
  other arithmetic  19.3 us (3%)
  between operations  17.3 us (3%)
  matrix products  9.63 us (2%)
    pallas_call x1, Pallas kernels, scatter_grads_kernel(): pl.pallas_call(scatter_kernel, out_shape=jax.ShapeDtypeStruct((GROUPS8, 8...  181 us
    pallas_call x1, Pallas kernels, gather_weights(): pl.pallas_call(gather_kernel, out_shape=jax.ShapeDtypeStruct((4, 4, 2, GR...  162 us
    pallas_call x1, Pallas kernels, backward(): pl.pallas_call(backward_kernel, out_shape=[shape((32 * UNITS // 8, 8, D),...  98.4 us
    pallas_call x1, Pallas kernels, forward(): pl.pallas_call(forward_kernel, out_shape=[shape((rows, D), f32), shape((7...  69.8 us
    psum x1, blocking collectives, on_device(): lax.psum((jnp.sum(grad_units * grad_units), grad_soft), axes)  39.1 us
  transfers between devices with their start and end apart: 2, of which 0 were waited for; matrix products, arithmetic and copies ran while one was open for 1% of the time, Pallas kernels for 56%

profile of v2, /device:TPU:0, one launch (start us, length us, event | category | flops | bytes accessed | tf_op | source)
XLA Modules:
  0.0 616.8 jit_solution(7132249835461318079)
XLA Ops:
  7.2 0.0 all-reduce.5.cloned.1.call-start
  7.3 0.7 fusion.12
  8.0 0.5 broadcast_in_dim.52
  8.5 1.1 reshape.165
  9.6 0.1 fusion.11
  9.8 2.0 convert_element_type.49
  11.8 0.0 copy-start.8
  11.8 0.0 copy-start.9
  11.8 0.0 copy-start.2
  11.8 1.7 convert_element_type.56
  13.5 0.3 fusion.27
  13.8 0.7 reshape.166
  14.5 0.0 all-reduce.5.cloned.1.call-update
  14.5 0.0 all-reduce.7.cloned.1.call-start
  14.6 0.0 copy-done.8
  14.6 0.0 copy-done.9
  14.7 0.0 copy-done.2
  14.7 0.1 pad.14.clone
  14.8 0.7 pad_maximum_fusion.3.b_qkv
  15.5 2.8 convert_element_type.50.shard
  18.3 0.6 broadcast_in_dim.56.b_proj
  18.9 0.6 broadcast_in_dim.57.b_down
  19.5 162.2 %gather_weights.1 = bf16[4,4,2,81,8,1152]{5,4,3,2,1,0:T(8,128)(2,1)} custom-call(bf16[81,8,1152]{2,1,0:T(8,128)(2,1)} %convert_element_type.50.shard), custom_call_target="tpu_custom_call" | custom-call | tf_op jit(solution)/shard_map/gather_weights/pallas_call | solution.py:290
  181.7 0.6 slice.48.b_up
  182.3 0.6 mul.156
  183.0 0.0 slice-done
  183.0 0.9 broadcast_add_fusion
  183.9 0.1 broadcast_in_dim.53
  184.0 0.8 gather_fusion
  184.8 1.0 fusion.1.mods
  185.8 69.8 %block_forward.1 = (f32[384,1152]{1,0:T(8,128)}, bf16[7,144,8,1152]{3,2,1,0:T(8,128)(2,1)}, bf16[384,1152]{1,0:T(8,128)(2,1)}, bf16[3,384,1152]{2,1,0:T(8,128)(2...) custom-call(bf16[2592,8,1152]{2,1,0:T(8,128)(2,1)} %bitcast.35, ...), custom_call_target="tpu_custom_call" | custom-call | tf_op jit(solution)/shard_map/block_forward/pallas_call | solution.py:751
  255.6 0.0 copy-start.4
  255.6 98.4 %block_backward.1 = (bf16[2592,8,1152]{2,1,0:T(8,128)(2,1)}, f32[384,1152]{1,0:T(8,128)}, f32[5,24,1152]{2,1,0:T(8,128)}, f32[16,1152]{1,0:T(8,128)}) custom-call(bf16[2592,8,1152]{2,1,0:T(8,128)(2,1)} %bitcast.36, bf16[7,144,8,1152]{3,2,1,0:T(8,128)(2,1)} %get-tuple-element.26.natural, bf16[384,1152]{1,0:T(8,128)(2,1)} %tokens.3, ...), custom_call_target="tpu_custom_call" | custom-call | tf_op jit(solution)/shard_map/block_backward/pallas_call | solution.py:979
  354.0 0.9 slice.53
  354.9 0.8 fusion.25
  355.7 0.8 slice.52
  356.5 0.0 copy-done.4
  356.5 2.0 fusion.2
  358.5 0.0 all-reduce.7.cloned.1.call-update
  358.6 180.6 %scatter_grads.1 = bf16[81,8,1152]{2,1,0:T(8,128)(2,1)} custom-call(bf16[4,4,2,81,8,1152]{5,4,3,2,1,0:T(8,128)(2,1)} %bitcast.37), custom_call_target="tpu_custom_call" | custom-call | tf_op jit(solution)/shard_map/scatter_grads/pallas_call | solution.py:506
  539.2 0.0 all-reduce.7.cloned.1.call-done
  539.2 1.0 reshape.168
  540.2 1.3 convolution_bitcast_fusion
  541.5 0.0 copy-start
  541.6 0.3 dynamic_update_slice.3
  541.9 0.1 slice.57
  542.0 1.8 reshape.170
  543.8 0.0 copy-start.1
  543.8 0.6 reduce_sum.46
  544.4 0.0 copy-done
  544.4 6.0 multiply_reduce_fusion
  550.4 39.1 %all-reduce.1 = (f32[3,1152]{1,0:T(4,128)S(1)}, f32[]{:T(128)}, f32[9216]{0:T(1024)S(1)}) all-reduce(f32[3,1152]{1,0:T(4,128)S(1)} %reduce_sum.46, f32[]{:T(128)} %get-tuple-element.57, f32[9216]{0:T(1024)S(1)} %reshape.172), channel_id=1, replica_groups=mesh['outer'=4,'inner'=8] {'outer','inner'}, use_global_device_ids=true, to_apply=%region_4.5 | all-reduce | flops 12673 | bytes 101384 | tf_op jit(solution)/shard_map/psum | solution.py:1123
  589.5 0.0 copy-done.1
  589.5 0.1 reduce_sum.48
  589.6 0.6 multiply_reduce_fusion.2
  591.6 3.7 broadcast_multiply_fusion.1
  595.3 4.2 mul.161
  599.4 0.0 copy-done.5
  599.4 0.6 fusion.10
  600.1 0.0 copy-done.3
  600.1 0.0 copy-done.6
  600.1 0.0 copy-done.7
  600.1 0.7 multiply_subtract_fusion.1
  600.8 7.5 %multiply_subtract_fusion = (f32[746496]{0:T(1024)}, f32[746496]{0:T(1024)}, f32[746496]{0:T(1024)}) fusion(f32[746496]{0:T(1024)} %param.16, f32[746496]{0:T(1024)} %param.17, f32[746496]{0:T(1024)} %mul.161, f32[746496]{0:T(1024)} %param.18), kind=kLoop, calls=%fused_computation.4 | loop fusion | flops 10450944 | bytes 20901888 | tf_op jit(solution)/shard_map/sub | solution.py:1057
  (26 shorter events, 0.3 us)
Async XLA Ops:
  7.2 175.8 %all-reduce.5.cloned.1.call-start = ((), (), s32[]{:S(2)}) async-start(), calls=%async_computation | async-start | bytes 221184 | tf_op jit(solution)/shard_map/psum | solution.py:1089
  11.8 2.8 copy-start.8
  11.8 2.9 copy-start.9
  11.8 2.9 copy-start.2
  14.5 524.7 %all-reduce.7.cloned.1.call-start = ((), (), s32[]{:S(2)}) async-start(), calls=%async_computation.1 | async-start | bytes 221184 | tf_op jit(solution)/shard_map/psum | solution.py:1110
  19.5 163.5 %slice-start = ((f32[16128]{0:T(1024)}), f32[6912]{0:T(1024)S(1)}, s32[]{:S(2)}) async-start(f32[16128]{0:T(1024)} %param.19), calls=%async_computation.2 | async-start | bytes 57344 | tf_op jit(solution)/shard_map/slice | solution.py:1028
  255.6 100.9 %copy-start.4 = (f32[24,1152]{1,0:T(8,128)S(1)}, f32[24,1152]{1,0:T(8,128)}, u32[]{:S(2)}) copy-start(f32[24,1152]{1,0:T(8,128)} %get-tuple-element.37) | copy-start | bytes 331780
  541.5 2.9 copy-start
  543.8 45.7 %copy-start.1 = (f32[3,6912]{1,0:T(4,128)S(1)}, f32[3,6912]{1,0:T(4,128)}, u32[]{:S(2)}) copy-start(f32[3,6912]{1,0:T(4,128)} %all-reduce.7.cloned.1.call-done) | copy-start | bytes 248836
  595.3 4.2 copy-start.5
  595.3 4.8 copy-start.3
  595.3 4.8 copy-start.6
  595.3 4.8 copy-start.7
Sparse Core Ops, SparseCore 0:
  14.7 150.5 all-reduce.4
  358.7 158.0 all-reduce.6

commit v3 on v2

--- a/solution.py
+++ b/solution.py
@@ -131,11 +131,7 @@
 GATHER_COPIES = 3 * (3 + 3 + 4 * 4 + 8) + 7
 
 
-def gather_kernel(shard, full, send_sems, recv_sems, local_sems):
-    me = Place()
-    cp = Copies(send_sems, recv_sems)
-    me.greet()
-
+def gather_stages(me, cp, shard, full, local_sems):
     def part(p, zb, yb, x, c, first=0, n=QUART):
         return full.at[p, zb, yb, pl.ds((2 * QUART * x + QUART * c + first), n)]
 
@@ -281,25 +277,7 @@
         for h in (0, 1):
             cp.wait_recv(slots["tc", h], full.at[h * 2 + me.co, :, :, tails], me.dev(dc=1))
 
-    s0(0); s0(1); s0(2); s1(0); t1(); s2(0); s1(1); s3(0); t2(); s2(1); s1(2); s4(0); t3()
-    s3(1); s2(2); s5(0); s4(1); t4(); s3(2); s5(1); s4(2); s5(2); t5()
-    cp.drain()
-
-
-def gather_weights(shard):
-    return pl.pallas_call(
-        gather_kernel,
-        out_shape=jax.ShapeDtypeStruct((4, 4, 2, GROUPS8, 8, D), jnp.bfloat16),
-        in_specs=[pl.BlockSpec(memory_space=pl.ANY)],
-        out_specs=pl.BlockSpec(memory_space=pl.ANY),
-        scratch_shapes=[
-            pltpu.SemaphoreType.DMA((GATHER_COPIES,)),
-            pltpu.SemaphoreType.DMA((GATHER_COPIES,)),
-            pltpu.SemaphoreType.DMA((2,)),
-        ],
-        compiler_params=pltpu.CompilerParams(collective_id=0, has_side_effects=True),
-        name="gather_weights",
-    )(shard)
+    return dict(s0=s0, s1=s1, s2=s2, s3=s3, s4=s4, s5=s5, t1=t1, t2=t2, t3=t3, t4=t4, t5=t5)
 
 
 SCATTER_COPIES = 3 * (4 * 2 + 4 * 4 + 3 + 3) + 8
@@ -582,7 +560,7 @@
     lax.fori_loop(0, count, step, 0)
 
 
-def split_rows(src, spread, put, ways, step):
+def split_rows(src, spread, put, ways):
     units = src.shape[0] * 8
     rows = units // ways
     for q in range(9):
@@ -615,10 +593,49 @@
     return grown / jnp.sum(grown, axis=-1, keepdims=True)
 
 
-def forward_kernel(
+SUM_COPIES = 6
+SUM_SLOTS = 10
+
+
+def sum_stages(me, cp, mine, buf):
+    slots = {}
+
+    def send(name, src, dst, device):
+        slots[name] = cp.slot()
+        cp.send(slots[name], src, dst, device)
+
+    def m1():
+        send("c", mine, buf.at[0], me.dev(dc=1))
+
+    def m2():
+        cp.wait_recv(slots["c"], buf.at[0], me.dev(dc=1))
+        buf[1] = mine[...] + buf[0]
+        send("x", buf.at[1], buf.at[2], me.dev(dx=1))
+
+    def m3():
+        cp.wait_recv(slots["x"], buf.at[2], me.dev(dx=1))
+        buf[3] = buf[1] + buf[2]
+        send("y", buf.at[3], buf.at[4], me.dev(dy=1))
+
+    def m4():
+        cp.wait_recv(slots["y"], buf.at[4], me.dev(dy=1))
+        buf[5] = buf[3] + buf[4]
+        buf[6 + me.z] = buf[5]
+        for d in (1, 2, 3):
+            send(d, buf.at[5], buf.at[6 + me.z], me.dev(dz=d))
+
+    def total():
+        for d in (1, 2, 3):
+            cp.wait_recv(slots[d], buf.at[6 + flip(me.z, d)], me.dev(dz=d))
+        return (buf[6] + buf[7]) + (buf[8] + buf[9])
+
+    return m1, m2, m3, m4, total
+
+
+def forward_body(
     weights, tokens, upstream, mods, b_qkv, b_proj, b_up, b_down,
-    block_out, natural, input_att, proj, attended, branch, input_mlp, active, slope, grad_out,
-    grad_gate, held, stage, spread, acc, hid, copy_sems,
+    block_out, natural, input_att, proj_out, attended, branch, input_mlp, active_out, slope_out,
+    grad_out, grad_gate, held, stage, spread, acc, hid, proj, active, slope, copy_sems, ready,
 ):
     columns = mods.shape[1]
 
@@ -635,6 +652,9 @@
     def save(mat, slot):
         return pltpu.make_async_copy(held.at[slot], natural.at[mat], copy_sems.at[10 + mat])
 
+    def keep(src, dst, n):
+        return pltpu.make_async_copy(src, dst, copy_sems.at[17 + n])
+
     def unweave(first, ways, slot0, blocks=9):
         groups = 16 * ways
         fetch(first, groups, 0).start()
@@ -650,18 +670,18 @@
             def put(w, lanes, block):
                 held[slot0 + w, pl.ds(j * 16, 16), :, lanes] = block
 
-            split_rows(stage.at[slot, pl.ds(0, groups)], spread, put, ways, None)
+            split_rows(stage.at[slot, pl.ds(0, groups)], spread, put, ways)
             return carry
 
         lax.fori_loop(0, blocks, step, 0)
-
-    whole(3, 3).start()
 
     def first_norm(c, rows, at):
         normed, _ = norm_rows(tokens[rows].astype(f32))
         input_att[rows] = (normed * (1.0 + mods[1, at]) + mods[0, at]).astype(bf16)
 
     over_columns(columns, first_norm)
+    ready("qkv")
+    whole(3, 3).start()
     unweave(0, 3, 0)
     for p in range(3):
         save(p, p).start()
@@ -671,6 +691,7 @@
         return carry
 
     lax.fori_loop(0, 3, project, 0)
+    keep(proj, proj_out, 0).start()
 
     inside = same_column()
 
@@ -685,12 +706,11 @@
         return carry
 
     lax.fori_loop(0, columns * FRAMES // 128, attend, 0)
+    ready("proj")
     whole(3, 3).wait()
     branch[...] = nn_dot(attended[...], square(held.at[3])) + b_proj[...]
     for p in range(3):
         save(p, p).wait()
-    for b in range(4):
-        whole(8 + b, b).start()
 
     def second_norm(c, rows, at):
         middle = tokens[rows].astype(f32) + mods[2, at] * branch[rows]
@@ -698,6 +718,7 @@
         input_mlp[rows] = (normed * (1.0 + mods[4, at]) + mods[3, at]).astype(bf16)
 
     over_columns(columns, second_norm)
+    ready("up")
     unweave(AT_UP, 4, 4)
     for b in range(4):
         save(3 + b, 4 + b).start()
@@ -717,15 +738,15 @@
         return carry
 
     lax.fori_loop(0, 4, raise_, 0)
+    keep(active, active_out, 1).start()
+    keep(slope, slope_out, 2).start()
     acc[...] = jnp.broadcast_to(b_down[...], acc.shape)
+    ready("down")
+    for b in range(4):
+        whole(8 + b, b).start()
     for b in range(4):
         whole(8 + b, b).wait()
-
-    def lower(b, carry):
         acc[...] += nn_dot(active[b], square(held.at[b]))
-        return carry
-
-    lax.fori_loop(0, 4, lower, 0)
 
     def last(c, rows, at):
         x = tokens[rows].astype(f32)
@@ -740,42 +761,149 @@
     over_columns(columns, last)
     for b in range(4):
         save(3 + b, 4 + b).wait()
+    keep(proj, proj_out, 0).wait()
+    keep(active, active_out, 1).wait()
+    keep(slope, slope_out, 2).wait()
+
+
+def forward_kernel(*refs):
+    forward_body(*refs, lambda name: None)
+
+
+def gather_forward_kernel(
+    shard, partial, chosen, base, tokens, upstream, b_qkv, b_proj, b_up, b_down,
+    full, mods, *refs,
+):
+    refs, (sums, send_sems, recv_sems, local_sems) = refs[:-4], refs[-4:]
+    me = Place()
+    cp = Copies(send_sems, recv_sems)
+    st = gather_stages(me, cp, shard, full, local_sems)
+    s0, s1, s2, s3, s4, s5 = (st["s%d" % n] for n in range(6))
+    t1, t2, t3, t4, t5 = (st["t%d" % n] for n in range(1, 6))
+    m1, m2, m3, m4, total = sum_stages(me, cp, partial, sums)
+    me.greet()
+    m1()
+    s0(0)
+    m2()
+    s0(1)
+    s1(0)
+    m3()
+    s0(2)
+    t1()
+    s2(0)
+    m4()
+    t2()
+    s1(1)
+    s3(0)
+    t3()
+    s2(1)
+    t4()
+    s1(2)
+    table = exact(chosen[...], total(), (((1,), (0,)), ((), ()))) + base[...]
+    columns = mods.shape[1]
+    for n in range(7):
+        mods[n] = table[n * columns : (n + 1) * columns]
+
+    def ready(name):
+        if name == "qkv":
+            s4(0)
+            s3(1)
+            t5()
+            s2(2)
+            s5(0)
+        if name == "proj":
+            s4(1)
+        if name == "up":
+            s3(2)
+            s5(1)
+        if name == "down":
+            s4(2)
+            s5(2)
+
+    forward_body(
+        full.reshape(4 * 4 * 2 * GROUPS8, 8, D), tokens, upstream, mods, b_qkv, b_proj, b_up,
+        b_down, *refs, ready,
+    )
+    cp.drain()
+
+
+def forward_shapes(rows, columns):
+    shape = jax.ShapeDtypeStruct
+    return [
+        shape((rows, D), f32),
+        shape((7, MATS, 8, D), bf16),
+        shape((rows, D), bf16),
+        shape((3, rows, D), bf16),
+        shape((rows, D), bf16),
+        shape((rows, D), f32),
+        shape((rows, D), bf16),
+        shape((4, rows, D), bf16),
+        shape((4, rows, D), f32),
+        shape((rows, D), bf16),
+        shape((columns, D), f32),
+    ]
+
+
+VMEM_SPEC = pl.BlockSpec(memory_space=pltpu.VMEM)
+HBM_SPEC = pl.BlockSpec(memory_space=pl.ANY)
+FORWARD_SPECS = [
+    VMEM_SPEC, HBM_SPEC, VMEM_SPEC, HBM_SPEC, VMEM_SPEC, VMEM_SPEC, VMEM_SPEC, HBM_SPEC, HBM_SPEC,
+    VMEM_SPEC, VMEM_SPEC,
+]
+
+
+def forward_scratch(rows):
+    return [
+        pltpu.VMEM((8, MATS, 8, D), bf16),
+        pltpu.VMEM((2, 64, 8, D), bf16),
+        pltpu.VMEM((9, 512, 128), f32),
+        pltpu.VMEM((rows, D), f32),
+        pltpu.VMEM((rows, D), f32),
+        pltpu.VMEM((3, rows, D), bf16),
+        pltpu.VMEM((4, rows, D), bf16),
+        pltpu.VMEM((4, rows, D), f32),
+        pltpu.SemaphoreType.DMA((20,)),
+    ]
 
 
 def forward(weights, tokens, upstream, mods, b_qkv, b_proj, b_up, b_down):
     rows = tokens.shape[0]
-    columns = mods.shape[1]
-    vmem = pl.BlockSpec(memory_space=pltpu.VMEM)
-    hbm = pl.BlockSpec(memory_space=pl.ANY)
-    shape = jax.ShapeDtypeStruct
     return pl.pallas_call(
         forward_kernel,
-        out_shape=[
-            shape((rows, D), f32),
-            shape((7, MATS, 8, D), bf16),
-            shape((rows, D), bf16),
-            shape((3, rows, D), bf16),
-            shape((rows, D), bf16),
-            shape((rows, D), f32),
-            shape((rows, D), bf16),
-            shape((4, rows, D), bf16),
-            shape((4, rows, D), f32),
-            shape((rows, D), bf16),
-            shape((columns, D), f32),
-        ],
-        in_specs=[hbm] + [vmem] * 7,
-        out_specs=[vmem, hbm] + [vmem] * 9,
-        scratch_shapes=[
-            pltpu.VMEM((8, MATS, 8, D), bf16),
-            pltpu.VMEM((2, 64, 8, D), bf16),
-            pltpu.VMEM((9, 512, 128), f32),
-            pltpu.VMEM((rows, D), f32),
-            pltpu.VMEM((rows, D), f32),
-            pltpu.SemaphoreType.DMA((17,)),
-        ],
+        out_shape=forward_shapes(rows, mods.shape[1]),
+        in_specs=[HBM_SPEC] + [VMEM_SPEC] * 7,
+        out_specs=FORWARD_SPECS,
+        scratch_shapes=forward_scratch(rows),
         compiler_params=pltpu.CompilerParams(vmem_limit_bytes=60 * 2**20),
         name="block_forward",
     )(weights, tokens, upstream, mods, b_qkv, b_proj, b_up, b_down)
+
+
+def gather_forward(shard, partial, chosen, base, tokens, upstream, b_qkv, b_proj, b_up, b_down):
+    rows = tokens.shape[0]
+    columns = rows // FRAMES
+    copies = GATHER_COPIES + SUM_COPIES
+    return pl.pallas_call(
+        gather_forward_kernel,
+        out_shape=[
+            jax.ShapeDtypeStruct((4, 4, 2, GROUPS8, 8, D), bf16),
+            jax.ShapeDtypeStruct((7, columns, D), f32),
+        ]
+        + forward_shapes(rows, columns),
+        in_specs=[HBM_SPEC] + [VMEM_SPEC] * 9,
+        out_specs=[HBM_SPEC, VMEM_SPEC] + FORWARD_SPECS,
+        scratch_shapes=forward_scratch(rows)
+        + [
+            pltpu.VMEM((SUM_SLOTS, *partial.shape), f32),
+            pltpu.SemaphoreType.DMA((copies,)),
+            pltpu.SemaphoreType.DMA((copies,)),
+            pltpu.SemaphoreType.DMA((2,)),
+        ],
+        compiler_params=pltpu.CompilerParams(
+            collective_id=0, has_side_effects=True, vmem_limit_bytes=62 * 2**20
+        ),
+        name="gather_forward",
+    )(shard, partial, chosen, base, tokens, upstream, b_qkv, b_proj, b_up, b_down)
 
 
 def backward_kernel(
@@ -1004,11 +1132,9 @@
     )(weights, natural, *operands)
 
 
-def gather_blocks(shard_low, kernels):
-    if not kernels:
-        whole = lax.all_gather(shard_low, ("outer", "inner"), axis=0, tiled=True)
-        return whole.reshape(-1, 8, D)
-    return gather_weights(shard_low.reshape(GROUPS8, 8, D)).reshape(-1, 8, D)
+def gather_blocks(shard_low):
+    whole = lax.all_gather(shard_low, ("outer", "inner"), axis=0, tiled=True)
+    return whole.reshape(-1, 8, D)
 
 
 def scatter_blocks(grads, units, kernels):
@@ -1081,25 +1207,38 @@
     first_unit = lax.axis_index(axes).astype(jnp.int32) * units
     shard = weights.reshape(units, D)
     shard_low = shard.astype(bf16)
-    flat = gather_blocks(shard_low, kernels)
     b_query, b_value, b_proj, b_up, b_down, b_ada = split_bias(biases)
     soft_cond = jax.nn.silu(conditioning).astype(bf16)
     selector, ada_part = ada_selector(soft_cond, first_unit, units)
-    mods_all = tn_dot(selector.astype(bf16), shard_low)
-    mods_all = lax.psum(mods_all, axes).reshape(groups, 6 * D) + b_ada
-    video = jnp.broadcast_to(1.0 - is_image.astype(f32)[:, None], (groups, D))
-    table = jnp.concatenate([mods_all, video], axis=1)
+    mods_part = tn_dot(selector.astype(bf16), shard_low)
     membership = (column_sample[:, None] == jnp.arange(groups, dtype=jnp.int32)[None, :]).astype(
         f32
     )
-    mods = jnp.take(table, column_sample, axis=0).reshape(columns, 7, D).transpose(1, 0, 2)
+    video_cols = exact(membership, 1.0 - is_image.astype(f32)[:, None], (((1,), (0,)), ((), ())))
     b_qkv = jnp.stack([b_query, jnp.zeros((D,), f32), b_value])
+    bias_args = (b_qkv, b_proj[None], b_up.reshape(4, D), b_down[None])
+    video_plane = jnp.broadcast_to(video_cols, (columns, D))
+    if kernels:
+        eye = jnp.eye(6, dtype=f32)
+        chosen = membership[None, :, :, None] * eye[:, None, None, :]
+        chosen = jnp.pad(chosen.reshape(6 * columns, groups * 6), ((0, columns), (0, 0)))
+        base = jnp.repeat(b_ada.reshape(6, D), columns, axis=0)
+        base = jnp.concatenate([base, video_plane])
+        flat, mods, *saved = gather_forward(
+            shard_low.reshape(GROUPS8, 8, D), mods_part, chosen, base, tokens, output_grad,
+            *bias_args,
+        )
+        flat = flat.reshape(-1, 8, D)
+    else:
+        flat = gather_blocks(shard_low)
+        mods_all = lax.psum(mods_part, axes).reshape(groups, 6 * D) + b_ada
+        mods = jnp.take(mods_all, column_sample, axis=0).reshape(columns, 6, D).transpose(1, 0, 2)
+        mods = jnp.concatenate([mods, video_plane[None]])
+        saved = forward(flat, tokens, output_grad, mods, *bias_args)
     (
         block_out, natural, input_att, proj, attended, branch, input_mlp, active, slope, grad_out,
         grad_gate,
-    ) = forward(
-        flat, tokens, output_grad, mods, b_qkv, b_proj[None], b_up.reshape(4, D), b_down[None]
-    )
+    ) = saved
     grads, input_grad, grad_mods, bias_sums = backward(
         flat, natural, tokens, output_grad, mods, input_att, proj, attended, branch, input_mlp,
         active, slope, grad_out,

time: 625 us -> 581 us (0.930)
  Pallas kernels: 511 us -> 470 us
    pallas_call x2 -> x1, Pallas kernels: 232 us -> 203 us  [gather_forward(): pl.pallas_call(gather_forward_kernel, out_shape=[jax.ShapeDtypeStruct((4,...]
    pallas_call x1, Pallas kernels: 181 us -> 169 us  [scatter_grads_kernel(): pl.pallas_call(scatter_kernel, out_shape=jax.ShapeDtypeStruct((GROUPS8, 8...]
  transfers between devices with their start and end apart: 2 -> 1, of which waited for: 0 -> 0; matrix products, arithmetic and copies ran while one was open for 1% -> 0% of each run, Pallas kernels for 56% -> 29%
where the time goes in v3:
time: 581 us; the launch traced here: 574 us
  Pallas kernels  470 us (81%)
  blocking collectives  38.9 us (7%)
  local copies, waits for them, and re-layouts  23.3 us (4%)
  between operations  17.3 us (3%)
  other arithmetic  15.2 us (3%)
  matrix products  9.56 us (2%)
    pallas_call x1, Pallas kernels, gather_forward(): pl.pallas_call(gather_forward_kernel, out_shape=[jax.ShapeDtypeStruct((4,...  203 us
    pallas_call x1, Pallas kernels, scatter_grads_kernel(): pl.pallas_call(scatter_kernel, out_shape=jax.ShapeDtypeStruct((GROUPS8, 8...  169 us
    pallas_call x1, Pallas kernels, backward(): pl.pallas_call(backward_kernel, out_shape=[shape((32 * UNITS // 8, 8, D),...  98.1 us
    psum x1, blocking collectives, on_device(): lax.psum((jnp.sum(grad_units * grad_units), grad_soft), axes)  38.9 us
  transfers between devices with their start and end apart: 1, of which 0 were waited for; matrix products, arithmetic and copies ran while one was open for 0% of the time, Pallas kernels for 29%

profile of v3, /device:TPU:0, one launch (start us, length us, event | category | flops | bytes accessed | tf_op | source)
XLA Modules:
  0.0 574.3 jit_solution(6938675510914647592)
XLA Ops:
  7.2 0.0 all-reduce.5.cloned.1.call-start
  7.3 2.0 convert_element_type.64
  9.3 0.0 copy-start.3
  9.3 0.0 copy-start.5
  9.3 1.7 convert_element_type.71
  11.0 0.0 slice-start
  11.0 0.0 copy-start.8
  11.0 0.0 copy-start.9
  11.0 2.8 convert_element_type.65.shard
  13.8 0.0 copy-done.3
  13.9 0.0 copy-done.5
  13.9 1.7 broadcast_in_dim.19
  15.6 2.5 reshape.196
  18.2 0.1 fusion.10
  18.4 0.6 broadcast_in_dim.22.b_proj
  19.0 0.6 broadcast_in_dim.26.b_down
  19.6 0.0 slice-done
  19.6 0.0 copy-done.8
  19.6 0.0 copy-done.9
  19.6 0.1 convolution_bitcast_fusion.1
  19.7 0.1 pad.19.clone
  19.8 0.1 pad.22.clone
  19.9 0.1 broadcast_multiply_fusion.2
  19.9 0.1 mul.171
  20.0 0.1 copy.23
  20.2 0.6 pad.9.chosen
  20.8 0.6 slice.59.b_up
  21.4 1.0 fusion.32.partial
  22.4 1.0 pad_maximum_fusion.base
  23.4 0.7 pad_maximum_fusion.3.b_qkv
  24.1 203.2 %gather_forward.1 = (bf16[4,4,2,81,8,1152]{5,4,3,2,1,0:T(8,128)(2,1)}, f32[7,24,1152]{2,1,0:T(8,128)}, f32[384,1152]{1,0:T(8,128)}, bf16[7,144,8,1152]{3,2,1,0:T...) custom-call(bf16[81,8,1152]{2,1,0:T(8,128)(2,1)} %convert_element_ty, ...), custom_call_target="tpu_custom_call" | custom-call | tf_op jit(solution)/shard_map/gather_forward/pallas_call | solution.py:886
  227.3 0.0 copy-start.4
  227.3 98.1 %block_backward.1 = (bf16[2592,8,1152]{2,1,0:T(8,128)(2,1)}, f32[384,1152]{1,0:T(8,128)}, f32[5,24,1152]{2,1,0:T(8,128)}, f32[16,1152]{1,0:T(8,128)}) custom-call(bf16[2592,8,1152]{2,1,0:T(8,128)(2,1)} %bitcast.37, bf16[7,144,8,1152]{3,2,1,0:T(8,128)(2,1)} %get-tuple-element.29.natural, bf16[384,1152]{1,0:T(8,128)(2,1)} %tokens.3, ...), custom_call_target="tpu_custom_call" | custom-call | tf_op jit(solution)/shard_map/block_backward/pallas_call | solution.py:1107
  325.4 0.0 copy-done.4
  325.4 2.0 fusion.1
  327.4 0.0 all-reduce.5.cloned.1.call-update
  327.5 0.9 slice.64
  328.4 0.8 fusion.30
  329.2 0.8 slice.63
  330.0 168.6 %scatter_grads.1 = bf16[81,8,1152]{2,1,0:T(8,128)(2,1)} custom-call(bf16[4,4,2,81,8,1152]{5,4,3,2,1,0:T(8,128)(2,1)} %bitcast.36), custom_call_target="tpu_custom_call" | custom-call | tf_op jit(solution)/shard_map/scatter_grads/pallas_call | solution.py:484
  498.7 0.0 all-reduce.5.cloned.1.call-done
  498.7 1.0 reshape.200
  499.7 1.3 convolution_bitcast_fusion
  501.0 0.3 dynamic_update_slice.3
  501.4 0.1 slice.66
  501.5 1.8 reshape.202
  503.3 0.0 copy-start.2
  503.3 0.6 reduce_sum.46
  503.9 5.1 multiply_reduce_fusion
  509.0 38.9 %all-reduce.2 = (f32[3,1152]{1,0:T(4,128)S(1)}, f32[]{:T(128)}, f32[9216]{0:T(1024)S(1)}) all-reduce(f32[3,1152]{1,0:T(4,128)S(1)} %reduce_sum.46, f32[]{:T(128)} %get-tuple-element.61, f32[9216]{0:T(1024)S(1)} %reshape.204), channel_id=1, replica_groups=mesh['outer'=4,'inner'=8] {'outer','inner'}, use_global_device_ids=true, to_apply=%region_3.4 | all-reduce | flops 12673 | bytes 101384 | tf_op jit(solution)/shard_map/psum | solution.py:1262
  547.9 0.0 copy-done.2
  547.9 0.1 reduce_sum.48
  548.0 0.6 multiply_reduce_fusion.2
  550.0 1.8 broadcast_multiply_fusion.1
  551.8 0.0 copy-start.6
  551.8 4.5 mul.182
  556.4 0.6 fusion.9
  557.0 0.0 copy-done.6
  557.0 0.0 copy-done.7
  557.0 0.7 multiply_subtract_fusion.1
  557.7 0.0 copy-done
  557.7 7.0 %multiply_subtract_fusion = (f32[746496]{0:T(1024)}, f32[746496]{0:T(1024)}, f32[746496]{0:T(1024)}) fusion(f32[746496]{0:T(1024)S(1)} %copy-done, f32[746496]{0:T(1024)} %param.17, f32[746496]{0:T(1024)} %mul.182, f32[746496]{0:T(1024)} %param.18), kind=kLoop, calls=%fused_computation.3 | loop fusion | flops 10450944 | bytes 20901888 | tf_op jit(solution)/shard_map/sub | solution.py:1183
  564.7 0.0 copy-done.1
  564.7 1.2 copy.27
  (24 shorter events, 0.3 us)
Async XLA Ops:
  7.2 491.5 %all-reduce.5.cloned.1.call-start = ((), (), s32[]{:S(2)}) async-start(), calls=%async_computation | async-start | bytes 221184 | tf_op jit(solution)/shard_map/psum | solution.py:1249
  9.3 4.6 copy-start.3
  9.3 4.6 copy-start.5
  11.0 8.6 %slice-start = ((f32[16128]{0:T(1024)}), f32[6912]{0:T(1024)S(1)}, s32[]{:S(2)}) async-start(f32[16128]{0:T(1024)} %param.19), calls=%async_computation.1 | async-start | bytes 57344 | tf_op jit(solution)/shard_map/slice | solution.py:1154
  11.0 8.6 %copy-start.8 = (s32[24]{0:T(128)S(1)}, s32[24]{0:T(128)}, u32[]{:S(2)}) copy-start(s32[24]{0:T(128)} %param.13) | copy-start | bytes 292
  11.0 8.6 %copy-start.9 = (s32[3]{0:T(128)S(1)}, s32[3]{0:T(128)}, u32[]{:S(2)}) copy-start(s32[3]{0:T(128)} %param.14) | copy-start | bytes 40
  227.3 98.1 %copy-start.4 = (f32[24,1152]{1,0:T(8,128)S(1)}, f32[24,1152]{1,0:T(8,128)}, u32[]{:S(2)}) copy-start(f32[24,1152]{1,0:T(8,128)} %get-tuple-element.41) | copy-start | bytes 331780
  503.3 44.6 %copy-start.2 = (f32[3,6912]{1,0:T(4,128)S(1)}, f32[3,6912]{1,0:T(4,128)}, u32[]{:S(2)}) copy-start(f32[3,6912]{1,0:T(4,128)} %all-reduce.5.cloned.1.call-done) | copy-start | bytes 248836
  551.8 5.2 copy-start.6
  551.8 5.2 copy-start.7
  551.8 5.9 %copy-start = (f32[746496]{0:T(1024)S(1)}, f32[746496]{0:T(1024)}, u32[]{:S(2)}) copy-start(f32[746496]{0:T(1024)} %param.16) | copy-start | bytes 8957956
  557.7 7.0 %copy-start.1 = (f32[384,1152]{1,0:T(8,128)S(1)}, f32[384,1152]{1,0:T(8,128)}, u32[]{:S(2)}) copy-start(f32[384,1152]{1,0:T(8,128)} %get-tuple-element.73) | copy-start | bytes 5308420
Sparse Core Ops, SparseCore 0:
  327.6 147.4 all-reduce.4

commit v4 on v3

--- a/solution.py
+++ b/solution.py
@@ -30,7 +30,8 @@
 UNITS = 648
 GROUPS8 = 81
 QUART = 20
-HALFQ = 10
+FIRST = 8
+SECOND = QUART - FIRST
 MAIN = 80
 TAIL = 1
 DEPTH = (4, 4, 3)
@@ -104,6 +105,19 @@
             go()
         else:
             pl.when(cond)(go)
+
+    def wait_send(self, wanted):
+        for entry in self.sent:
+            if entry[0] == wanted:
+                slot, src, dst, device, cond = entry
+
+                def go():
+                    self.make(slot, src, dst, device).wait_send()
+                if cond is None:
+                    go()
+                else:
+                    pl.when(cond)(go)
+        self.sent = [entry for entry in self.sent if entry[0] != wanted]
 
     def drain(self):
         for slot, src, dst, device, cond in self.sent:
@@ -208,13 +222,13 @@
                 slots["y1", p, d], part(p, zb, me.yo, me.x, me.c), me.dev(dy=1), ok(zb, p)
             )
             s = slots["x2", p, d] = cp.slot()
-            out = part(p, zb, me.yo, me.x, me.c, 0, HALFQ)
+            out = part(p, zb, me.yo, me.x, me.c, 0, FIRST)
             cp.send(s, out, out, me.dev(dx=1), ok(zb, p))
             cp.wait_recv(
                 slots["x1", p, d], part(p, zb, me.y, me.xo, me.c), me.dev(dx=1), ok(zb, p)
             )
             s = slots["y2", p, d] = cp.slot()
-            out = part(p, zb, me.y, me.xo, me.c, HALFQ, HALFQ)
+            out = part(p, zb, me.y, me.xo, me.c, FIRST, SECOND)
             cp.send(s, out, out, me.dev(dy=1), ok(zb, p))
 
     def lane(p, zb, x, c):
@@ -224,11 +238,11 @@
         for d in (0, 1, 2, 3):
             zb = flip(me.z, d)
             cp.wait_recv(
-                slots["x2", p, d], part(p, zb, me.yo, me.xo, me.c, 0, HALFQ), me.dev(dx=1),
+                slots["x2", p, d], part(p, zb, me.yo, me.xo, me.c, 0, FIRST), me.dev(dx=1),
                 ok(zb, p),
             )
             cp.wait_recv(
-                slots["y2", p, d], part(p, zb, me.yo, me.xo, me.c, HALFQ, HALFQ), me.dev(dy=1),
+                slots["y2", p, d], part(p, zb, me.yo, me.xo, me.c, FIRST, SECOND), me.dev(dy=1),
                 ok(zb, p),
             )
             for h in (0, 1):
@@ -281,7 +295,16 @@
 
 
 SCATTER_COPIES = 3 * (4 * 2 + 4 * 4 + 3 + 3) + 8
+RING = 6
+ORDER = (3, 2, 1, 0)
 f32 = jnp.float32
+
+
+def guarded(cond, fn):
+    if cond is None:
+        fn()
+    else:
+        pl.when(cond)(fn)
 
 
 def add_rows(dst, srcs, n):
@@ -298,136 +321,160 @@
     lax.fori_loop(0, n // step, body, 0)
 
 
-def scatter_kernel(
-    partial, out, own, other, rx2, ry2, rx1, ry1, rz, final, tail, tail_in, tail_z,
-    send_sems, recv_sems, local_sems,
+def scatter_stages(
+    me, cp, partial, out, other, own, stage, rx2, ry2, rx1, ry1, rz, final, tail, tail_in, tail_z,
+    local_sems, credit,
 ):
-    me = Place()
-    cp = Copies(send_sems, recv_sems)
-    me.greet()
     slots = {}
-    order = (3, 2, 1, 0)
-
-    def guarded(cond, fn):
-        if cond is None:
-            fn()
-        else:
-            pl.when(cond)(fn)
-
-    def load(p, d, h):
+
+    def block(k):
+        p, d = 2 - k // 4, ORDER[k % 4]
         zb = flip(me.z, d)
-        return pltpu.make_async_copy(
-            partial.at[p, zb, :, pl.ds((2 * QUART * h + QUART * me.c), QUART)],
-            own.at[BASE[p] + zb, :, h], local_sems.at[(p * 4 + d) * 2 + h],
-        )
-
-    def s0(p):
-        for d in order:
+        return p, d, zb, ok(zb, p), k % RING
+
+    def exchange(p):
+        for d in ORDER:
             zb = flip(me.z, d)
             for h in (0, 1):
-                guarded(ok(zb, p), lambda d=d, h=h: load(p, d, h).start())
                 s = slots["c", p, d, h] = cp.slot()
+                view = pl.ds(2 * QUART * h + QUART * me.co, QUART)
                 cp.send(
-                    s, partial.at[p, zb, :, pl.ds((2 * QUART * h + QUART * me.co), QUART)],
-                    other.at[BASE[p] + zb, :, h], me.dev(dc=1), ok(zb, p),
+                    s, partial.at[p, zb, :, view], other.at[p, zb, :, h], me.dev(dc=1), ok(zb, p)
                 )
 
-    def s1(p):
-        for d in order:
-            zb = flip(me.z, d)
-            b = BASE[p] + zb
-            for h in (0, 1):
-                guarded(ok(zb, p), lambda d=d, h=h: load(p, d, h).wait())
-                cp.wait_recv(slots["c", p, d, h], other.at[b, :, h], me.dev(dc=1), ok(zb, p))
-
-            def fold(b=b):
-                def body(q, carry):
-                    add_rows(own.at[b, q // 2, q % 2], [own.at[b, q // 2, q % 2], other.at[b, q // 2, q % 2]], QUART)
-                    return carry
-                lax.fori_loop(0, 4, body, 0)
-            guarded(ok(zb, p), fold)
-            s = slots["x2", p, d] = cp.slot()
-            cp.send(s, own.at[b, me.yo, me.xo, pl.ds(0, HALFQ)], rx2.at[b], me.dev(dx=1), ok(zb, p))
-            s = slots["y2", p, d] = cp.slot()
-            cp.send(s, own.at[b, me.yo, me.xo, pl.ds(HALFQ, HALFQ)], ry2.at[b], me.dev(dy=1), ok(zb, p))
-
-    def s2(p):
-        for d in order:
-            zb = flip(me.z, d)
-            b = BASE[p] + zb
-            cp.wait_recv(slots["x2", p, d], rx2.at[b], me.dev(dx=1), ok(zb, p))
-            view = own.at[b, me.yo, me.x, pl.ds(0, HALFQ)]
-            guarded(ok(zb, p), lambda view=view, b=b: add_rows(view, [view, rx2.at[b]], HALFQ))
-            s = slots["y1", p, d] = cp.slot()
-            cp.send(s, own.at[b, me.yo, me.x], ry1.at[b], me.dev(dy=1), ok(zb, p))
-            cp.wait_recv(slots["y2", p, d], ry2.at[b], me.dev(dy=1), ok(zb, p))
-            view = own.at[b, me.y, me.xo, pl.ds(HALFQ, HALFQ)]
-            guarded(ok(zb, p), lambda view=view, b=b: add_rows(view, [view, ry2.at[b]], HALFQ))
-            s = slots["x1", p, d] = cp.slot()
-            cp.send(s, own.at[b, me.y, me.xo], rx1.at[b], me.dev(dx=1), ok(zb, p))
-
-    def s3(p):
-        for d in order:
-            zb = flip(me.z, d)
-            b = BASE[p] + zb
-            cp.wait_recv(slots["y1", p, d], ry1.at[b], me.dev(dy=1), ok(zb, p))
-            cp.wait_recv(slots["x1", p, d], rx1.at[b], me.dev(dx=1), ok(zb, p))
-            view = own.at[b, me.y, me.x]
-            guarded(
-                ok(zb, p),
-                lambda view=view, b=b: add_rows(view, [view, ry1.at[b], rx1.at[b]], QUART),
+    def loads(k):
+        p, d, zb, cond, slot = block(k)
+        copies = []
+        for h in (0, 1):
+            view = pl.ds(2 * QUART * h + QUART * me.c, QUART)
+            copies.append(
+                pltpu.make_async_copy(
+                    partial.at[p, zb, :, view], own.at[slot, :, h], local_sems.at[h]
+                )
             )
-            if d:
-                s = slots["z", p, d] = cp.slot()
-                cp.send(s, view, rz.at[p, d - 1], me.dev(dz=d), ok(zb, p))
-
-    def s4(p):
+            copies.append(
+                pltpu.make_async_copy(other.at[p, zb, :, h], stage.at[h], local_sems.at[2 + h])
+            )
+        return copies
+
+    def prefetch(k):
+        p, d, zb, cond, slot = block(k)
+        if k >= RING:
+            old = block(k - RING)
+            for name in ("x2", "y2", "x1", "y1", "z"):
+                if (name, old[0], old[1]) in slots:
+                    cp.wait_send(slots[name, old[0], old[1]])
+        for h in (0, 1):
+            cp.wait_recv(slots["c", p, d, h], other.at[p, zb, :, h], me.dev(dc=1), cond)
+
+        def go():
+            for copy in loads(k):
+                copy.start()
+
+        guarded(cond, go)
+
+    def fold(k):
+        p, d, zb, cond, slot = block(k)
+
+        def go():
+            for copy in loads(k):
+                copy.wait()
+
+            def body(q, carry):
+                y, h = q // 2, q % 2
+                add_rows(own.at[slot, y, h], [own.at[slot, y, h], stage.at[h, y]], QUART)
+                return carry
+
+            lax.fori_loop(0, 4, body, 0)
+
+        guarded(cond, go)
+        if k >= RING:
+            pl.semaphore_wait(credit.at[0], 1)
+            pl.semaphore_wait(credit.at[1], 1)
+        far = own.at[slot, me.yo, me.xo]
+        s = slots["x2", p, d] = cp.slot()
+        cp.send(s, far.at[pl.ds(0, FIRST)], rx2.at[slot], me.dev(dx=1), cond)
+        s = slots["y2", p, d] = cp.slot()
+        cp.send(s, far.at[pl.ds(FIRST, SECOND)], ry2.at[slot], me.dev(dy=1), cond)
+
+    def second(k):
+        p, d, zb, cond, slot = block(k)
+        cp.wait_recv(slots["x2", p, d], rx2.at[slot], me.dev(dx=1), cond)
+        view = own.at[slot, me.yo, me.x, pl.ds(0, FIRST)]
+        guarded(cond, lambda: add_rows(view, [view, rx2.at[slot]], FIRST))
+        s = slots["y1", p, d] = cp.slot()
+        cp.send(s, own.at[slot, me.yo, me.x], ry1.at[slot], me.dev(dy=1), cond)
+        cp.wait_recv(slots["y2", p, d], ry2.at[slot], me.dev(dy=1), cond)
+        view2 = own.at[slot, me.y, me.xo, pl.ds(FIRST, SECOND)]
+        guarded(cond, lambda: add_rows(view2, [view2, ry2.at[slot]], SECOND))
+        s = slots["x1", p, d] = cp.slot()
+        cp.send(s, own.at[slot, me.y, me.xo], rx1.at[slot], me.dev(dx=1), cond)
+
+    def third(k):
+        p, d, zb, cond, slot = block(k)
+        cp.wait_recv(slots["y1", p, d], ry1.at[slot], me.dev(dy=1), cond)
+        cp.wait_recv(slots["x1", p, d], rx1.at[slot], me.dev(dx=1), cond)
+        view = own.at[slot, me.y, me.x]
+        guarded(cond, lambda: add_rows(view, [view, ry1.at[slot], rx1.at[slot]], QUART))
+        if k + RING < 12:
+            pl.semaphore_signal(
+                credit.at[0], inc=1, device_id=me.dev(dx=1), device_id_type=MESH
+            )
+            pl.semaphore_signal(
+                credit.at[1], inc=1, device_id=me.dev(dy=1), device_id_type=MESH
+            )
+        if d:
+            s = slots["z", p, d] = cp.slot()
+            cp.send(s, view, rz.at[p, d - 1], me.dev(dz=d), cond)
+
+    def quarter(x, c):
+        return out.at[pl.ds(2 * QUART * x + QUART * c, QUART)]
+
+    def settle(p):
         mine = ok(me.z, p)
         for d in (1, 2, 3):
             cp.wait_recv(slots["z", p, d], rz.at[p, d - 1], me.dev(dz=d), mine)
-        view = own.at[BASE[p] + me.z, me.y, me.x]
+        view = own.at[(4 * (2 - p) + 3) % RING, me.y, me.x]
         guarded(
             mine,
             lambda: add_rows(final.at[p], [view, rz.at[p, 0], rz.at[p, 1], rz.at[p, 2]], QUART),
         )
         ox, oc = p // 2, p % 2
-        quarter = out.at[pl.ds((2 * QUART * me.x + QUART * me.c), QUART)]
         for dx, dc in ((1, 0), (0, 1), (1, 1)):
             x = me.xo if dx else me.x
             c = me.co if dc else me.c
             s = slots["f", p, dx, dc] = cp.slot()
             cond = both(jnp.logical_and(x == ox, c == oc), mine)
-            cp.send(s, final.at[p], quarter, me.dev(dx=dx, dc=dc), cond)
+            cp.send(s, final.at[p], quarter(me.x, me.c), me.dev(dx=dx, dc=dc), cond)
 
         @pl.when(both(me.o == p, mine))
         def _():
-            pltpu.make_async_copy(final.at[p], quarter, local_sems.at[24]).start()
-
-    def s5(p):
+            pltpu.make_async_copy(final.at[p], quarter(me.x, me.c), local_sems.at[4]).start()
+
+    def finish(p):
         mine = both(me.o == p, ok(me.z, p))
         for dx, dc in ((1, 0), (0, 1), (1, 1)):
             x = me.xo if dx else me.x
             c = me.co if dc else me.c
-            cp.wait_recv(
-                slots["f", p, dx, dc], out.at[pl.ds((2 * QUART * x + QUART * c), QUART)],
-                me.dev(dx=dx, dc=dc), mine,
-            )
+            cp.wait_recv(slots["f", p, dx, dc], quarter(x, c), me.dev(dx=dx, dc=dc), mine)
 
         @pl.when(mine)
         def _():
-            quarter = out.at[pl.ds((2 * QUART * me.x + QUART * me.c), QUART)]
-            pltpu.make_async_copy(final.at[p], quarter, local_sems.at[24]).wait()
-
-    tail_load = pltpu.make_async_copy(
-        partial.at[:, :, :, pl.ds(MAIN, TAIL)], tail, local_sems.at[25]
-    )
-    tail_load.start()
+            pltpu.make_async_copy(final.at[p], quarter(me.x, me.c), local_sems.at[4]).wait()
+
+    def tail_load():
+        return pltpu.make_async_copy(
+            partial.at[:, :, :, pl.ds(MAIN, TAIL)], tail, local_sems.at[5]
+        )
 
     def tail_add(o, zb, yb, srcs):
         add_rows(tail.at[o, zb, yb], [tail.at[o, zb, yb]] + srcs, TAIL)
 
+    def t0():
+        tail_load().start()
+
     def t1():
-        tail_load.wait()
+        tail_load().wait()
         for h in (0, 1):
             s = slots["tc", h] = cp.slot()
             cp.send(s, tail.at[2 * h + me.co], tail_in.at[h], me.dev(dc=1))
@@ -436,7 +483,7 @@
         for h in (0, 1):
             cp.wait_recv(slots["tc", h], tail_in.at[h], me.dev(dc=1))
 
-            def body(q, carry, h=h):
+            def body(q, carry):
                 tail_add(2 * h + me.c, q // 2, q % 2, [tail_in.at[h, q // 2, q % 2]])
                 return carry
             lax.fori_loop(0, 8, body, 0)
@@ -469,44 +516,34 @@
             cp.wait_recv(slots["tz", d], tail_z.at[d - 1], me.dev(dz=d))
         tail_add(me.o, me.z, me.y, [tail_z.at[0], tail_z.at[1], tail_z.at[2]])
         copy = pltpu.make_async_copy(
-            tail.at[me.o, me.z, me.y], out.at[pl.ds(MAIN, TAIL)], local_sems.at[25]
+            tail.at[me.o, me.z, me.y], out.at[pl.ds(MAIN, TAIL)], local_sems.at[5]
         )
         copy.start()
         copy.wait()
 
-    s0(2); s0(1); s0(0); s1(2); t1(); s1(1); s2(2); t2(); s1(0); s3(2); s2(1); t3(); s4(2)
-    s2(0); s3(1); t4(); s4(1); s3(0); t5(); s4(0); s5(2); s5(1); s5(0)
-    cp.drain()
-
-
-def scatter_grads_kernel(partial):
+    return dict(
+        exchange=exchange, prefetch=prefetch, fold=fold, second=second, third=third,
+        settle=settle, finish=finish, tails=(t0, t1, t2, t3, t4, t5),
+    )
+
+
+def scatter_scratch():
     bf = jnp.bfloat16
-    return pl.pallas_call(
-        scatter_kernel,
-        out_shape=jax.ShapeDtypeStruct((GROUPS8, 8, D), bf),
-        in_specs=[pl.BlockSpec(memory_space=pl.ANY)],
-        out_specs=pl.BlockSpec(memory_space=pl.ANY),
-        scratch_shapes=[
-            pltpu.VMEM((11, 2, 2, QUART, 8, D), bf),
-            pltpu.VMEM((11, 2, 2, QUART, 8, D), bf),
-            pltpu.VMEM((11, HALFQ, 8, D), bf),
-            pltpu.VMEM((11, HALFQ, 8, D), bf),
-            pltpu.VMEM((11, QUART, 8, D), bf),
-            pltpu.VMEM((11, QUART, 8, D), bf),
-            pltpu.VMEM((3, 3, QUART, 8, D), bf),
-            pltpu.VMEM((3, QUART, 8, D), bf),
-            pltpu.VMEM((4, 4, 2, TAIL, 8, D), bf),
-            pltpu.VMEM((4, 4, 2, TAIL, 8, D), bf),
-            pltpu.VMEM((3, TAIL, 8, D), bf),
-            pltpu.SemaphoreType.DMA((SCATTER_COPIES,)),
-            pltpu.SemaphoreType.DMA((SCATTER_COPIES,)),
-            pltpu.SemaphoreType.DMA((26,)),
-        ],
-        compiler_params=pltpu.CompilerParams(
-            collective_id=1, has_side_effects=True, vmem_limit_bytes=60 * 2**20
-        ),
-        name="scatter_grads",
-    )(partial)
+    return [
+        pltpu.VMEM((RING, 2, 2, QUART, 8, D), bf),
+        pltpu.VMEM((2, 2, QUART, 8, D), bf),
+        pltpu.VMEM((RING, FIRST, 8, D), bf),
+        pltpu.VMEM((RING, SECOND, 8, D), bf),
+        pltpu.VMEM((RING, QUART, 8, D), bf),
+        pltpu.VMEM((RING, QUART, 8, D), bf),
+        pltpu.VMEM((3, 3, QUART, 8, D), bf),
+        pltpu.VMEM((3, QUART, 8, D), bf),
+        pltpu.VMEM((4, 4, 2, TAIL, 8, D), bf),
+        pltpu.VMEM((4, 4, 2, TAIL, 8, D), bf),
+        pltpu.VMEM((3, TAIL, 8, D), bf),
+        pltpu.SemaphoreType.DMA((6,)),
+        pltpu.SemaphoreType.REGULAR((2,)),
+    ]
 
 
 bf16 = jnp.bfloat16
@@ -732,7 +769,9 @@
             t = jnp.tanh(ROOT * (v + CUBIC * sq * v))
             half = 0.5 * (1.0 + t)
             active[b, rows] = (v * half).astype(bf16)
-            slope[b, rows] = half + (0.5 * ROOT) * v * (1.0 - t * t) * (1.0 + 3.0 * CUBIC * sq)
+            rise = half + (0.5 * ROOT) * v * (1.0 - t * t) * (1.0 + 3.0 * CUBIC * sq)
+            for q in range(9):
+                slope[b, q, rows] = rise[:, 128 * q : 128 * q + 128]
 
         over_columns(columns, gelu)
         return carry
@@ -838,7 +877,7 @@
         shape((rows, D), f32),
         shape((rows, D), bf16),
         shape((4, rows, D), bf16),
-        shape((4, rows, D), f32),
+        shape((4, 9, rows, 128), f32),
         shape((rows, D), bf16),
         shape((columns, D), f32),
     ]
@@ -861,7 +900,7 @@
         pltpu.VMEM((rows, D), f32),
         pltpu.VMEM((3, rows, D), bf16),
         pltpu.VMEM((4, rows, D), bf16),
-        pltpu.VMEM((4, rows, D), f32),
+        pltpu.VMEM((4, 9, rows, 128), f32),
         pltpu.SemaphoreType.DMA((20,)),
     ]
 
@@ -906,26 +945,38 @@
     )(shard, partial, chosen, base, tokens, upstream, b_qkv, b_proj, b_up, b_down)
 
 
-def backward_kernel(
-    weights, natural, tokens, upstream, mods, input_att, proj, attended, branch, input_mlp, active,
-    slope, grad_out,
+UP_RUNS = ((0, 256), (256, 256), (512, 256), (768, 256), (1024, 128))
+QKV_RUNS = ((0, 384), (384, 384), (768, 384))
+
+
+def backward_body(
+    weights, natural, active, slope, tokens, upstream, mods, input_att, proj, attended, branch,
+    input_mlp, grad_out,
     grads, input_grad, grad_mods, bias_sums,
-    held, woven, spread, flat, grad_hidden, middle_grad, grad_branch, grad_att, grad_proj, acc,
-    copy_sems,
+    held, woven, spread, acts, grad_hidden, grad_branch, grad_att, acc, copy_sems, tick,
 ):
     columns = mods.shape[1]
-
-    def fetch(source, first, slot):
-        return pltpu.make_async_copy(source.at[first], held.at[slot], copy_sems.at[slot])
+    row_count = columns * FRAMES
+
+    def fetch(first, slot):
+        return pltpu.make_async_copy(natural.at[first], held.at[slot], copy_sems.at[slot])
 
     def flat_mat(first, slot):
         return pltpu.make_async_copy(
             weights.at[pl.ds(first, MATS)], held.at[slot], copy_sems.at[slot]
         )
 
-    def store_flat(first, slot):
+    def stream(b, slot):
+        at = pl.ds(pl.multiple_of(slot * row_count, row_count), row_count)
+        return (
+            flat_mat(AT_DOWN + b * MATS, slot),
+            pltpu.make_async_copy(active.at[b], acts.at[slot], copy_sems.at[2 + slot]),
+            pltpu.make_async_copy(slope.at[b], spread.at[:, at], copy_sems.at[4 + slot]),
+        )
+
+    def store(first, offset, groups, n):
         return pltpu.make_async_copy(
-            flat.at[slot], grads.at[pl.ds(first, MATS)], copy_sems.at[2 + slot]
+            woven.at[pl.ds(offset, groups)], grads.at[pl.ds(first, groups)], copy_sems.at[6 + n]
         )
 
     bias_sums[...] = jnp.zeros_like(bias_sums)
@@ -933,85 +984,92 @@
     def add_bias(row, values):
         bias_sums[pl.ds(row, 1)] += jnp.sum(values.astype(f32), axis=0, keepdims=True)
 
-    flat_mat(AT_DOWN, 0).start()
+    def outer(first, left, right, pending):
+        for r in range(3):
+            part = tn_dot(left[:, 384 * r : 384 * r + 384], right[...])
+            if pending is not None:
+                pending(r)
+            woven[pl.ds(48 * r, 48)] = part.reshape(48, 8, D).astype(bf16)
+            store(first + 48 * r, 48 * r, 48, r).start()
+
+    for copy in stream(0, 0):
+        copy.start()
 
     def down(b, carry):
         slot = lax.rem(b, 2)
-        flat_mat(AT_DOWN + b * MATS, slot).wait()
+        for copy in stream(b, slot):
+            copy.wait()
 
         @pl.when(b < 3)
         def _():
-            flat_mat(AT_DOWN + (b + 1) * MATS, 1 - slot).start()
+            for copy in stream(b + 1, 1 - slot):
+                copy.start()
 
         acc[...] = nt_dot(grad_out[...], square(held.at[slot]))
 
         def through(c, rows, at):
-            grad = (acc[rows] * slope[b, rows]).astype(bf16)
+            there = pl.ds(pl.multiple_of(slot * row_count + c * FRAMES, FRAMES), FRAMES)
+            rise = jnp.concatenate([spread[q, there] for q in range(9)], axis=1)
+            grad = (acc[rows] * rise).astype(bf16)
             grad_hidden[b, rows] = grad
             add_bias(5 + b, grad)
 
         over_columns(columns, through)
-
-        @pl.when(b >= 2)
-        def _():
-            store_flat(AT_DOWN + (b - 2) * MATS, slot).wait()
-
-        flat[slot] = tn_dot(active[b], grad_out[...]).reshape(MATS, 8, D).astype(bf16)
-        store_flat(AT_DOWN + b * MATS, slot).start()
+        first = AT_DOWN + b * MATS
+
+        def pending(r):
+            @pl.when(b > 0)
+            def _():
+                store(first - MATS + 48 * r, 48 * r, 48, r).wait()
+
+        outer(first, acts.at[slot], grad_out, pending)
         return carry
 
     lax.fori_loop(0, 4, down, 0)
-    fetch(natural, 3, 0).start()
+    fetch(3, 0).start()
 
     def down_bias(c, rows, at):
         add_bias(4, grad_out[rows])
 
     over_columns(columns, down_bias)
-
-    def weave(first, ways, left, right_of):
-        groups = 48 * ways
-
-        def store(k):
-            return pltpu.make_async_copy(
-                woven.at[pl.ds(0, groups)], grads.at[pl.ds(first + k * groups, groups)],
-                copy_sems.at[4],
-            )
-
-        for k in range(3):
+    for r in range(3):
+        store(AT_DOWN + 3 * MATS + 48 * r, 48 * r, 48, r).wait()
+    tick("down")
+
+    def weave(first, ways, left, right, runs, name):
+        before = None
+        for k, (start, count) in enumerate(runs):
             for w in range(ways):
-                part = tn_dot(left[:, 384 * k : 384 * k + 384], right_of(w))
+                part = tn_dot(left[:, start : start + count], right[w])
                 for q in range(9):
-                    spread[q, pl.ds(w, 384, stride=ways), :] = part[:, 128 * q : 128 * q + 128]
-            if k:
-                store(k - 1).wait()
+                    spread[q, pl.ds(w, count, stride=ways), :] = part[:, 128 * q : 128 * q + 128]
+            if before is not None:
+                before.wait()
 
             def pack(j, carry):
                 for q in range(9):
-                    block = spread[q, pl.ds(pl.multiple_of(j * 128, 128), 128), :]
-                    woven[pl.ds(j * 16, 16), :, 128 * q : 128 * q + 128] = block.reshape(
+                    lines = spread[q, pl.ds(pl.multiple_of(j * 128, 128), 128), :]
+                    woven[pl.ds(j * 16, 16), :, 128 * q : 128 * q + 128] = lines.reshape(
                         16, 8, 128
                     ).astype(bf16)
                 return carry
 
+            groups = count * ways // 8
             lax.fori_loop(0, groups // 16, pack, 0)
-            store(k).start()
-        return lambda: store(2).wait()
-
-    up_done = weave(AT_UP, 4, input_mlp, lambda w: grad_hidden[w])
+            before = store(first + start * ways // 8, 0, groups, 0)
+            before.start()
+            tick(name, k)
+        before.wait()
+
+    weave(AT_UP, 4, input_mlp, grad_hidden, UP_RUNS, "up run")
+    tick("up")
     acc[...] = jnp.zeros_like(acc)
-
-    def up(b, carry):
-        slot = lax.rem(b, 2)
-        fetch(natural, 3 + b, slot).wait()
-
-        @pl.when(b < 3)
-        def _():
-            fetch(natural, 4 + b, 1 - slot).start()
-
-        acc[...] += nt_dot(grad_hidden[b], square(held.at[slot]))
-        return carry
-
-    lax.fori_loop(0, 4, up, 0)
+    for b in range(4):
+        fetch(3 + b, b % 2).wait()
+        if b < 3:
+            fetch(4 + b, 1 - b % 2).start()
+        acc[...] += nt_dot(grad_hidden[b], square(held.at[b % 2]))
+        tick("up input", b)
     flat_mat(AT_PROJ, 0).start()
 
     def second_norm_back(c, rows, at):
@@ -1023,22 +1081,22 @@
         grad_mods[4, at] = jnp.sum(grad * normed, axis=0, keepdims=True)
         grad_block = jnp.where(mods[6, at] > 0.5, upstream[rows].astype(f32), 0.0)
         grad_middle = grad_block + norm_rows_back(grad * (1.0 + mods[4, at]), normed, inverse)
-        middle_grad[rows] = grad_middle
+        input_grad[rows] = grad_middle
         grad_mods[2, at] = jnp.sum(grad_middle * br, axis=0, keepdims=True)
         grad = (grad_middle * gate).astype(bf16)
         grad_branch[rows] = grad
         add_bias(3, grad)
 
     over_columns(columns, second_norm_back)
-    store_flat(AT_DOWN + 2 * MATS, 0).wait()
-    store_flat(AT_DOWN + 3 * MATS, 1).wait()
-    flat[0] = tn_dot(attended[...], grad_branch[...]).reshape(MATS, 8, D).astype(bf16)
-    store_flat(AT_PROJ, 0).start()
+    tick("norm")
+    outer(AT_PROJ, attended, grad_branch, None)
     flat_mat(AT_PROJ, 0).wait()
     grad_att[...] = nt_dot(grad_branch[...], square(held.at[0])).astype(bf16)
-    fetch(natural, 0, 0).start()
+    fetch(0, 0).start()
+    for r in range(3):
+        store(AT_PROJ + 48 * r, 48 * r, 48, r).wait()
+    tick("proj")
     inside = same_column()
-    top = pl.ds(0, 128)
 
     def attend_back(g, carry):
         rows = pl.ds(pl.multiple_of(g * 128, 128), 128)
@@ -1059,77 +1117,240 @@
         for p in range(3):
             scale = SCORE_SCALE if p < 2 else 1.0
             grad = (acc[pl.ds(p * 128, 128)] * scale).astype(bf16)
-            grad_proj[p, rows] = grad
+            grad_hidden[p, rows] = grad
             add_bias(p, grad)
         return carry
 
-    lax.fori_loop(0, columns * FRAMES // 128, attend_back, 0)
-    up_done()
-    qkv_done = weave(0, 3, input_att, lambda w: grad_proj[w])
+    for g in range(row_count // 128):
+        lax.fori_loop(g, g + 1, attend_back, 0)
+        tick("attend", g)
+    weave(0, 3, input_att, grad_hidden, QKV_RUNS, "qkv run")
+    tick("qkv")
     acc[...] = jnp.zeros_like(acc)
-
-    def qkv(p, carry):
-        slot = lax.rem(p, 2)
-        fetch(natural, p, slot).wait()
-
-        @pl.when(p < 2)
-        def _():
-            fetch(natural, p + 1, 1 - slot).start()
-
-        acc[...] += nt_dot(grad_proj[p], square(held.at[slot]))
-        return carry
-
-    lax.fori_loop(0, 3, qkv, 0)
+    for p in range(3):
+        fetch(p, p % 2).wait()
+        if p < 2:
+            fetch(p + 1, 1 - p % 2).start()
+        acc[...] += nt_dot(grad_hidden[p], square(held.at[p % 2]))
+        tick("qkv input", p)
 
     def first_norm_back(c, rows, at):
         normed, inverse = norm_rows(tokens[rows].astype(f32))
         grad = acc[rows]
         grad_mods[0, at] = jnp.sum(grad, axis=0, keepdims=True)
         grad_mods[1, at] = jnp.sum(grad * normed, axis=0, keepdims=True)
-        grad_states = middle_grad[rows] + norm_rows_back(
+        grad_states = input_grad[rows] + norm_rows_back(
             grad * (1.0 + mods[1, at]), normed, inverse
         )
         up_rows = upstream[rows].astype(f32)
         input_grad[rows] = jnp.where(mods[6, at] > 0.5, grad_states, up_rows)
 
     over_columns(columns, first_norm_back)
-    store_flat(AT_PROJ, 0).wait()
-    qkv_done()
-
-
-def backward(weights, natural, *operands):
-    tokens, mods = operands[0], operands[2]
-    rows = tokens.shape[0]
-    columns = mods.shape[1]
-    vmem = pl.BlockSpec(memory_space=pltpu.VMEM)
-    hbm = pl.BlockSpec(memory_space=pl.ANY)
+    tick("end")
+
+
+def backward_kernel(*refs):
+    backward_body(*refs, lambda name, step=0: None)
+
+
+def backward_scatter_kernel(*refs):
+    (
+        weights, natural, active, slope, tokens, upstream, mods, input_att, proj, attended, branch,
+        input_mlp, grad_out, grad_gate, member,
+        out, grads, other, input_grad, total_small,
+        grad_mods, bias_sums, held, woven, spread, acts, grad_hidden, grad_branch, grad_att, acc, copy_sems,
+        own, stage, rx2, ry2, rx1, ry1, rz, final, tail, tail_in, tail_z, local_sems, credit,
+        small, sums, send_sems, recv_sems,
+    ) = refs
+    me = Place()
+    cp = Copies(send_sems, recv_sems)
+    me.greet()
+    st = scatter_stages(
+        me, cp, grads, out, other, own, stage, rx2, ry2, rx1, ry1, rz, final, tail, tail_in,
+        tail_z, local_sems, credit,
+    )
+    t0, t1, t2, t3, t4, t5 = st["tails"]
+    m1, m2, m3, m4, total = sum_stages(me, cp, small, sums)
+    groups = member.shape[0]
+
+    def move(t):
+        if t < 12:
+            st["fold"](t)
+            if t % 4 != 3:
+                st["prefetch"](t + 1)
+        if 0 <= t - 1 < 12:
+            st["second"](t - 1)
+        if 0 <= t - 2 < 12:
+            st["third"](t - 2)
+
+    def tick(name, step=0):
+        if name == "down":
+            st["exchange"](2)
+            st["prefetch"](0)
+        elif name == "up run" and step in (0, 2, 4):
+            move(step // 2)
+        elif name == "up":
+            st["exchange"](1)
+        elif name == "up input" and step == 1:
+            move(3)
+            st["prefetch"](4)
+        elif name == "norm":
+            move(4)
+        elif name == "attend":
+            move(5 + step)
+            if step == 1:
+                st["settle"](2)
+        elif name == "qkv":
+            st["exchange"](0)
+            st["prefetch"](8)
+            t0()
+        elif name == "qkv input" and step == 0:
+            move(8)
+            t1()
+        elif name == "qkv input" and step == 2:
+            t2()
+        elif name == "end":
+            for n in range(6):
+                plane = grad_mods[n] if n < 5 else grad_gate[...]
+                small[pl.ds(n * groups, groups)] = exact(
+                    member[...], plane, (((1,), (0,)), ((), ()))
+                )
+            small[pl.ds(6 * groups, 9)] = bias_sums[pl.ds(0, 9)]
+            small[pl.ds(6 * groups + 9, small.shape[0] - 6 * groups - 9)] = jnp.zeros(
+                (small.shape[0] - 6 * groups - 9, D), f32
+            )
+            m1()
+            move(9)
+            t3()
+            m2()
+            move(10)
+            t4()
+            m3()
+            st["settle"](1)
+            move(11)
+            t5()
+            m4()
+            move(12)
+            total_small[...] = total()
+            move(13)
+            st["settle"](0)
+            for p in (2, 1, 0):
+                st["finish"](p)
+            cp.drain()
+
+    backward_body(
+        weights, natural, active, slope, tokens, upstream, mods, input_att, proj, attended, branch,
+        input_mlp, grad_out,
+        grads.reshape(4 * 4 * 2 * GROUPS8, 8, D), input_grad, grad_mods, bias_sums,
+        held, woven, spread, acts, grad_hidden, grad_branch, grad_att, acc, copy_sems,
+        tick,
+    )
+
+
+def backward_shapes(rows, columns):
     shape = jax.ShapeDtypeStruct
+    return [
+        shape((rows, D), f32),
+        shape((5, columns, D), f32),
+        shape((16, D), f32),
+    ]
+
+
+def backward_scratch(rows):
+    return [
+        pltpu.VMEM((2, MATS, 8, D), bf16),
+        pltpu.VMEM((MATS, 8, D), bf16),
+        pltpu.VMEM((9, D, 128), f32),
+        pltpu.VMEM((2, rows, D), bf16),
+        pltpu.VMEM((4, rows, D), bf16),
+        pltpu.VMEM((rows, D), bf16),
+        pltpu.VMEM((rows, D), bf16),
+        pltpu.VMEM((rows, D), f32),
+        pltpu.SemaphoreType.DMA((9,)),
+    ]
+
+
+def backward(*operands):
+    rows, columns = operands[4].shape[0], operands[6].shape[1]
     return pl.pallas_call(
         backward_kernel,
-        out_shape=[
-            shape((32 * UNITS // 8, 8, D), bf16),
-            shape((rows, D), f32),
-            shape((5, columns, D), f32),
-            shape((16, D), f32),
-        ],
-        in_specs=[hbm, hbm] + [vmem] * len(operands),
-        out_specs=[hbm] + [vmem] * 3,
-        scratch_shapes=[
-            pltpu.VMEM((2, MATS, 8, D), bf16),
-            pltpu.VMEM((192, 8, D), bf16),
-            pltpu.VMEM((9, 1536, 128), f32),
-            pltpu.VMEM((2, MATS, 8, D), bf16),
-            pltpu.VMEM((4, rows, D), bf16),
-            pltpu.VMEM((rows, D), f32),
-            pltpu.VMEM((rows, D), bf16),
-            pltpu.VMEM((rows, D), bf16),
-            pltpu.VMEM((3, rows, D), bf16),
-            pltpu.VMEM((rows, D), f32),
-            pltpu.SemaphoreType.DMA((5,)),
-        ],
+        out_shape=[jax.ShapeDtypeStruct((32 * UNITS // 8, 8, D), bf16)]
+        + backward_shapes(rows, columns),
+        in_specs=[HBM_SPEC] * 4 + [VMEM_SPEC] * 9,
+        out_specs=[HBM_SPEC] + [VMEM_SPEC] * 3,
+        scratch_shapes=backward_scratch(rows),
         compiler_params=pltpu.CompilerParams(vmem_limit_bytes=62 * 2**20),
         name="block_backward",
-    )(weights, natural, *operands)
+    )(*operands)
+
+
+def backward_scatter(operands, grad_gate, member):
+    rows, columns = operands[4].shape[0], operands[6].shape[1]
+    small = small_rows(member.shape[0])
+    copies = SCATTER_COPIES + SUM_COPIES
+    shape = jax.ShapeDtypeStruct
+    input_grad, grad_mods, bias_sums = backward_shapes(rows, columns)
+    return pl.pallas_call(
+        backward_scatter_kernel,
+        out_shape=[
+            shape((GROUPS8, 8, D), bf16),
+            shape((4, 4, 2, GROUPS8, 8, D), bf16),
+            shape((3, 4, 2, 2, QUART, 8, D), bf16),
+            input_grad,
+            shape((small, D), f32),
+        ],
+        in_specs=[HBM_SPEC] * 4 + [VMEM_SPEC] * 11,
+        out_specs=[HBM_SPEC] * 3 + [VMEM_SPEC] * 2,
+        scratch_shapes=[
+            pltpu.VMEM(grad_mods.shape, f32),
+            pltpu.VMEM(bias_sums.shape, f32),
+        ]
+        + backward_scratch(rows)
+        + scatter_scratch()
+        + [
+            pltpu.VMEM((small, D), f32),
+            pltpu.VMEM((SUM_SLOTS, small, D), f32),
+            pltpu.SemaphoreType.DMA((copies,)),
+            pltpu.SemaphoreType.DMA((copies,)),
+        ],
+        compiler_params=pltpu.CompilerParams(
+            collective_id=1, has_side_effects=True, vmem_limit_bytes=63 * 2**20
+        ),
+        name="backward_scatter",
+    )(*operands, grad_gate, member)
+
+
+def small_rows(groups):
+    return -(-(6 * groups + 9) // 8) * 8
+
+
+def sum_kernel(mine, out, sums, send_sems, recv_sems):
+    me = Place()
+    cp = Copies(send_sems, recv_sems)
+    me.greet()
+    m1, m2, m3, m4, total = sum_stages(me, cp, mine, sums)
+    m1()
+    m2()
+    m3()
+    m4()
+    out[...] = total()
+    cp.drain()
+
+
+def sum_everywhere(values):
+    return pl.pallas_call(
+        sum_kernel,
+        out_shape=jax.ShapeDtypeStruct(values.shape, f32),
+        in_specs=[VMEM_SPEC],
+        out_specs=VMEM_SPEC,
+        scratch_shapes=[
+            pltpu.VMEM((SUM_SLOTS, *values.shape), f32),
+            pltpu.SemaphoreType.DMA((SUM_COPIES,)),
+            pltpu.SemaphoreType.DMA((SUM_COPIES,)),
+        ],
+        compiler_params=pltpu.CompilerParams(collective_id=2, has_side_effects=True),
+        name="sum_everywhere",
+    )(values)
 
 
 def gather_blocks(shard_low):
@@ -1137,13 +1358,10 @@
     return whole.reshape(-1, 8, D)
 
 
-def scatter_blocks(grads, units, kernels):
+def scatter_blocks(grads, units):
     axes = ("outer", "inner")
-    if not kernels:
-        whole = grads.reshape(-1, D)[: lax.axis_size(axes) * units].astype(f32)
-        return lax.psum_scatter(whole, axes, scatter_dimension=0, tiled=True)
-    summed = scatter_grads_kernel(grads.reshape(4, 4, 2, GROUPS8, 8, D))
-    return summed.reshape(UNITS, D).astype(f32)
+    whole = grads.reshape(-1, D)[: lax.axis_size(axes) * units].astype(f32)
+    return lax.psum_scatter(whole, axes, scatter_dimension=0, tiled=True)
 
 
 def split_bias(vector):
@@ -1239,16 +1457,24 @@
         block_out, natural, input_att, proj, attended, branch, input_mlp, active, slope, grad_out,
         grad_gate,
     ) = saved
-    grads, input_grad, grad_mods, bias_sums = backward(
-        flat, natural, tokens, output_grad, mods, input_att, proj, attended, branch, input_mlp,
-        active, slope, grad_out,
+    operands = (
+        flat, natural, active, slope, tokens, output_grad, mods, input_att, proj, attended, branch,
+        input_mlp, grad_out,
     )
-    grad_mods = jnp.concatenate([grad_mods, grad_gate[None]])
-    mods_local = exact(membership, grad_mods, (((0,), (1,)), ((), ()))).reshape(groups, 6 * D)
+    if kernels:
+        shard_sum, _, _, input_grad, small = backward_scatter(operands, grad_gate, membership.T)
+        block_shard = shard_sum.reshape(units, D).astype(f32)
+        grad_mods_all = small[: 6 * groups].reshape(6, groups, D)
+        bias_sums = small[6 * groups : 6 * groups + 9]
+    else:
+        grads, input_grad, grad_mods, bias_sums = backward(*operands)
+        grad_mods = jnp.concatenate([grad_mods, grad_gate[None]])
+        mods_local = exact(membership, grad_mods, (((0,), (1,)), ((), ())))
+        bias_sums, grad_mods_all = lax.psum((bias_sums, mods_local.transpose(1, 0, 2)), axes)
+        block_shard = scatter_blocks(grads, units)
+    grad_mods_all = grad_mods_all.transpose(1, 0, 2).reshape(groups, 6 * D)
     bias_head = jnp.concatenate([bias_sums[:1], bias_sums[2:4], bias_sums[5:9], bias_sums[4:5]])
-    bias_head, grad_mods_all = lax.psum((bias_head.reshape(-1), mods_local), axes)
-    first_sum = jnp.concatenate([bias_head, jnp.sum(grad_mods_all, axis=0)])
-    block_shard = scatter_blocks(grads, units, kernels)
+    first_sum = jnp.concatenate([bias_head.reshape(-1), jnp.sum(grad_mods_all, axis=0)])
     mods_parts = grad_mods_all.reshape(groups * 6, D)
     ada_shard = exact(selector, mods_parts, (((1,), (0,)), ((), ())))
     unit = first_unit + jnp.arange(units, dtype=jnp.int32)
@@ -1259,7 +1485,13 @@
     start = jnp.clip(first_unit - BLOCK_UNITS + units, 0, 6 * D + units)
     spread = lax.dynamic_update_slice(spread, products.T, (jnp.int32(0), start))
     grad_soft = jnp.sum(spread[:, units : units + 6 * D].reshape(groups, D, 6), axis=2)
-    square_sum, grad_soft = lax.psum((jnp.sum(grad_units * grad_units), grad_soft), axes)
+    square_sum = jnp.sum(grad_units * grad_units)
+    if kernels:
+        rows = jnp.concatenate([grad_soft, jnp.full((8 - groups % 8, D), square_sum / D, f32)])
+        rows = sum_everywhere(rows)
+        grad_soft, square_sum = rows[:groups], jnp.sum(rows[groups])
+    else:
+        square_sum, grad_soft = lax.psum((square_sum, grad_soft), axes)
     silu_out, silu_back = jax.vjp(jax.nn.silu, conditioning)
     second_sum = silu_back(grad_soft)[0]
     grad_shard = grad_units.reshape(-1)

time: 581 us -> 501 us (0.86)
  blocking collectives: 38.9 us -> 0 us
  Pallas kernels: 470 us -> 439 us
  between operations: 17.3 us -> 4.65 us
    psum x1 -> x0, blocking collectives: 38.9 us -> none  [on_device(): lax.psum((jnp.sum(grad_units * grad_units), grad_soft), axes)]
    pallas_call x2, Pallas kernels: 267 us -> 245 us  [the longest x1 223 us: backward_scatter(): pl.pallas_call(backward_scatter_kernel, out_shape=[shape((GROUPS8, 8, D),...]
    pallas_call x1, Pallas kernels: 203 us -> 194 us  [gather_forward(): pl.pallas_call(gather_forward_kernel, out_shape=[jax.ShapeDtypeStruct((4,...]
  transfers between devices with their start and end apart: 1 -> 0, of which waited for: 0 -> 0; matrix products, arithmetic and copies ran while one was open for 0% -> 0% of each run, Pallas kernels for 29% -> 0%
where the time goes in v4:
time: 501 us; the launch traced here: 495 us
  Pallas kernels  439 us (88%)
  local copies, waits for them, and re-layouts  23.8 us (5%)
  other arithmetic  18 us (4%)
  matrix products  9.03 us (2%)
    pallas_call x1, Pallas kernels, backward_scatter(): pl.pallas_call(backward_scatter_kernel, out_shape=[shape((GROUPS8, 8, D),...  223 us
    pallas_call x1, Pallas kernels, gather_forward(): pl.pallas_call(gather_forward_kernel, out_shape=[jax.ShapeDtypeStruct((4,...  194 us
    pallas_call x1, Pallas kernels, sum_everywhere(): pl.pallas_call(sum_kernel, out_shape=jax.ShapeDtypeStruct(values.shape, f...  21.4 us

profile of v4, /device:TPU:0, one launch (start us, length us, event | category | flops | bytes accessed | tf_op | source)
XLA Modules:
  0.0 494.6 jit_solution(9252726972630452706)
XLA Ops:
  0.6 0.0 copy-start.5
  0.7 2.0 convert_element_type.67
  2.7 2.8 convert_element_type.68.shard
  5.5 0.0 copy-done.5
  5.5 0.5 broadcast_in_dim.17
  6.1 0.0 copy-start.8
  6.1 1.1 reshape.182
  7.1 0.0 slice-start
  7.1 0.1 fusion.10
  7.3 0.0 copy-start.9
  7.3 0.0 copy-start.4
  7.3 1.7 convert_element_type.74
  9.0 0.0 copy-start
  9.0 1.1 copy-done
  10.1 1.0 fusion.29.partial
  11.1 0.0 copy-done.8
  11.1 0.1 broadcast_multiply_fusion.2
  11.2 0.1 mul.162
  11.3 0.1 copy.22
  11.4 0.6 pad.10.chosen
  12.1 0.0 slice-done
  12.1 0.0 copy-done.9
  12.1 0.1 convolution_bitcast_fusion.2
  12.2 0.1 pad.19.clone
  12.3 1.0 pad_maximum_fusion.base
  13.3 0.0 copy-done.4
  13.4 0.1 pad.16.clone
  13.4 0.7 pad_maximum_fusion.2.b_qkv
  14.1 0.6 broadcast_in_dim.20.b_proj
  14.7 0.6 slice.73.b_up
  15.4 0.6 broadcast_in_dim.21.b_down
  15.9 194.3 %gather_forward.1 = (bf16[4,4,2,81,8,1152]{5,4,3,2,1,0:T(8,128)(2,1)}, f32[7,24,1152]{2,1,0:T(8,128)}, f32[384,1152]{1,0:T(8,128)}, bf16[7,144,8,1152]{3,2,1,0:T...) custom-call(bf16[81,8,1152]{2,1,0:T(8,128)(2,1)} %convert_element_ty, ...), custom_call_target="tpu_custom_call" | custom-call | tf_op jit(solution)/shard_map/gather_forward/pallas_call | solution.py:925
  210.3 0.6 fusion.19.refs_14_
  210.8 223.4 %backward_scatter.1 = (bf16[81,8,1152]{2,1,0:T(8,128)(2,1)}, bf16[4,4,2,81,8,1152]{5,4,3,2,1,0:T(8,128)(2,1)}, bf16[3,4,2,2,20,8,1152]{6,5,4,3,2,1,0:T(8,128)(2,1)}, f32[384,1152]{1,0:T(8,128)}, f32[32,1152]{1,0:T(8,128)}) custom-call(bf16[2592,8,1152]{2,1,0:T(8,128)(2,1)} %bitcast.38, bf16[7,144,8,1152]{3,2,1,0:T(8,128)(2,1)} %get-tuple-element.28.refs_1_, ...), custom_call_target="tpu_custom_call" | custom-call | tf_op jit(solution)/shard_map/backward_scatter/pallas_call | solution.py:1293
  434.3 0.9 slice.75
  435.3 2.7 convolution_bitcast_fusion.1
  438.1 0.6 dynamic_update_slice.3
  438.7 0.1 slice.83
  438.8 1.8 reshape.187
  440.6 0.6 reduce_sum.57
  441.2 5.3 %multiply_reduce_fusion = (f32[]{:T(128)}, f32[648,1152]{1,0:T(8,128)S(1)}) fusion(bf16[81,8,1152]{2,1,0:T(8,128)(2,1)} %get-tuple-element.41, f32[6,3,1152]{2,1,0:T(4,128)S(1)} %reshape.185, f32[648,6]{0,1:T(8,128)S(1)} %fusion.7, f32[648,3]{0,1:T(4,128)S(1)} %fusion.10, pred[648]{0:T(1024)(128)(4,1)S(1)} %add_compare_fusion), kind=kOutput, calls=%fused_computation.5 | convolution fusion | flops 164240784 | bytes 4585900 | tf_op jit(solution)/shard_map/dot_general | solution.py:1378
  447.1 0.6 concatenate.13.mine
  447.7 21.4 %sum_everywhere.1 = f32[8,1152]{1,0:T(8,128)} custom-call(f32[8,1152]{1,0:T(8,128)} %concatenate.13.mine), custom_call_target="tpu_custom_call" | custom-call | tf_op jit(solution)/shard_map/sum_everywhere/pallas_call | solution.py:1341
  469.1 1.4 fusion.9
  470.5 1.4 slice_reduce_fusion
  471.9 0.9 fusion.27
  472.7 0.9 slice.81
  473.6 0.8 slice.80
  474.5 0.6 multiply_reduce_fusion.2
  476.5 1.8 broadcast_multiply_fusion.1
  478.3 0.0 copy-start.1
  478.3 4.5 mul.172
  482.8 0.0 copy-done.1
  482.8 0.0 copy-start.6
  482.8 0.0 copy-start.7
  482.8 0.0 copy-start.2
  482.8 7.0 %multiply_subtract_fusion = (f32[746496]{0:T(1024)}, f32[746496]{0:T(1024)}, f32[746496]{0:T(1024)}) fusion(f32[746496]{0:T(1024)S(1)} %copy-done.1, f32[746496]{0:T(1024)} %param.17, f32[746496]{0:T(1024)} %mul.172, f32[746496]{0:T(1024)} %param.18), kind=kLoop, calls=%fused_computation.4 | loop fusion | flops 10450944 | bytes 20901888 | tf_op jit(solution)/shard_map/sub | solution.py:1401
  489.8 0.0 copy-done.6
  489.8 0.0 copy-done.7
  489.8 0.7 multiply_subtract_fusion.1
  490.5 0.0 copy-done.2
  490.5 1.2 copy.35
  491.8 0.0 copy-done.3
  491.8 1.2 copy.36
  (28 shorter events, 0.4 us)
Async XLA Ops:
  0.6 4.9 copy-start.5
  6.1 5.1 %copy-start.8 = (s32[24]{0:T(128)S(1)}, s32[24]{0:T(128)}, u32[]{:S(2)}) copy-start(s32[24]{0:T(128)} %param.13) | copy-start | bytes 292
  7.1 4.9 slice-start
  7.3 4.9 copy-start.9
  7.3 6.0 %copy-start.4 = (f32[16128]{0:T(1024)S(1)}, f32[16128]{0:T(1024)}, u32[]{:S(2)}) copy-start(f32[16128]{0:T(1024)} %param.19) | copy-start | bytes 193540
  9.0 1.1 copy-start
  478.3 4.5 copy-start.1
  482.8 7.0 %copy-start.6 = (f32[16128]{0:T(1024)S(1)}, f32[16128]{0:T(1024)}, u32[]{:S(2)}) copy-start(f32[16128]{0:T(1024)} %param.20) | copy-start | bytes 193540
  482.8 7.0 %copy-start.7 = (f32[16128]{0:T(1024)S(1)}, f32[16128]{0:T(1024)}, u32[]{:S(2)}) copy-start(f32[16128]{0:T(1024)} %param.21) | copy-start | bytes 193540
  482.8 7.7 %copy-start.2 = (f32[384,1152]{1,0:T(8,128)S(1)}, f32[384,1152]{1,0:T(8,128)}, u32[]{:S(2)}) copy-start(f32[384,1152]{1,0:T(8,128)} %get-tuple-element.66) | copy-start | bytes 5308420
  489.8 2.0 copy-start.3
